TPU v7x, 128 devices: a whole 4x4x4 slice. The times are simulated.
128 devices in a mesh: ti: 16 (over z, x), kz: 8 (over y, core).
Axes of the slice: x: 4, y: 4, z: 4, core: 2. Of those that a mesh axis runs over, the one named last changes fastest.
Arguments:
- point_maps: float32 [3, 8, 160, 256], P(None, None, 'kz'), may hold values from 0.3 to 3, as said below
- point_coils: float32 [2, 8, 8, 160, 256], P(None, None, None, 'kz'), may hold values from -2 to 2
- direction_maps: float32 [3, 8, 160, 256], P(None, None, 'kz', 'ti'), may hold values from -12 to 12
- direction_coils: float32 [2, 8, 8, 160, 256], P(None, None, None, 'kz', 'ti'), may hold values from -12 to 12
- residual_maps: float32 [3, 8, 160, 256], P(None, None, 'kz', 'ti'), may hold values from -12 to 12
- residual_coils: float32 [2, 8, 8, 160, 256], P(None, None, None, 'kz', 'ti'), may hold values from -12 to 12
- inversion_times: float32 [32], P('ti'), may hold values from 0.05 to 3
- sampling_mask: int32 [32, 160, 256], P('ti'), may hold values 0 or 1
Outputs:
- new_residual_maps: float32 [3, 8, 160, 256], P(None, None, 'kz', 'ti')
- new_residual_coils: float32 [2, 8, 8, 160, 256], P(None, None, None, 'kz', 'ti')
- new_direction_maps: float32 [3, 8, 160, 256], P(None, None, 'kz', 'ti')
- new_direction_coils: float32 [2, 8, 8, 160, 256], P(None, None, None, 'kz', 'ti')
Inputs may be any that keep to these rules, and one draw needn't show every extreme that they name: `sampling_mask`: 1 where the sample of that bin was acquired. `point_maps`: component 1 lies between 1.4 and 2 times component 0.
All inputs are finite; a program needn't handle non-finite values. No bound on the sum of `sampling_mask` on one device may be relied on, other than what follows from the above.
Results may differ from a plain program's by a relative error of at most 0.0003.
Values sent between devices are 32-bit elements; how exact they have to be, the bound alone decides.
No kernel may reach another device: no remote copies, remote signals or barrier semaphores. Data moves between devices by JAX's collectives and lax.ppermute only.
A program may use at most 128 MiB of HBM per device.

v0:
```python
from functools import partial
import math

import jax
import jax.numpy as jnp
from jax import lax
from jax.sharding import PartitionSpec as P

regular_weight = 2.0


def dft_tables(length, orient):
    indices = jnp.arange(length, dtype=jnp.int32)
    phases = indices[:, None] * indices[None, :] % length
    angles = phases.astype(jnp.float32) * (2.0 * math.pi / length)
    factor = 1.0 / math.sqrt(length)
    return (jnp.cos(angles) * factor, orient * jnp.sin(angles) * factor)


def along_last(real_part, imag_part, tables):
    cos_part, sin_part = tables
    matmul = partial(jnp.dot, precision=lax.Precision.HIGHEST, preferred_element_type=jnp.float32)
    new_real = matmul(real_part, cos_part) - matmul(imag_part, sin_part)
    new_imag = matmul(real_part, sin_part) + matmul(imag_part, cos_part)
    return (new_real, new_imag)


def along_second(real_part, imag_part, tables):
    cos_part, sin_part = tables

    def contract(matrix, values):
        return jnp.einsum(
            "kz,...zy->...ky",
            matrix,
            values,
            precision=lax.Precision.HIGHEST,
            preferred_element_type=jnp.float32,
        )

    new_real = contract(cos_part, real_part) - contract(sin_part, imag_part)
    new_imag = contract(cos_part, imag_part) + contract(sin_part, real_part)
    return (new_real, new_imag)


def inner_sum(left_side, right_side):
    return jnp.sum(left_side[0] * right_side[0]) + jnp.sum(left_side[1] * right_side[1])


def model_terms(maps, bin_times):
    decays = jnp.exp(-bin_times * maps[2][None])
    signal = maps[0][None] - maps[1][None] * decays
    return (decays, signal)


def gradients(returned, maps, coils, decays, signal, bin_times):
    back_re = returned[0]
    back_im = returned[1]
    projected = jnp.sum(coils[0][None] * back_re + coils[1][None] * back_im, axis=1)
    grad_maps = jnp.stack(
        [
            jnp.sum(projected, axis=0),
            -jnp.sum(decays * projected, axis=0),
            maps[1] * jnp.sum(bin_times * decays * projected, axis=0),
        ]
    )
    grad_coils = jnp.stack(
        [jnp.sum(signal[:, None] * back_re, axis=0), jnp.sum(signal[:, None] * back_im, axis=0)]
    )
    return (grad_maps, grad_coils)


def shards(
    point_maps,
    point_coils,
    direction_maps,
    direction_coils,
    residual_maps,
    residual_coils,
    inversion_times,
    sampling_mask,
):
    full_maps, full_coils = (
        lax.all_gather(direction_maps, "ti", axis=3, tiled=True),
        lax.all_gather(direction_coils, "ti", axis=4, tiled=True),
    )
    amplitude = point_maps[1]
    bin_times = inversion_times[:, None, None, None]
    decays, signal = model_terms(point_maps, bin_times)
    signal_step = (
        full_maps[0][None]
        - full_maps[1][None] * decays
        + amplitude[None] * bin_times * decays * full_maps[2][None]
    )
    image_re = point_coils[0][None] * signal_step[:, None] + full_coils[0][None] * signal[:, None]
    image_im = point_coils[1][None] * signal_step[:, None] + full_coils[1][None] * signal[:, None]
    images = jnp.stack([image_re, image_im])
    partitions = sampling_mask.shape[1]
    encodes = sampling_mask.shape[2]
    weights = sampling_mask.astype(jnp.float32)[:, None, None]
    forward_y = dft_tables(encodes, -1.0)
    backward_y = dft_tables(encodes, 1.0)
    forward_z = dft_tables(partitions, -1.0)
    backward_z = dft_tables(partitions, 1.0)
    received = lax.all_to_all(images, "kz", split_axis=3, concat_axis=4, tiled=True)
    real_part, imag_part = along_last(received[0], received[1], forward_y)
    real_part, imag_part = along_second(real_part, imag_part, forward_z)
    real_part = real_part * weights
    imag_part = imag_part * weights
    real_part, imag_part = along_last(real_part, imag_part, backward_y)
    real_part, imag_part = along_second(real_part, imag_part, backward_z)
    returned = lax.all_to_all(
        jnp.stack([real_part, imag_part]), "kz", split_axis=4, concat_axis=3, tiled=True
    )
    grad_maps, grad_coils = gradients(returned, point_maps, point_coils, decays, signal, bin_times)
    share_width = direction_maps.shape[3]
    total_maps, total_coils = lax.psum((grad_maps, grad_coils), "ti")
    offset = lax.axis_index("ti") * share_width
    share_maps = lax.dynamic_slice_in_dim(total_maps, offset, share_width, 3)
    share_coils = lax.dynamic_slice_in_dim(total_coils, offset, share_width, 4)
    applied_maps = share_maps + regular_weight * direction_maps
    applied_coils = share_coils + regular_weight * direction_coils
    directions = (direction_maps, direction_coils)
    residuals = (residual_maps, residual_coils)
    applied = (applied_maps, applied_coils)
    old_norm = lax.psum(inner_sum(residuals, residuals), ("ti", "kz"))
    curvature = lax.psum(inner_sum(directions, applied), ("ti", "kz"))
    step_size = old_norm / curvature
    new_residual_maps = residual_maps - step_size * applied_maps
    new_residual_coils = residual_coils - step_size * applied_coils
    updated = (new_residual_maps, new_residual_coils)
    new_norm = lax.psum(inner_sum(updated, updated), ("ti", "kz"))
    conjugacy = new_norm / old_norm
    new_direction_maps = new_residual_maps + conjugacy * direction_maps
    new_direction_coils = new_residual_coils + conjugacy * direction_coils
    return (new_residual_maps, new_residual_coils, new_direction_maps, new_direction_coils)


def solution(mesh):
    in_specs = (
        P(None, None, "kz", None),
        P(None, None, None, "kz", None),
        P(None, None, "kz", "ti"),
        P(None, None, None, "kz", "ti"),
        P(None, None, "kz", "ti"),
        P(None, None, None, "kz", "ti"),
        P("ti"),
        P("ti", None, None),
    )
    out_specs = (
        P(None, None, "kz", "ti"),
        P(None, None, None, "kz", "ti"),
        P(None, None, "kz", "ti"),
        P(None, None, None, "kz", "ti"),
    )
    return jax.shard_map(shards, mesh=mesh, in_specs=in_specs, out_specs=out_specs, check_vma=False)
```

profile of v0, /device:TPU:1, one launch (start us, length us, event | category | flops | bytes accessed | tf_op | source)
XLA Modules:
  0.0 631.6 jit_solution(4369861340846186824)
XLA Ops:
  12.0 39.2 %all_gather.6 = f32[3,8,20,256]{2,3,1,0:T(8,128)S(1)} all-gather(f32[3,8,20,16]{2,3,1,0:T(8,128)S(1)} %copy-done.3), channel_id=1, replica_groups=mesh['ti'=16,'kz'=8] {'ti'}, dimensions={3}, use_global_device_ids=true | all-gather | bytes 522240 | tf_op jit(solution)/shard_map/all_gather | solution.py:83
  57.3 3.4 fusion.185
  60.7 82.7 %all-gather.2.cloned.1.call-done = f32[2,8,8,20,256]{3,4,2,1,0:T(8,128)} async-done(((f32[2,8,8,20,16]{3,4,2,1,0:T(8,128)}), f32[2,8,8,20,256]{3,4,2,1,0:T(8,128)}) %all-gather.2.cloned.1.call-update) | async-done | bytes 2621456 | tf_op jit(solution)/shard_map/all_gather | solution.py:84
  143.4 11.0 %slice_bitcast_fusion.1 = (f32[8,8,20,256]{2,3,1,0:T(8,128)}, f32[8,8,20,256]{2,3,1,0:T(8,128)}) fusion(f32[2,8,8,20,256]{3,4,2,1,0:T(8,128)} %all-gather.2.cloned.1.call-done), kind=kLoop, calls=%fused_computation.1 | loop fusion | bytes 5242880 | tf_op jit(solution)/shard_map/mul | solution.py:94
  154.4 5.3 copy.59
  159.6 5.3 copy.62
  170.2 6.6 %all-to-all-start = ((f32[2,2,8,8,20,256]{5,2,4,1,0,3:T(8,128)}), f32[2,2,8,8,20,256]{5,2,4,1,0,3:T(8,128)}, u32[]{:S(2)}, u32[]{:S(2)}) async-start(f32[2,2,8,8,20,256]{5,2,4,1,0,3:T(8,128)} %pad_maximum_fusion), calls=%async_computation | async-start | bytes 10485760 | tf_op jit(solution)/shard_map/all_to_all | solution.py:104
  176.9 59.7 %all-to-all-done = f32[2,2,8,8,20,256]{5,2,4,1,0,3:T(8,128)} async-done(((f32[2,2,8,8,20,256]{5,2,4,1,0,3:T(8,128)}), f32[2,2,8,8,20,256]{5,2,4,1,0,3:T(8,128)}, u32[]{:S(2)}, u32[]{:S(2)}) %all-to-all-start) | async-done | bytes 5242912 | tf_op jit(solution)/shard_map/all_to_all | solution.py:104
  239.7 3.8 fusion.2
  243.4 3.8 fusion.4
  247.4 4.0 fusion.13
  251.4 3.8 fusion.10
  261.7 3.8 fusion.1
  272.0 3.5 fusion
  275.5 3.7 convolution_add_fusion
  279.3 3.4 convolution_subtract_fusion
  285.9 3.4 fusion.42
  296.4 5.4 copy.69
  301.8 5.5 all-to-all-start.1
  308.8 58.6 %all-to-all-done.1 = f32[2,2,8,1,160,256]{5,2,1,3,0,4:T(8,128)} async-done(((f32[2,2,8,1,160,256]{5,2,1,3,0,4:T(8,128)}), f32[2,2,8,1,160,256]{5,2,1,3,0,4:T(8,128)}, u32[]{:S(2)}, u32[]{:S(2)}) %all-to-all-start.1) | async-done | bytes 5242912 | tf_op jit(solution)/shard_map/all_to_all | solution.py:111
  367.5 7.0 %multiply_reduce_fusion.1 = (f32[8,160,256]{2,0,1:T(8,128)S(1)}, f32[8,160,256]{2,0,1:T(8,128)S(1)}, f32[2,160,256]{2,0,1:T(2,128)S(1)}, f32[160,256]{1,0:T(8,128)}) fusion(f32[2,2,8,1,160,256]{5,2,1,3,0,4:T(8,128)} %all-to-all-done.1, f32[2,160,256]{2,0,1:T(2,128)} %multiply_subtract_fusion.2, f32[8,160,256]{2,0,1:T(8,128)} %bitcast.123, ...), kind=kLoop, calls=%fused_computation.10 | loop fusion | flops 5120000 | bytes 11304960 | tf_op jit(solution)/shard_map/reduce_sum | solution.py:67
  386.7 87.9 %all-reduce.4.cloned.1.call-done = (f32[3,8,20,256]{3,2,1,0:T(8,128)}, f32[2,8,8,20,256]{4,1,3,2,0:T(8,128)}) async-done(((f32[3,8,20,256]{3,2,1,0:T(8,128)}, f32[2,8,8,20,256]{4,1,3,2,0:T(8,128)}), (f32[3,8,20,256]{3,2,1,0:T(8,128)}, f32[2,8,8,20,256]{4,1,3,2,0:T(8,128)})) %all-reduce.4.cloned.1.call-update) | async-done | bytes 3112976 | tf_op jit(solution)/shard_map/psum | solution.py:116
  481.0 64.5 %all-reduce = (f32[]{:T(128)}, f32[]{:T(128)}) all-reduce(f32[]{:T(128)S(6)} %add.137, f32[]{:T(128)S(6)} %add.155), channel_id=1, replica_groups=mesh['ti'=16,'kz'=8] {'ti','kz'}, use_global_device_ids=true, to_apply=%region_2.3 | all-reduce | flops 2 | bytes 16 | tf_op jit(solution)/shard_map/psum | solution.py:125
  551.8 63.5 %psum.39 = f32[]{:T(128)} all-reduce(f32[]{:T(128)S(6)} %add.156), channel_id=1, replica_groups=mesh['ti'=16,'kz'=8] {'ti','kz'}, use_global_device_ids=true, to_apply=%region_16.17 | all-reduce | flops 1 | bytes 8 | tf_op jit(solution)/shard_map/psum | solution.py:131
  (83 shorter events, 71.6 us)
Async XLA Ops:
  7.2 4.8 copy-start.3
  7.2 136.2 %all-gather.2.cloned.1.call-start = ((), (), s32[]{:S(2)}) async-start(), calls=%async_computation.2 | async-start | bytes 17825792 | tf_op jit(solution)/shard_map/all_gather | solution.py:84
  51.4 1.7 copy-start.11
  52.4 0.9 copy-start.2
  170.2 6.6 %copy-start.10 = (s32[2,160,256]{2,1,0:T(8,128)S(1)}, s32[2,160,256]{2,1,0:T(8,128)}, u32[]{:S(2)}) copy-start(s32[2,160,256]{2,1,0:T(8,128)} %param.15) | copy-start | bytes 983044
  170.2 66.4 %all-to-all-start = ((f32[2,2,8,8,20,256]{5,2,4,1,0,3:T(8,128)}), f32[2,2,8,8,20,256]{5,2,4,1,0,3:T(8,128)}, u32[]{:S(2)}, u32[]{:S(2)}) async-start(f32[2,2,8,8,20,256]{5,2,4,1,0,3:T(8,128)} %pad_maximum_fusion), calls=%async_computation | async-start | bytes 10485760 | tf_op jit(solution)/shard_map/all_to_all | solution.py:104
  301.8 5.8 copy-start.7
  301.8 5.9 copy-start.6
  301.8 65.7 %all-to-all-start.1 = ((f32[2,2,8,1,160,256]{5,2,1,3,0,4:T(8,128)}), f32[2,2,8,1,160,256]{5,2,1,3,0,4:T(8,128)}, u32[]{:S(2)}, u32[]{:S(2)}) async-start(f32[2,2,8,1,160,256]{5,2,1,3,0,4:T(8,128)} %copy.69), calls=%async_computation.1 | async-start | bytes 10485760 | tf_op jit(solution)/shard_map/all_to_all | solution.py:111
  307.3 167.3 %all-reduce.4.cloned.1.call-start = ((), (), s32[]{:S(2)}) async-start(), calls=%async_computation.3 | async-start | bytes 6422528 | tf_op jit(solution)/shard_map/psum | solution.py:116
  380.0 1.0 copy-start.4
  380.0 1.5 copy-start
  380.9 1.6 copy-start.5
  382.4 96.6 %copy-start.1 = (f32[2,8,8,20,16]{3,4,2,1,0:T(8,128)S(1)}, f32[2,8,8,20,16]{3,4,2,1,0:T(8,128)}, u32[]{:S(2)}) copy-start(f32[2,8,8,20,16]{3,4,2,1,0:T(8,128)} %param.13) | copy-start | bytes 491524
  474.6 2.4 copy-start.8
  546.9 2.8 copy-start.9
Sparse Core Ops, SparseCore 0:
  10.1 133.2 all-gather.1
  381.0 93.5 all-reduce.3
where the time goes:
time: 638 us; the launch traced here: 632 us
  waiting for transfers between devices  290 us (45%)
  blocking collectives  167 us (26%)
  matrix products  55.9 us (9%)
  local copies, waits for them, and re-layouts  53.5 us (8%)
  other arithmetic  31.7 us (5%)
  between operations  21.2 us (3%)
  starting transfers between devices  12.4 us (2%)
    psum x1, waiting for transfers between devices, shards(): total_maps, total_coils = lax.psum((grad_maps, grad_coils), 'ti')  87.9 us
    all_gather x1, waiting for transfers between devices, shards(): lax.all_gather(direction_coils, 'ti', axis=4, tiled=True)  82.7 us
    psum x1, blocking collectives, shards(): old_norm = lax.psum(inner_sum(residuals, residuals), ('ti', 'kz'))  64.5 us
    psum x1, blocking collectives, shards(): new_norm = lax.psum(inner_sum(updated, updated), ('ti', 'kz'))  63.5 us
    all_to_all x1, waiting for transfers between devices, shards(): lax.all_to_all(images, 'kz', split_axis=3, concat_axis=4, tiled=True)  59.7 us
    all_to_all x1, waiting for transfers between devices, shards(): lax.all_to_all(jnp.stack([real_part, imag_part]), 'kz', split_axis=4, con...  58.6 us
    all_gather x1, blocking collectives, shards(): lax.all_gather(direction_maps, 'ti', axis=3, tiled=True)  39.2 us
    dot_general x8, matrix products, contract(): jnp.einsum('kz,...zy->...ky', matrix, values, precision=lax.Precision.HIG...  26.8 us
  transfers between devices with their start and end apart: 4, of which 4 were waited for; matrix products, arithmetic and copies ran while one was open for 3% of the time, Pallas kernels for 0%

commit v1 on v0

v1 whole, which is shorter than its diff:
```python
import math

import jax
import jax.numpy as jnp
import numpy as np
from jax import lax
from jax.experimental import pallas as pl
from jax.experimental.pallas import tpu as pltpu
from jax.sharding import PartitionSpec as P

regular_weight = 2.0
AXES = ("ti", "kz")
NZ, NY, ZB, YB, XS = 160, 256, 20, 16, 8
HALF_Z, HALF_Y = NZ // 2, NY // 2
LANES = 128
TILES = 18
MSG = TILES * LANES
HALF_MSG = MSG // 2
POINT_ROWS = 9
FEATURES = 7
VMEM_LIMIT = 50 * 1024 * 1024
f32 = jnp.float32
bf16 = jnp.bfloat16


def split_pair(table):
    high = table.astype(np.float32).astype(jnp.bfloat16)
    low = (table - high.astype(np.float64)).astype(np.float32).astype(jnp.bfloat16)
    return high, low


def real_form(matrix):
    return np.block([[matrix.real, matrix.imag], [-matrix.imag, matrix.real]])


def right_table(table):
    high, low = split_pair(table)
    return np.concatenate([high, high, low], axis=0)


def left_table(table):
    high, low = split_pair(table)
    pad = np.zeros((table.shape[0], 32), dtype=jnp.bfloat16)
    return np.concatenate([high, high, low, pad], axis=1)


def z_of_rows():
    rows = np.arange(HALF_Z)
    return (rows % 8) * ZB + 2 * (rows // 8)


def make_tables():
    n, m = np.arange(HALF_Y)[:, None], np.arange(HALF_Y)[None, :]
    y_even = real_form(np.exp(-2j * np.pi * (n * (2 * m) % NY) / NY) / math.sqrt(NY))
    y_odd = real_form(np.exp(-2j * np.pi * (n * (2 * m + 1) % NY) / NY) / math.sqrt(NY))
    spots, freq = z_of_rows()[None, :], np.arange(HALF_Z)[:, None]
    z_even = real_form((np.exp(-2j * np.pi * (freq * spots % NZ) / NZ) / math.sqrt(NZ)).T).T
    z_odd = real_form((np.exp(-2j * np.pi * (freq * (spots + 1) % NZ) / NZ) / math.sqrt(NZ)).T).T
    forward_y = np.stack([right_table(y_even), right_table(y_odd)])
    backward_y = np.stack([right_table(y_even.T), right_table(y_odd.T)])
    forward_z = np.stack([left_table(z_even), left_table(z_odd)])
    backward_z = np.stack([left_table(z_even.T), left_table(z_odd.T)])
    order = np.zeros((NY, NY), dtype=jnp.bfloat16)
    for lane in range(NY):
        order[2 * (lane % HALF_Y) + lane // HALF_Y, lane] = 1
    return forward_y, forward_z, backward_y, backward_z, order


def iota(shape, axis):
    return lax.broadcasted_iota(jnp.int32, shape, axis)


def block_transpose(tiles):
    group = iota((8, LANES), 1) >> 4
    tiles = list(tiles)
    for bit in (1, 2, 4):
        unset = (group & bit) == 0
        for i in range(8):
            if i & bit:
                continue
            a, c = tiles[i], tiles[i | bit]
            tiles[i] = jnp.where(unset, a, pltpu.roll(c, 16 * bit, 1))
            tiles[i | bit] = jnp.where(unset, pltpu.roll(a, LANES - 16 * bit, 1), c)
    return tiles


def inner_transpose(tile):
    group, row = iota((8, LANES), 1) >> 4, iota((8, LANES), 0)
    for bit in (1, 2, 4):
        g, s = (group & bit) != 0, (row & bit) != 0
        down = pltpu.roll(pltpu.roll(tile, bit, 0), LANES - 16 * bit, 1)
        up = pltpu.roll(pltpu.roll(tile, 8 - bit, 0), 16 * bit, 1)
        tile = jnp.where(g == s, tile, jnp.where(s, down, up))
    return tile


def pair_of(tile, member):
    if tile < 2 * FEATURES:
        return tile // 2, 8 * (tile % 2) + member
    feature = 2 * (tile - 2 * FEATURES) + member // 4
    return (feature, 16 + member % 4) if feature < FEATURES else None


def row_of(z):
    return (z & 1) * HALF_Z + (z >> 1) * 8


def halves(values):
    high = values.astype(bf16)
    return high, (values - high.astype(f32)).astype(bf16)


def times_right(values, table):
    high, low = halves(values)
    return jnp.dot(jnp.concatenate([high, low, high], axis=1), table, preferred_element_type=f32)


def times_left(table, values):
    high, low = halves(values)
    pad = jnp.zeros((32, values.shape[1]), bf16)
    return jnp.dot(table, jnp.concatenate([high, low, high, pad], axis=0), preferred_element_type=f32)


def pack_kernel(place, times, maps, coils, point_maps, point_coils, send, dense):
    t = place[0]
    row, lane = iota((8, LANES), 0), iota((8, LANES), 1)
    even = (row & 1) == 0
    for f in range(3 + 2 * 8):
        block = maps[f] if f < 3 else coils[(f - 3) // 8, (f - 3) % 8]
        turned = jnp.swapaxes(block.reshape(8 * YB, ZB), 0, 1)
        turned = jnp.concatenate([turned, turned[:4]], axis=0)
        for a in range(3):
            dense[f, a] = inner_transpose(turned[8 * a : 8 * a + 8])
    own_times = jnp.where(lane == 64, times[0], jnp.where(lane == 65, times[1], 0.0))
    for g in range(4):
        names = [0, 1, 2] + [3 + 8 * p + 2 * g + e for p in range(2) for e in range(2)]
        for u in range(TILES):
            if u < 2 * FEATURES:
                direction = dense[names[u // 2], u % 2]
            else:
                f = 2 * (u - 2 * FEATURES)
                upper = own_times if f + 1 == FEATURES else pltpu.roll(dense[names[f + 1], 2], 64, 1)
                direction = jnp.where(lane < 64, dense[names[f], 2], upper)
            item = jnp.minimum(t * POINT_ROWS + u // 2, FEATURES * ZB - 1)
            f = item // ZB
            z = item - f * ZB
            side = slice((u % 2) * LANES, (u % 2 + 1) * LANES)
            q = jnp.maximum(f - 3, 0)
            of_maps = point_maps[jnp.minimum(f, 2), z, :, side]
            of_coils = point_coils[q // 2, 2 * g + q % 2, z, :, side]
            point = jnp.where(f < 3, of_maps, of_coils)
            for h in range(2):
                if h == 0:
                    tile = jnp.where(even, direction, pltpu.roll(point, 1, 0))
                else:
                    tile = jnp.where(even, pltpu.roll(direction, 7, 0), point)
                for upper_z in range(2):
                    target = (2 * upper_z + g // 2) * 4 + 2 * (g % 2) + h
                    send[8 * target : 8 * target + 8, u * LANES : (u + 1) * LANES] = tile


def forward_kernel(place, own, other, table_y, table_z, spectrum, point, taus, direction, stamps):
    step = pl.program_id(0)
    t, core = place[0], place[1]

    def unpack(of_direction, of_point):
        for half in range(2):
            for u in range(TILES):
                side = slice(u * LANES, (u + 1) * LANES)
                tiles = [of_direction[8 * (8 * half + i) : 8 * (8 * half + i) + 8, side] for i in range(8)]
                for member, tile in enumerate(block_transpose(tiles)):
                    pair = pair_of(u, member)
                    if pair is not None:
                        f, z = pair
                        direction[f, row_of(z) : row_of(z) + 8, half * LANES : (half + 1) * LANES] = tile
        for item in range(FEATURES * ZB):
            source, i = item // POINT_ROWS, item % POINT_ROWS
            f, z = item // ZB, item % ZB
            point[f, row_of(z) : row_of(z) + 8, :] = of_point[8 * source : 8 * source + 8, i * NY : (i + 1) * NY]
        stamps[...] = of_direction[:, MSG - LANES : MSG]

    @pl.when((step == 0) & (core == 0))
    def _():
        unpack(own, other)

    @pl.when((step == 0) & (core == 1))
    def _():
        unpack(other, own)

    bin_of = (((t >> 2) ^ (step >> 2)) << 2) | ((t + step) & 3)
    block = stamps[pl.ds(pl.multiple_of(bin_of * 8, 8), 8), :]
    chosen = (iota((8, LANES), 0) == 0) & (iota((8, LANES), 1) == 64 + core)
    tau = jnp.sum(jnp.where(chosen, block, 0.0), axis=(0, 1), keepdims=True)
    taus[0] = jnp.broadcast_to(tau, (8, LANES))

    decays = jnp.exp(-tau * point[2])
    signal = point[0] - point[1] * decays
    change = direction[0] - direction[1] * decays + point[1] * tau * decays * direction[2]
    evens, odds = [], []
    for c in range(2):
        re = point[3 + c] * change + direction[3 + c] * signal
        im = point[5 + c] * change + direction[5 + c] * signal
        re_low, re_high, im_low, im_high = re[:, :HALF_Y], re[:, HALF_Y:], im[:, :HALF_Y], im[:, HALF_Y:]
        evens.append(jnp.concatenate([re_low + re_high, im_low + im_high], axis=1))
        odds.append(jnp.concatenate([re_low - re_high, im_low - im_high], axis=1))
    along_even = times_right(jnp.concatenate(evens, axis=0), table_y[0])
    along_odd = times_right(jnp.concatenate(odds, axis=0), table_y[1])
    for c in range(2):
        parts = []
        for parity in range(2):
            rows = slice(c * NZ + parity * HALF_Z, c * NZ + (parity + 1) * HALF_Z)
            re = jnp.concatenate([along_even[rows, :HALF_Y], along_odd[rows, :HALF_Y]], axis=1)
            im = jnp.concatenate([along_even[rows, HALF_Y:], along_odd[rows, HALF_Y:]], axis=1)
            parts.append(times_left(table_z[parity], jnp.concatenate([re, im], axis=0)))
        for part in range(2):
            a = parts[0][part * HALF_Z : (part + 1) * HALF_Z]
            b = parts[1][part * HALF_Z : (part + 1) * HALF_Z]
            spectrum[0, c, part, :HALF_Z] = a + b
            spectrum[0, c, part, HALF_Z:] = a - b


def backward_kernel(place, *refs):
    masks, refs = refs[:8], refs[8:]
    spectrum, point, taus, table_y, table_z, order, mine, theirs, total, sent, weight = refs
    step = pl.program_id(0)
    core = place[1]
    for s in range(8):

        @pl.when(step == s)
        def _():
            weight[...] = jnp.dot(masks[s][...].astype(f32).astype(bf16), order[...], preferred_element_type=f32)

    @pl.when(step == 0)
    def _():
        total[...] = jnp.zeros_like(total)

    tau = taus[0, 0:1, 0:1]
    weights = weight[...]
    evens, odds = [], []
    for c in range(2):
        plus, minus = [], []
        for part in range(2):
            values = spectrum[0, c, part] * weights
            plus.append(values[:HALF_Z] + values[HALF_Z:])
            minus.append(values[:HALF_Z] - values[HALF_Z:])
        for side in (plus, minus):
            out = times_left(table_z[0 if side is plus else 1], jnp.concatenate(side, axis=0))
            re, im = out[:HALF_Z], out[HALF_Z:]
            evens.append(jnp.concatenate([re[:, :HALF_Y], im[:, :HALF_Y]], axis=1))
            odds.append(jnp.concatenate([re[:, HALF_Y:], im[:, HALF_Y:]], axis=1))
    from_even = times_right(jnp.concatenate(evens, axis=0), table_y[0])
    from_odd = times_right(jnp.concatenate(odds, axis=0), table_y[1])
    low, high = from_even + from_odd, from_even - from_odd

    decays = jnp.exp(-tau * point[2])
    signal = point[0] - point[1] * decays
    projected = None
    for c in range(2):
        rows = slice(c * NZ, (c + 1) * NZ)
        re = jnp.concatenate([low[rows, :HALF_Y], high[rows, :HALF_Y]], axis=1)
        im = jnp.concatenate([low[rows, HALF_Y:], high[rows, HALF_Y:]], axis=1)
        term = point[3 + c] * re + point[5 + c] * im
        projected = term if projected is None else projected + term
        total[3 + c] += signal * re
        total[5 + c] += signal * im
    total[0] += projected
    faded = decays * projected
    total[1] -= faded
    total[2] += point[1] * (tau * faded)

    @pl.when(step == 7)
    def _():
        for half in range(2):
            for u in range(TILES):
                tiles = []
                for member in range(8):
                    pair = pair_of(u, member)
                    f, z = pair if pair is not None else (0, 0)
                    tiles.append(total[f, row_of(z) : row_of(z) + 8, half * LANES : (half + 1) * LANES])
                slot = core if u < TILES // 2 else 1 - core
                lane = (u % (TILES // 2)) * LANES
                for i, tile in enumerate(block_transpose(tiles)):
                    target = 8 * (8 * half + i)
                    sent[slot, target : target + 8, lane : lane + LANES] = tile
        mine[...] = sent[0]
        theirs[...] = sent[1]


def sums_kernel(received, dir_maps, dir_coils, res_maps, res_coils, out_maps, out_coils, out_sums):
    row, lane = iota((8, LANES), 0), iota((8, LANES), 1)
    even = (row & 1) == 0
    half_tiles = TILES // 2

    def piece(h, g, u):
        total = None
        for upper_z in range(2):
            source = (2 * upper_z + g // 2) * 4 + 2 * (g % 2) + h
            tile = received[8 * source : 8 * source + 8, u * LANES : (u + 1) * LANES]
            total = tile if total is None else total + tile
        return total

    def whole(groups, tile):
        u = tile % half_tiles
        sides = []
        for h in range(2):
            total = None
            for g in groups:
                term = piece(h, g, u)
                total = term if total is None else total + term
            sides.append(total)
        if tile < half_tiles:
            return jnp.where(even, sides[0], pltpu.roll(sides[1], 1, 0))
        return jnp.where(even, pltpu.roll(sides[0], 7, 0), sides[1])

    def feature(groups, f):
        last = whole(groups, 2 * FEATURES + f // 2)
        if f % 2:
            last = pltpu.roll(last, 64, 1)
        stack = [inner_transpose(tile) for tile in (whole(groups, 2 * f), whole(groups, 2 * f + 1), last)]
        turned = jnp.swapaxes(jnp.concatenate(stack, axis=0), 0, 1)
        return turned[:, :ZB].reshape(XS, YB, ZB)

    sums = [jnp.zeros((XS, YB, ZB), f32) for _ in range(4)]
    for f in range(3 + 16):
        if f < 3:
            gradient = feature(range(4), f)
            direction, residual = dir_maps[f], res_maps[f]
        else:
            part, coil = (f - 3) // 8, (f - 3) % 8
            gradient = feature([coil // 2], 3 + 2 * part + coil % 2)
            direction, residual = dir_coils[part, coil], res_coils[part, coil]
        applied = gradient + regular_weight * direction
        if f < 3:
            out_maps[f] = applied
        else:
            out_coils[part, coil] = applied
        for i, (a, b) in enumerate(
            ((residual, residual), (direction, applied), (residual, applied), (applied, applied))
        ):
            sums[i] = sums[i] + a * b
    line = jnp.zeros((1, LANES), f32)
    for i in range(4):
        value = jnp.sum(jnp.sum(sums[i], axis=0), axis=(0, 1), keepdims=True)
        line = jnp.where(iota((1, LANES), 1) == i, value, line)
    out_sums[...] = jnp.broadcast_to(line, (LANES, LANES))


def step_kernel(sums, app_maps, app_coils, dir_maps, dir_coils, res_maps, res_coils, *outs):
    line = jnp.sum(sums[...], axis=0, keepdims=True)
    lane = iota((1, LANES), 1)
    old, curve, cross, square = (
        jnp.sum(jnp.where(lane == i, line, 0.0), axis=1, keepdims=True) for i in range(4)
    )
    size = old / curve
    new = old - 2.0 * size * cross + size * size * square
    ratio = (new / old).reshape(1, 1, 1)
    size = size.reshape(1, 1, 1)
    for f in range(3):
        fresh = res_maps[f] - size * app_maps[f]
        outs[0][f] = fresh
        outs[2][f] = fresh + ratio * dir_maps[f]
    for part in range(2):
        for coil in range(8):
            fresh = res_coils[part, coil] - size * app_coils[part, coil]
            outs[1][part, coil] = fresh
            outs[3][part, coil] = fresh + ratio * dir_coils[part, coil]


def struct(*shape):
    return jax.ShapeDtypeStruct(shape, f32)


SMEM = pl.BlockSpec(memory_space=pltpu.SMEM)
VMEM = pl.BlockSpec(memory_space=pltpu.VMEM)


def params():
    return pltpu.CompilerParams(vmem_limit_bytes=VMEM_LIMIT)


def constant_block(shape):
    return pl.BlockSpec(shape, lambda s: (0,) * len(shape))


def stepping_block(shape):
    return pl.BlockSpec((1,) + shape, lambda s: (s,) + (0,) * len(shape))


def core_swap(values):
    return lax.ppermute(values, "kz", [(i, i ^ 1) for i in range(8)])


def shards(
    point_maps,
    point_coils,
    direction_maps,
    direction_coils,
    residual_maps,
    residual_coils,
    inversion_times,
    sampling_mask,
):
    forward_y, forward_z, backward_y, backward_z, order = make_tables()
    t, k = lax.axis_index("ti"), lax.axis_index("kz")
    core = k & 1
    place = jnp.stack([t, core]).astype(jnp.int32)

    own_mask = lax.dynamic_index_in_dim(sampling_mask, core, 0, keepdims=False)
    masks = [own_mask]
    for s in range(1, 8):
        pairs = [((((i >> 2) ^ (s >> 2)) << 2) | ((i + s) & 3), i) for i in range(16)]
        masks.append(lax.ppermute(own_mask, "ti", pairs))

    dir_maps, dir_coils = jnp.swapaxes(direction_maps, 2, 3), jnp.swapaxes(direction_coils, 3, 4)
    res_maps, res_coils = jnp.swapaxes(residual_maps, 2, 3), jnp.swapaxes(residual_coils, 3, 4)
    pnt_maps, pnt_coils = jnp.swapaxes(point_maps, 1, 2), jnp.swapaxes(point_coils, 2, 3)

    send = pl.pallas_call(
        pack_kernel,
        out_shape=struct(128, MSG),
        in_specs=[SMEM, SMEM] + [VMEM] * 4,
        out_specs=VMEM,
        scratch_shapes=[pltpu.VMEM((19, 3, 8, LANES), f32)],
        compiler_params=params(),
        name="pack",
    )(place, inversion_times, dir_maps, dir_coils, pnt_maps, pnt_coils)
    own = lax.all_to_all(send, AXES, 0, 0, tiled=True)
    other = core_swap(own)

    spectrum, point, taus = pl.pallas_call(
        forward_kernel,
        grid=(8,),
        out_shape=(struct(8, 2, 2, NZ, NY), struct(FEATURES, NZ, NY), struct(8, 8, LANES)),
        in_specs=[SMEM]
        + [constant_block(a.shape) for a in (own, other, forward_y, forward_z)],
        out_specs=(stepping_block((2, 2, NZ, NY)), constant_block((FEATURES, NZ, NY)), stepping_block((8, LANES))),
        scratch_shapes=[pltpu.VMEM((FEATURES, NZ, NY), f32), pltpu.VMEM((LANES, LANES), f32)],
        compiler_params=params(),
        name="forward",
    )(place, own, other, jnp.asarray(forward_y), jnp.asarray(forward_z))

    mine, theirs = pl.pallas_call(
        backward_kernel,
        grid=(8,),
        out_shape=(struct(128, HALF_MSG), struct(128, HALF_MSG)),
        in_specs=[SMEM]
        + [constant_block((NZ, NY))] * 8
        + [stepping_block((2, 2, NZ, NY)), constant_block((FEATURES, NZ, NY)), stepping_block((8, LANES))]
        + [constant_block(a.shape) for a in (backward_y, backward_z, order)],
        out_specs=(constant_block((128, HALF_MSG)),) * 2,
        scratch_shapes=[
            pltpu.VMEM((FEATURES, NZ, NY), f32),
            pltpu.VMEM((2, 128, HALF_MSG), f32),
            pltpu.VMEM((NZ, NY), f32),
        ],
        compiler_params=params(),
        name="backward",
    )(place, *masks, spectrum, point, taus, jnp.asarray(backward_y), jnp.asarray(backward_z), jnp.asarray(order))

    summed = mine + core_swap(theirs)
    received = lax.all_to_all(summed, AXES, 0, 0, tiled=True)

    maps_shape, coils_shape = struct(*dir_maps.shape), struct(*dir_coils.shape)
    app_maps, app_coils, sums = pl.pallas_call(
        sums_kernel,
        out_shape=(maps_shape, coils_shape, struct(128, LANES)),
        in_specs=[VMEM] * 5,
        out_specs=(VMEM,) * 3,
        compiler_params=params(),
        name="sums",
    )(received, dir_maps, dir_coils, res_maps, res_coils)
    all_sums = lax.all_to_all(sums.reshape(128, 1, LANES), AXES, 0, 0).reshape(128, LANES)

    outs = pl.pallas_call(
        step_kernel,
        out_shape=(maps_shape, coils_shape, maps_shape, coils_shape),
        in_specs=[VMEM] * 7,
        out_specs=(VMEM,) * 4,
        compiler_params=params(),
        name="step",
    )(all_sums, app_maps, app_coils, dir_maps, dir_coils, res_maps, res_coils)
    return tuple(jnp.swapaxes(out, -2, -1) for out in outs)


def solution(mesh):
    in_specs = (
        P(None, None, "kz", None),
        P(None, None, None, "kz", None),
        P(None, None, "kz", "ti"),
        P(None, None, None, "kz", "ti"),
        P(None, None, "kz", "ti"),
        P(None, None, None, "kz", "ti"),
        P("ti"),
        P("ti", None, None),
    )
    out_specs = (
        P(None, None, "kz", "ti"),
        P(None, None, None, "kz", "ti"),
        P(None, None, "kz", "ti"),
        P(None, None, None, "kz", "ti"),
    )
    return jax.shard_map(shards, mesh=mesh, in_specs=in_specs, out_specs=out_specs, check_vma=False)
```

time: 638 us -> 133 us (0.21)
  waiting for transfers between devices: 290 us -> 5.31 us
  blocking collectives: 167 us -> 64.5 us
  matrix products: 55.9 us -> 0 us
  local copies, waits for them, and re-layouts: 53.5 us -> 6.91 us
  Pallas kernels: 0 us -> 42.3 us
  other arithmetic: 31.7 us -> 0.14 us
  between operations: 21.2 us -> 0.84 us
    psum x2 -> x0, blocking collectives: 128 us -> none  [the longest x1 64.5 us: shards(): old_norm = lax.psum(inner_sum(residuals, residuals), ('ti', 'kz'))]
    all_to_all x2 -> x0, waiting for transfers between devices: 118 us -> none  [the longest x1 59.7 us: shards(): lax.all_to_all(images, 'kz', split_axis=3, concat_axis=4, tiled=True)]
    psum x1 -> x0, waiting for transfers between devices: 87.9 us -> none  [shards(): total_maps, total_coils = lax.psum((grad_maps, grad_coils), 'ti')]
    all_gather x1 -> x0, waiting for transfers between devices: 82.7 us -> none  [shards(): lax.all_gather(direction_coils, 'ti', axis=4, tiled=True)]
    all_to_all x0 -> x3, blocking collectives: none -> 64.5 us  [the longest x1 31.6 us: shards(): own = lax.all_to_all(send, AXES, 0, 0, tiled=True)]
    dot_general x16 -> x0, matrix products: 55.9 us -> none  [the longest x8 26.8 us: contract(): jnp.einsum('kz,...zy->...ky', matrix, values, precision=lax.Precision.HIG...]
    pallas_call x0 -> x5, Pallas kernels: none -> 42.3 us  [the longest x1 14.5 us: shards(): pl.pallas_call(backward_kernel, grid=(8,), out_shape=(struct(128, HALF_MS...]
    all_gather x1 -> x0, blocking collectives: 39.2 us -> none  [shards(): lax.all_gather(direction_maps, 'ti', axis=3, tiled=True)]
  transfers between devices with their start and end apart: 4 -> 9, of which waited for: 4 -> 3; matrix products, arithmetic and copies ran while one was open for 3% -> 0% of each run, Pallas kernels for 0% -> 11%
where the time goes in v1:
time: 133 us
  blocking collectives  64.5 us (48%)
  Pallas kernels  42.3 us (32%)
  starting transfers between devices  12.8 us (10%)
  local copies, waits for them, and re-layouts  6.91 us (5%)
  waiting for transfers between devices  5.31 us (4%)
    all_to_all x1, blocking collectives, shards(): own = lax.all_to_all(send, AXES, 0, 0, tiled=True)  31.6 us
    all_to_all x1, blocking collectives, shards(): received = lax.all_to_all(summed, AXES, 0, 0, tiled=True)  18.9 us
    pallas_call x1, Pallas kernels, shards(): pl.pallas_call(backward_kernel, grid=(8,), out_shape=(struct(128, HALF_MS...  14.5 us
    pallas_call x1, Pallas kernels, shards(): pl.pallas_call(forward_kernel, grid=(8,), out_shape=(struct(8, 2, 2, NZ,...  14.2 us
    all_to_all x1, blocking collectives, shards(): lax.all_to_all(sums.reshape(128, 1, LANES), AXES, 0, 0).reshape(128, LANES)  14 us
    ppermute x7, starting transfers between devices, shards(): masks.append(lax.ppermute(own_mask, 'ti', pairs))  9.57 us
    pallas_call x1, Pallas kernels, shards(): pl.pallas_call(sums_kernel, out_shape=(maps_shape, coils_shape, struct(12...  6.12 us
    pallas_call x1, Pallas kernels, shards(): pl.pallas_call(pack_kernel, out_shape=struct(128, MSG), in_specs=[SMEM, S...  5.86 us
  transfers between devices with their start and end apart: 9, of which 3 were waited for; matrix products, arithmetic and copies ran while one was open for 0% of the time, Pallas kernels for 11%

profile of v1, /device:TPU:1, one launch (start us, length us, event | category | flops | bytes accessed | tf_op | source)
XLA Modules:
  0.0 132.8 jit_solution(5672023502724906231)
XLA Ops:
  0.7 1.3 copy-done.1
  2.0 0.9 copy-done.4
  2.9 1.0 copy-done.10
  3.9 0.7 copy-done.14
  4.6 5.9 %pack.1 = f32[128,2304]{1,0:T(8,128)S(1)} custom-call(s32[2]{0:T(128)S(1)} %pad_add_fusion.place, f32[2]{0:T(128)S(1)} %copy-done.14, f32[3,8,16,20]{3,2,1,0:T(8,128)S(1)} %bitcast.36, f32[2,8,8,16,20]{4,3,2,1,0:T(8,128)S(1)} %bitcast.27, f32[3,20,8,256]{3,2,1,0:T(8,128)S(1)} %bitcast.41, f32[2,8,20,8,256]{4,3,2,1,0:T(8,128)} %bitcast.44), custom_call_target="tpu_custom_call" | custom-call | tf_op jit(solution)/shard_map/pack/pallas_call | solution.py:418
  10.5 1.2 copy.17
  11.7 31.6 %all_to_all.27 = f32[128,1,2304]{2,1,0:T(1,128)S(1)} all-to-all(f32[128,1,2304]{2,1,0:T(1,128)S(1)} %copy.17), channel_id=1, replica_groups=mesh['ti'=16,'kz'=8] {'ti','kz'}, dimensions={0} | all-to-all | bytes 2359296 | tf_op jit(solution)/shard_map/all_to_all | solution.py:427
  43.4 1.4 %collective-permute-start.7 = (f32[128,2304]{1,0:T(8,128)S(1)}, f32[128,2304]{1,0:T(8,128)}, u32[]{:S(2)}, u32[]{:S(2)}) collective-permute-start(f32[128,2304]{1,0:T(8,128)S(1)} %bitcast.30), channel_id=1, source_target_pairs={{0,1},{1,0},{2,3},{3,2},{4,5},{5,4},{6,7},{7,6},{8,9},{9,8},{10,11... | collective-permute-start | bytes 3538952 | tf_op jit(solution)/shard_map/ppermute | solution.py:390
  44.8 1.0 collective-permute-start
  45.8 1.2 collective-permute-start.1
  47.6 3.1 %collective-permute-done.refs_1_ = s32[160,256]{1,0:T(8,128)S(1)} collective-permute-done((s32[160,256]{1,0:T(8,128)S(1)}, s32[160,256]{1,0:T(8,128)S(1)}, u32[]{:S(2)}, u32[]{:S(2)}) %collective-permute-start) | collective-permute-done | bytes 163872 | tf_op jit(solution)/shard_map/ppermute | solution.py:412
  50.6 1.6 %collective-permute-start.4 = (s32[160,256]{1,0:T(8,128)S(1)}, s32[160,256]{1,0:T(8,128)S(1)}, u32[]{:S(2)}, u32[]{:S(2)}) collective-permute-start(s32[160,256]{1,0:T(8,128)S(1)} %dynamic-slice_bitcast_fusion.refs_0_), channel_id=1, source_target_pairs={{40,0},{48,8},{56,16},{32,24},{8,32},{16,40},{24,48},{0,56},{104,6... | collective-permute-start | bytes 491528 | tf_op jit(solution)/shard_map/ppermute | solution.py:412
  52.8 1.5 %collective-permute-start.5 = (s32[160,256]{1,0:T(8,128)S(1)}, s32[160,256]{1,0:T(8,128)S(1)}, u32[]{:S(2)}, u32[]{:S(2)}) collective-permute-start(s32[160,256]{1,0:T(8,128)S(1)} %dynamic-slice_bitcast_fusion.refs_0_), channel_id=1, source_target_pairs={{48,0},{56,8},{32,16},{40,24},{16,32},{24,40},{0,48},{8,56},{112,6... | collective-permute-start | bytes 491528 | tf_op jit(solution)/shard_map/ppermute | solution.py:412
  54.3 3.7 %collective-permute-start.6 = (s32[160,256]{1,0:T(8,128)S(1)}, s32[160,256]{1,0:T(8,128)S(1)}, u32[]{:S(2)}, u32[]{:S(2)}) collective-permute-start(s32[160,256]{1,0:T(8,128)S(1)} %dynamic-slice_bitcast_fusion.refs_0_), channel_id=1, source_target_pairs={{56,0},{32,8},{40,16},{48,24},{24,32},{0,40},{8,48},{16,56},{120,6... | collective-permute-start | bytes 491528 | tf_op jit(solution)/shard_map/ppermute | solution.py:412
  58.0 14.2 %forward.1 = (f32[8,2,2,160,256]{4,3,2,1,0:T(8,128)}, f32[7,160,256]{2,1,0:T(8,128)S(1)}, f32[8,8,128]{2,1,0:T(8,128)S(1)}) custom-call(s32[2]{0:T(128)S(1)} %pad_add_fusion.place, f32[128,2304]{1,0:T(8,128)S(1)} %bitcast.31, f32[128,2304]{1,0:T(8,128)} %collective-permute-done.7.other, bf16[2,768,256]{2,1,0:T(8,128)(2,1)S(1)} %copy-done.8, ...), custom_call_target="tpu_custom_call" | custom-call | tf_op jit(solution)/shard_map/forward/pallas_call | solution.py:430
  72.2 1.0 copy-done.6
  73.3 14.5 %backward.1 = (f32[128,1152]{1,0:T(8,128)S(1)}, f32[128,1152]{1,0:T(8,128)S(1)}) custom-call(s32[2]{0:T(128)S(1)} %pad_add_fusion.place, s32[160,256]{1,0:T(8,128)S(1)} %dynamic-slice_bitcast_fusion.refs_0_, s32[160,256]{1,0:T(8,128)S(1)} %collective-permute-done.refs_1_, s32[160,256]{1,0:T(8,128)S(1)} %collective-permute-done.1.refs_2_, ...), custom_call_target="tpu_custom_call" | custom-call | tf_op jit(solution)/shard_map/backward/pallas_call | solution.py:442
  87.8 1.9 %collective-permute-start.8 = (f32[128,1152]{1,0:T(8,128)S(1)}, f32[128,1152]{1,0:T(8,128)S(1)}, u32[]{:S(2)}, u32[]{:S(2)}) collective-permute-start(f32[128,1152]{1,0:T(8,128)S(1)} %get-tuple-element.20), channel_id=1, source_target_pairs={{0,1},{1,0},{2,3},{3,2},{4,5},{5,4},{6,7},{7,6},{8,9},{9,8},{10,11... | collective-permute-start | bytes 1769480 | tf_op jit(solution)/shard_map/ppermute | solution.py:390
  89.7 1.6 %collective-permute-done.8 = f32[128,1152]{1,0:T(8,128)S(1)} collective-permute-done((f32[128,1152]{1,0:T(8,128)S(1)}, f32[128,1152]{1,0:T(8,128)S(1)}, u32[]{:S(2)}, u32[]{:S(2)}) %collective-permute-start.8) | collective-permute-done | bytes 589856 | tf_op jit(solution)/shard_map/ppermute | solution.py:390
  91.4 0.6 copy.18
  92.0 18.9 %all_to_all.28 = f32[128,1,1152]{2,1,0:T(1,128)S(1)} all-to-all(f32[128,1,1152]{2,1,0:T(1,128)S(1)} %copy.18), channel_id=1, replica_groups=mesh['ti'=16,'kz'=8] {'ti','kz'}, dimensions={0} | all-to-all | bytes 1179648 | tf_op jit(solution)/shard_map/all_to_all | solution.py:461
  111.0 6.1 %sums.1 = (f32[3,8,16,20]{3,2,1,0:T(8,128)S(1)}, f32[2,8,8,16,20]{4,3,2,1,0:T(8,128)S(1)}, f32[128,128]{1,0:T(8,128)S(1)}) custom-call(f32[128,1152]{1,0:T(8,128)S(1)} %bitcast.35, f32[3,8,16,20]{3,2,1,0:T(8,128)S(1)} %bitcast.37, f32[2,8,8,16,20]{4,3,2,1,0:T(8,128)S(1)} %bitcast.28, f32[3,8,16,20]{3,2,1,0:T(8,128)S(1)} %bitcast.39, ...), custom_call_target="tpu_custom_call" | custom-call | tf_op jit(solution)/shard_map/sums/pallas_call | solution.py:464
  117.1 14.0 %all_to_all.29 = f32[128,1,128]{2,1,0:T(1,128)S(1)} all-to-all(f32[128,1,128]{2,1,0:T(1,128)S(1)} %bitcast.43), channel_id=1, replica_groups=mesh['ti'=16,'kz'=8] {'ti','kz'}, dimensions={0} | all-to-all | bytes 131072 | tf_op jit(solution)/shard_map/all_to_all | solution.py:472
  131.1 1.7 %step.1 = (f32[3,8,16,20]{3,2,1,0:T(8,128)}, f32[2,8,8,16,20]{4,3,2,1,0:T(8,128)}, f32[3,8,16,20]{3,2,1,0:T(8,128)}, f32[2,8,8,16,20]{4,3,2,1,0:T(8,128)}) custom-call(f32[128,128]{1,0:T(8,128)S(1)} %bitcast.42, f32[3,8,16,20]{3,2,1,0:T(8,128)S(1)} %get-tuple-element.22.app_maps, f32[2,8,8,16,20]{4,3,2,1,0:T(8,128)S(1)} %get-tuple-element.23.app_coils, ...), custom_call_target="tpu_custom_call" | custom-call | tf_op jit(solution)/shard_map/step/pallas_call | solution.py:474
  (39 shorter events, 1.5 us)
Async XLA Ops:
  0.6 44.1 %copy-start = (s32[2,160,256]{2,1,0:T(8,128)S(1)}, s32[2,160,256]{2,1,0:T(8,128)}, u32[]{:S(2)}) copy-start(s32[2,160,256]{2,1,0:T(8,128)} %param.20) | copy-start | bytes 983044
  0.7 1.3 copy-start.1
  2.0 0.9 copy-start.4
  2.9 1.0 copy-start.10
  3.9 0.7 copy-start.14
  43.3 14.7 %copy-start.8 = (bf16[2,768,256]{2,1,0:T(8,128)(2,1)S(1)}, bf16[2,768,256]{2,1,0:T(8,128)(2,1)}, u32[]{:S(2)}) copy-start(bf16[2,768,256]{2,1,0:T(8,128)(2,1)} %constant.27.clone.table_y) | copy-start | bytes 2359300
  43.3 14.7 %copy-start.12 = (bf16[2,160,512]{2,1,0:T(8,128)(2,1)S(1)}, bf16[2,160,512]{2,1,0:T(8,128)(2,1)}, u32[]{:S(2)}) copy-start(bf16[2,160,512]{2,1,0:T(8,128)(2,1)} %constant.28.clone.table_z) | copy-start | bytes 983044
  43.4 10.9 %collective-permute-start.7 = (f32[128,2304]{1,0:T(8,128)S(1)}, f32[128,2304]{1,0:T(8,128)}, u32[]{:S(2)}, u32[]{:S(2)}) collective-permute-start(f32[128,2304]{1,0:T(8,128)S(1)} %bitcast.30), channel_id=1, source_target_pairs={{0,1},{1,0},{2,3},{3,2},{4,5},{5,4},{6,7},{7,6},{8,9},{9,8},{10,11... | collective-permute-start | bytes 3538952 | tf_op jit(solution)/shard_map/ppermute | solution.py:390
  44.7 28.5 %copy-start.7 = (bf16[2,768,256]{2,1,0:T(8,128)(2,1)S(1)}, bf16[2,768,256]{2,1,0:T(8,128)(2,1)}, u32[]{:S(2)}) copy-start(bf16[2,768,256]{2,1,0:T(8,128)(2,1)} %constant.29.clone.refs_11_) | copy-start | bytes 2359300
  44.7 28.5 %copy-start.11 = (bf16[2,160,512]{2,1,0:T(8,128)(2,1)S(1)}, bf16[2,160,512]{2,1,0:T(8,128)(2,1)}, u32[]{:S(2)}) copy-start(bf16[2,160,512]{2,1,0:T(8,128)(2,1)} %constant.30.clone.refs_12_) | copy-start | bytes 983044
  44.8 28.5 %copy-start.13 = (bf16[256,256]{1,0:T(8,128)(2,1)S(1)}, bf16[256,256]{1,0:T(8,128)(2,1)}, u32[]{:S(2)}) copy-start(bf16[256,256]{1,0:T(8,128)(2,1)} %constant.31.clone.refs_13_) | copy-start | bytes 393220
  44.8 5.9 %collective-permute-start = (s32[160,256]{1,0:T(8,128)S(1)}, s32[160,256]{1,0:T(8,128)S(1)}, u32[]{:S(2)}, u32[]{:S(2)}) collective-permute-start(s32[160,256]{1,0:T(8,128)S(1)} %dynamic-slice_bitcast_fusion.refs_0_), channel_id=1, source_target_pairs={{8,0},{16,8},{24,16},{0,24},{40,32},{48,40},{56,48},{32,56},{72,64... | collective-permute-start | bytes 491528 | tf_op jit(solution)/shard_map/ppermute | solution.py:412
  45.8 7.0 %collective-permute-start.1 = (s32[160,256]{1,0:T(8,128)S(1)}, s32[160,256]{1,0:T(8,128)S(1)}, u32[]{:S(2)}, u32[]{:S(2)}) collective-permute-start(s32[160,256]{1,0:T(8,128)S(1)} %dynamic-slice_bitcast_fusion.refs_0_), channel_id=1, source_target_pairs={{16,0},{24,8},{0,16},{8,24},{48,32},{56,40},{32,48},{40,56},{80,64... | collective-permute-start | bytes 491528 | tf_op jit(solution)/shard_map/ppermute | solution.py:412
  47.0 26.2 %collective-permute-start.2 = (s32[160,256]{1,0:T(8,128)S(1)}, s32[160,256]{1,0:T(8,128)S(1)}, u32[]{:S(2)}, u32[]{:S(2)}) collective-permute-start(s32[160,256]{1,0:T(8,128)S(1)} %dynamic-slice_bitcast_fusion.refs_0_), channel_id=1, source_target_pairs={{24,0},{0,8},{8,16},{16,24},{56,32},{32,40},{40,48},{48,56},{88,64... | collective-permute-start | bytes 491528 | tf_op jit(solution)/shard_map/ppermute | solution.py:412
  47.0 26.2 %collective-permute-start.3 = (s32[160,256]{1,0:T(8,128)S(1)}, s32[160,256]{1,0:T(8,128)S(1)}, u32[]{:S(2)}, u32[]{:S(2)}) collective-permute-start(s32[160,256]{1,0:T(8,128)S(1)} %dynamic-slice_bitcast_fusion.refs_0_), channel_id=1, source_target_pairs={{32,0},{40,8},{48,16},{56,24},{0,32},{8,40},{16,48},{24,56},{96,64... | collective-permute-start | bytes 491528 | tf_op jit(solution)/shard_map/ppermute | solution.py:412
  50.6 22.6 %collective-permute-start.4 = (s32[160,256]{1,0:T(8,128)S(1)}, s32[160,256]{1,0:T(8,128)S(1)}, u32[]{:S(2)}, u32[]{:S(2)}) collective-permute-start(s32[160,256]{1,0:T(8,128)S(1)} %dynamic-slice_bitcast_fusion.refs_0_), channel_id=1, source_target_pairs={{40,0},{48,8},{56,16},{32,24},{8,32},{16,40},{24,48},{0,56},{104,6... | collective-permute-start | bytes 491528 | tf_op jit(solution)/shard_map/ppermute | solution.py:412
  52.8 20.5 %collective-permute-start.5 = (s32[160,256]{1,0:T(8,128)S(1)}, s32[160,256]{1,0:T(8,128)S(1)}, u32[]{:S(2)}, u32[]{:S(2)}) collective-permute-start(s32[160,256]{1,0:T(8,128)S(1)} %dynamic-slice_bitcast_fusion.refs_0_), channel_id=1, source_target_pairs={{48,0},{56,8},{32,16},{40,24},{16,32},{24,40},{0,48},{8,56},{112,6... | collective-permute-start | bytes 491528 | tf_op jit(solution)/shard_map/ppermute | solution.py:412
  54.3 18.9 %collective-permute-start.6 = (s32[160,256]{1,0:T(8,128)S(1)}, s32[160,256]{1,0:T(8,128)S(1)}, u32[]{:S(2)}, u32[]{:S(2)}) collective-permute-start(s32[160,256]{1,0:T(8,128)S(1)} %dynamic-slice_bitcast_fusion.refs_0_), channel_id=1, source_target_pairs={{56,0},{32,8},{40,16},{48,24},{24,32},{0,40},{8,48},{16,56},{120,6... | collective-permute-start | bytes 491528 | tf_op jit(solution)/shard_map/ppermute | solution.py:412
  72.2 1.0 copy-start.6
  87.8 3.5 %collective-permute-start.8 = (f32[128,1152]{1,0:T(8,128)S(1)}, f32[128,1152]{1,0:T(8,128)S(1)}, u32[]{:S(2)}, u32[]{:S(2)}) collective-permute-start(f32[128,1152]{1,0:T(8,128)S(1)} %get-tuple-element.20), channel_id=1, source_target_pairs={{0,1},{1,0},{2,3},{3,2},{4,5},{5,4},{6,7},{7,6},{8,9},{9,8},{10,11... | collective-permute-start | bytes 1769480 | tf_op jit(solution)/shard_map/ppermute | solution.py:390
  92.0 18.9 %copy-start.2 = (f32[2,8,8,20,16]{3,4,2,1,0:T(8,128)S(1)}, f32[2,8,8,20,16]{3,4,2,1,0:T(8,128)}, u32[]{:S(2)}) copy-start(f32[2,8,8,20,16]{3,4,2,1,0:T(8,128)} %param.16) | copy-start | bytes 491524
  92.0 18.9 %copy-start.5 = (f32[3,8,20,16]{2,3,1,0:T(8,128)S(1)}, f32[3,8,20,16]{2,3,1,0:T(8,128)}, u32[]{:S(2)}) copy-start(f32[3,8,20,16]{2,3,1,0:T(8,128)} %param.15) | copy-start | bytes 92164
  92.0 18.9 %copy-start.9 = (f32[3,8,20,16]{2,3,1,0:T(8,128)S(1)}, f32[3,8,20,16]{2,3,1,0:T(8,128)}, u32[]{:S(2)}) copy-start(f32[3,8,20,16]{2,3,1,0:T(8,128)} %param.17) | copy-start | bytes 92164
  110.9 20.2 %copy-start.3 = (f32[2,8,8,20,16]{3,4,2,1,0:T(8,128)S(1)}, f32[2,8,8,20,16]{3,4,2,1,0:T(8,128)}, u32[]{:S(2)}) copy-start(f32[2,8,8,20,16]{3,4,2,1,0:T(8,128)} %param.18) | copy-start | bytes 491524

commit v2 on v1

v2 whole, which is shorter than its diff:
```python
import math

import jax
import jax.numpy as jnp
import numpy as np
from jax import lax
from jax.experimental import pallas as pl
from jax.experimental.pallas import tpu as pltpu
from jax.sharding import PartitionSpec as P

regular_weight = 2.0
AXES = ("ti", "kz")
NZ, NY, ZB, YB, XS = 160, 256, 20, 16, 8
HALF_Z, HALF_Y = NZ // 2, NY // 2
LANES = 128
FEATURES = 7
PAIRS = FEATURES * ZB
MAIN = 16
TILES = 18
MSG = TILES * LANES
ITEMS = 9
VMEM_LIMIT = 32 * 1024 * 1024
f32 = jnp.float32
bf16 = jnp.bfloat16


def split_pair(table):
    high = table.astype(np.float32).astype(jnp.bfloat16)
    low = (table - high.astype(np.float64)).astype(np.float32).astype(jnp.bfloat16)
    return high, low


def real_form(matrix):
    return np.block([[matrix.real, matrix.imag], [-matrix.imag, matrix.real]])


def right_table(table):
    high, low = split_pair(table)
    return np.concatenate([high, high, low], axis=0)


def left_table(table):
    high, low = split_pair(table)
    pad = np.zeros((table.shape[0], 32), dtype=jnp.bfloat16)
    return np.concatenate([high, high, low, pad], axis=1)


def z_of_rows():
    rows = np.arange(HALF_Z)
    return (rows % 8) * ZB + 2 * (rows // 8)


def make_tables():
    n, m = np.arange(HALF_Y)[:, None], np.arange(HALF_Y)[None, :]
    y_even = real_form(np.exp(-2j * np.pi * (n * (2 * m) % NY) / NY) / math.sqrt(NY))
    y_odd = real_form(np.exp(-2j * np.pi * (n * (2 * m + 1) % NY) / NY) / math.sqrt(NY))
    spots, freq = z_of_rows()[None, :], np.arange(HALF_Z)[:, None]
    z_even = real_form((np.exp(-2j * np.pi * (freq * spots % NZ) / NZ) / math.sqrt(NZ)).T).T
    z_odd = real_form((np.exp(-2j * np.pi * (freq * (spots + 1) % NZ) / NZ) / math.sqrt(NZ)).T).T
    forward_y = np.stack([right_table(y_even), right_table(y_odd)])
    backward_y = np.stack([right_table(y_even.T), right_table(y_odd.T)])
    forward_z = np.stack([left_table(z_even), left_table(z_odd)])
    backward_z = np.stack([left_table(z_even.T), left_table(z_odd.T)])
    order = np.zeros((NY, NY), dtype=jnp.bfloat16)
    for lane in range(NY):
        order[2 * (lane % HALF_Y) + lane // HALF_Y, lane] = 1
    return forward_y, forward_z, backward_y, backward_z, order


def iota(shape, axis):
    return lax.broadcasted_iota(jnp.int32, shape, axis)


def block_transpose(tiles):
    group = iota((8, LANES), 1) >> 4
    tiles = list(tiles)
    for bit in (1, 2, 4):
        unset = (group & bit) == 0
        for i in range(8):
            if i & bit:
                continue
            a, c = tiles[i], tiles[i | bit]
            tiles[i] = jnp.where(unset, a, pltpu.roll(c, 16 * bit, 1))
            tiles[i | bit] = jnp.where(unset, pltpu.roll(a, LANES - 16 * bit, 1), c)
    return tiles


def inner_transpose(tile):
    group, row = iota((8, LANES), 1) >> 4, iota((8, LANES), 0)
    for bit in (1, 2, 4):
        g, s = (group & bit) != 0, (row & bit) != 0
        down = pltpu.roll(pltpu.roll(tile, bit, 0), LANES - 16 * bit, 1)
        up = pltpu.roll(pltpu.roll(tile, 8 - bit, 0), 16 * bit, 1)
        tile = jnp.where(g == s, tile, jnp.where(s, down, up))
    return tile


def halves(values):
    high = values.astype(bf16)
    return high, (values - high.astype(f32)).astype(bf16)


def times_right(values, table):
    high, low = halves(values)
    return jnp.dot(jnp.concatenate([high, low, high], axis=1), table, preferred_element_type=f32)


def times_left(table, values):
    high, low = halves(values)
    pad = jnp.zeros((32, values.shape[1]), bf16)
    return jnp.dot(table, jnp.concatenate([high, low, high, pad], axis=0), preferred_element_type=f32)


def split_rows(values):
    grouped = values.reshape(ZB // 2, 2, 8, values.shape[1])
    return [grouped[:, parity].reshape(HALF_Z, values.shape[1]) for parity in range(2)]


def join_rows(even, odd):
    parts = [side.reshape(ZB // 2, 1, 8, side.shape[1]) for side in (even, odd)]
    return jnp.concatenate(parts, axis=1).reshape(NZ, even.shape[1])


def plane(ref, f):
    return jnp.concatenate([ref[0, f * NZ : (f + 1) * NZ], ref[1, f * NZ : (f + 1) * NZ]], axis=1)


def names_of(g):
    return [0, 1, 2] + [3 + 8 * p + 2 * g + e for p in range(2) for e in range(2)]


def dense_tiles(maps, coils, stacked, turned, emit):
    blank = jnp.zeros((8, LANES), f32)
    for g in range(4):
        stacked[g, 136:144] = blank
        for i, name in enumerate(names_of(g)):
            if name < 3:
                if g == 0:
                    rows = jnp.swapaxes(maps[name].reshape(8 * YB, ZB), 0, 1)
                    for other in range(4):
                        stacked[other, i * ZB : (i + 1) * ZB] = rows
            else:
                block = coils[(name - 3) // 8, (name - 3) % 8]
                stacked[g, i * ZB : (i + 1) * ZB] = jnp.swapaxes(block.reshape(8 * YB, ZB), 0, 1)
        turned[g] = jnp.swapaxes(stacked[g, :LANES], 0, 1)
        for j in range(MAIN):
            emit(g, j, turned[g, pl.ds(j, 8, stride=YB), :])
        for v in range(2):
            emit(g, MAIN + v, inner_transpose(stacked[g, LANES + 8 * v : LANES + 8 * v + 8]))


def pack_kernel(
    times, mask, maps_in, coils_in, point_maps, point_coils,
    send, dense, mask_send,
    maps, coils, of_maps, of_coils, stamp, stacked, turned, sems,
):
    t, core = lax.axis_index("ti"), lax.axis_index("kz") & 1
    copies = [
        pltpu.make_async_copy(maps_in, maps, sems.at[0]),
        pltpu.make_async_copy(coils_in, coils, sems.at[1]),
        pltpu.make_async_copy(times, stamp, sems.at[2]),
    ]
    mask_copies = [pltpu.make_async_copy(mask.at[core], mask_send.at[s], sems.at[3 + s]) for s in range(8)]
    point_copies = []
    items = []
    for i in range(ITEMS):
        item = jnp.minimum((t >> 1) * 18 + 2 * i + (t & 1), PAIRS - 1)
        f = item // ZB
        z = item - f * ZB
        q = jnp.maximum(f - 3, 0)
        items.append(f)
        point_copies.append(
            pltpu.make_async_copy(point_maps.at[jnp.minimum(f, 2), z], of_maps.at[i], sems.at[11 + i])
        )
        point_copies.append(
            pltpu.make_async_copy(point_coils.at[q >> 1, :, q & 1, z], of_coils.at[i], sems.at[20 + i])
        )
    for copy in copies + point_copies + mask_copies:
        copy.start()
    for copy in copies:
        copy.wait()
    lane = iota((8, LANES), 1)
    spare = jnp.where(lane == 64, stamp[0], jnp.where(lane == 65, stamp[1], 0.0))

    def emit(g, u, tile):
        dense[g, u] = tile
        if u == TILES - 1:
            tile = jnp.where(lane < 64, tile, spare)
        for m in (g, g + 4):
            send[8 * m : 8 * m + 8, u * LANES : (u + 1) * LANES] = tile

    dense_tiles(maps, coils, stacked, turned, emit)
    for copy in point_copies:
        copy.wait()
    for i in range(ITEMS):
        for g in range(4):
            tile = jnp.where(items[i] < 3, of_maps[i], of_coils[i, g])
            for m in (g, g + 4):
                send[8 * m : 8 * m + 8, MSG + i * NY : MSG + (i + 1) * NY] = tile
    for copy in mask_copies:
        copy.wait()


def dense_kernel(maps, coils, dense, stacked, turned):
    def emit(g, u, tile):
        dense[g, u] = tile

    dense_tiles(maps, coils, stacked, turned, emit)


def forward_kernel(own, other, table_y, table_z, spectrum, point, taus, direction, main, rest):
    step = pl.program_id(0)
    t, core = lax.axis_index("ti"), lax.axis_index("kz") & 1

    @pl.when(step == 0)
    def _():
        for part, c in ((own, core), (other, 1 - core)):
            for j in range(MAIN):
                main[j * 64 : (j + 1) * 64, :] = part[:, j * LANES : (j + 1) * LANES]
            for y in range(4):
                for half in range(2):
                    rows = [
                        main[pl.ds(8 * 64 * side + 4 * (8 * half + i) + y, 8, stride=64), :]
                        for i in range(8)
                        for side in range(2)
                    ]
                    pairs = jnp.swapaxes(jnp.concatenate(rows, axis=0), 0, 1)
                    direction[half, pl.ds(2 * y + c, LANES, stride=8), :] = pairs
            for v in range(2):
                rest[v, pl.ds(c, 64, stride=2), :] = part[:, (MAIN + v) * LANES : (MAIN + v + 1) * LANES]
            for i in range(ITEMS):
                for half in range(2):
                    side = slice(MSG + i * NY + half * LANES, MSG + i * NY + (half + 1) * LANES)
                    for m in range(8):
                        n = 18 * m + 2 * i
                        if n < PAIRS:
                            point[half, pl.ds(8 * n + c, 8, stride=2), :] = part[8 * m : 8 * m + 8, side]
        for v in range(2):
            for half in range(2):
                tiles = [rest[v, 8 * (8 * half + i) : 8 * (8 * half + i) + 8] for i in range(8)]
                for member, tile in enumerate(block_transpose(tiles)):
                    n = LANES + 8 * v + member
                    if n < PAIRS:
                        direction[half, 8 * n : 8 * n + 8] = tile

    block = rest[1, pl.ds(pl.multiple_of(((t & 8) + step) * 8, 8), 8), :]
    chosen = (iota((8, LANES), 0) == 0) & (iota((8, LANES), 1) == 64 + core)
    tau = jnp.sum(jnp.where(chosen, block, 0.0), axis=(0, 1), keepdims=True)
    taus[0] = jnp.broadcast_to(tau, (8, LANES))

    amplitude = plane(point, 1)
    decays = jnp.exp(-tau * plane(point, 2))
    signal = plane(point, 0) - amplitude * decays
    change = plane(direction, 0) - plane(direction, 1) * decays + amplitude * tau * decays * plane(direction, 2)
    evens, odds = [], []
    for c in range(2):
        re = plane(point, 3 + c) * change + plane(direction, 3 + c) * signal
        im = plane(point, 5 + c) * change + plane(direction, 5 + c) * signal
        re_low, re_high, im_low, im_high = re[:, :HALF_Y], re[:, HALF_Y:], im[:, :HALF_Y], im[:, HALF_Y:]
        evens.append(jnp.concatenate([re_low + re_high, im_low + im_high], axis=1))
        odds.append(jnp.concatenate([re_low - re_high, im_low - im_high], axis=1))
    along_even = times_right(jnp.concatenate(evens, axis=0), table_y[0])
    along_odd = times_right(jnp.concatenate(odds, axis=0), table_y[1])
    for c in range(2):
        rows = slice(c * NZ, (c + 1) * NZ)
        re = jnp.concatenate([along_even[rows, :HALF_Y], along_odd[rows, :HALF_Y]], axis=1)
        im = jnp.concatenate([along_even[rows, HALF_Y:], along_odd[rows, HALF_Y:]], axis=1)
        parts = [
            times_left(table_z[parity], jnp.concatenate(pair, axis=0))
            for parity, pair in enumerate(zip(split_rows(re), split_rows(im)))
        ]
        for part in range(2):
            a, b = (side[part * HALF_Z : (part + 1) * HALF_Z] for side in parts)
            spectrum[0, c, part, :HALF_Z] = a + b
            spectrum[0, c, part, HALF_Z:] = a - b


def backward_kernel(mask, spectrum, point, taus, table_y, table_z, order, mine, theirs, total, sent, rest):
    step = pl.program_id(0)
    core = lax.axis_index("kz") & 1

    @pl.when(step == 0)
    def _():
        total[...] = jnp.zeros_like(total)

    tau = taus[0, 0:1, 0:1]
    weights = jnp.dot(mask[0].astype(f32).astype(bf16), order[...], preferred_element_type=f32)
    evens, odds = [], []
    for c in range(2):
        plus, minus = [], []
        for part in range(2):
            values = spectrum[0, c, part] * weights
            plus.append(values[:HALF_Z] + values[HALF_Z:])
            minus.append(values[:HALF_Z] - values[HALF_Z:])
        for parity, side in enumerate((plus, minus)):
            out = times_left(table_z[parity], jnp.concatenate(side, axis=0))
            re, im = out[:HALF_Z], out[HALF_Z:]
            evens.append(jnp.concatenate([re[:, :HALF_Y], im[:, :HALF_Y]], axis=1))
            odds.append(jnp.concatenate([re[:, HALF_Y:], im[:, HALF_Y:]], axis=1))
    from_even = times_right(jnp.concatenate(evens, axis=0), table_y[0])
    from_odd = times_right(jnp.concatenate(odds, axis=0), table_y[1])
    low, high = from_even + from_odd, from_even - from_odd

    def add(f, values):
        for half in range(2):
            total[half, f * NZ : (f + 1) * NZ] += values[:, half * LANES : (half + 1) * LANES]

    amplitude = plane(point, 1)
    decays = jnp.exp(-tau * plane(point, 2))
    signal = plane(point, 0) - amplitude * decays
    projected = None
    for c in range(2):
        sides = []
        for lanes in (slice(0, HALF_Y), slice(HALF_Y, NY)):
            value = jnp.concatenate([low[:, lanes], high[:, lanes]], axis=1)
            first = 2 * c * HALF_Z
            sides.append(join_rows(value[first : first + HALF_Z], value[first + HALF_Z : first + NZ]))
        re, im = sides
        term = plane(point, 3 + c) * re + plane(point, 5 + c) * im
        projected = term if projected is None else projected + term
        add(3 + c, signal * re)
        add(5 + c, signal * im)
    add(0, projected)
    faded = decays * projected
    add(1, -faded)
    add(2, amplitude * (tau * faded))

    @pl.when(step == 7)
    def _():
        for k in range(8):
            slot = (k & 1) ^ core
            for half in range(2):
                pairs = jnp.swapaxes(total[half, pl.ds(k, LANES, stride=8), :], 0, 1)
                for i in range(8):
                    for side in range(2):
                        first = 8 * 64 * side + 4 * (8 * half + i) + (k >> 1)
                        rows = slice(16 * i + 8 * side, 16 * i + 8 * side + 8)
                        sent[slot, pl.ds(first, 8, stride=64), :] = pairs[rows]
        for v in range(2):
            for half in range(2):
                tiles = []
                for member in range(8):
                    n = min(LANES + 8 * v + member, PAIRS - 1)
                    tiles.append(total[half, 8 * n : 8 * n + 8])
                for i, tile in enumerate(block_transpose(tiles)):
                    rest[v, 8 * (8 * half + i) : 8 * (8 * half + i) + 8] = tile
            for c in range(2):
                rows = pl.ds((MAIN + v) * 64, 64)
                sent[c ^ core, rows, :] = rest[v, pl.ds(c, 64, stride=2), :]
        for u in range(TILES):
            mine[:, u * LANES : (u + 1) * LANES] = sent[0, u * 64 : (u + 1) * 64]
            theirs[:, u * LANES : (u + 1) * LANES] = sent[1, u * 64 : (u + 1) * 64]


def sums_kernel(received, direction, residual, applied, out_sums):
    lane = iota((8, LANES), 1)
    sums = [jnp.zeros((8, LANES), f32) for _ in range(4)]
    for u in range(TILES):
        sides = []
        for g in range(4):
            upper, lower = (received[8 * m : 8 * m + 8, u * LANES : (u + 1) * LANES] for m in (g, g + 4))
            sides.append(upper + lower)
        if u < MAIN:
            maps = sides[0] + sides[1] + sides[2] + sides[3]
        for g in range(4):
            d, r, value = direction[g, u], residual[g, u], sides[g]
            if u < MAIN:
                of_maps = lane < 3 * ZB
                if g == 0:
                    value = jnp.where(of_maps, maps, value)
                else:
                    d, r, value = (jnp.where(of_maps, 0.0, a) for a in (d, r, value))
            elif u == TILES - 1:
                d, r, value = (jnp.where(lane < 64, a, 0.0) for a in (d, r, value))
            q = value + regular_weight * d
            applied[g, u] = q
            for i, (a, b) in enumerate(((r, r), (d, q), (r, q), (q, q))):
                sums[i] = sums[i] + a * b
    line = jnp.zeros((1, LANES), f32)
    for i in range(4):
        value = jnp.sum(sums[i], axis=(0, 1), keepdims=True)
        line = jnp.where(iota((1, LANES), 1) == i, value, line)
    out_sums[...] = jnp.broadcast_to(line, (LANES, LANES))


def native_kernel(dense, maps, coils, stacked, turned):
    for g in range(4):
        for j in range(MAIN):
            turned[g, pl.ds(j, 8, stride=YB), :] = dense[g, j]
        stacked[g, :LANES] = jnp.swapaxes(turned[g], 0, 1)
        for v in range(2):
            stacked[g, LANES + 8 * v : LANES + 8 * v + 8] = inner_transpose(dense[g, MAIN + v])
        for i, name in enumerate(names_of(g)):
            if name < 3 and g:
                continue
            block = jnp.swapaxes(stacked[g, i * ZB : (i + 1) * ZB], 0, 1).reshape(XS, YB, ZB)
            if name < 3:
                maps[name] = block
            else:
                coils[(name - 3) // 8, (name - 3) % 8] = block


def step_kernel(sums, app_maps, app_coils, dir_maps, dir_coils, res_maps, res_coils, *outs):
    line = jnp.sum(sums[...], axis=0, keepdims=True)
    lane = iota((1, LANES), 1)
    old, curve, cross, square = (
        jnp.sum(jnp.where(lane == i, line, 0.0), axis=1, keepdims=True) for i in range(4)
    )
    size = old / curve
    new = old - 2.0 * size * cross + size * size * square
    ratio = (new / old).reshape(1, 1, 1)
    size = size.reshape(1, 1, 1)
    for f in range(3):
        fresh = res_maps[f] - size * app_maps[f]
        outs[0][f] = fresh
        outs[2][f] = fresh + ratio * dir_maps[f]
    for part in range(2):
        for coil in range(8):
            fresh = res_coils[part, coil] - size * app_coils[part, coil]
            outs[1][part, coil] = fresh
            outs[3][part, coil] = fresh + ratio * dir_coils[part, coil]


def struct(*shape):
    return jax.ShapeDtypeStruct(shape, f32)


ANY = pl.BlockSpec(memory_space=pl.ANY)
VMEM = pl.BlockSpec(memory_space=pltpu.VMEM)
SCRATCH_STACKED = pltpu.VMEM((4, 144, LANES), f32)
SCRATCH_TURNED = pltpu.VMEM((4, LANES, LANES), f32)


def params():
    return pltpu.CompilerParams(vmem_limit_bytes=VMEM_LIMIT)


def cost(micros):
    return pl.CostEstimate(flops=int(micros * 4e8), bytes_accessed=int(micros * 2e6), transcendentals=0)


def constant_block(shape):
    return pl.BlockSpec(shape, lambda s: (0,) * len(shape))


def stepping_block(shape):
    return pl.BlockSpec((1,) + shape, lambda s: (s,) + (0,) * len(shape))


def core_swap(values):
    return lax.ppermute(values, "kz", [(i, i ^ 1) for i in range(8)])


def by_parity(values):
    groups = [[i for i in range(128) if i & 1 == c] for c in range(2)]
    return lax.all_to_all(values, AXES, 0, 0, axis_index_groups=groups, tiled=True)


def shards(
    point_maps,
    point_coils,
    direction_maps,
    direction_coils,
    residual_maps,
    residual_coils,
    inversion_times,
    sampling_mask,
):
    forward_y, forward_z, backward_y, backward_z, order = (jnp.asarray(table) for table in make_tables())
    dir_maps, dir_coils = jnp.swapaxes(direction_maps, 2, 3), jnp.swapaxes(direction_coils, 3, 4)
    res_maps, res_coils = jnp.swapaxes(residual_maps, 2, 3), jnp.swapaxes(residual_coils, 3, 4)
    pnt_maps = jnp.swapaxes(point_maps, 1, 2)
    pnt_coils = jnp.swapaxes(point_coils, 2, 3).reshape(2, 4, 2, ZB, XS, NY)

    send, dir_dense, mask_send = pl.pallas_call(
        pack_kernel,
        out_shape=(
            struct(64, 2 * MSG),
            struct(4, TILES, 8, LANES),
            jax.ShapeDtypeStruct((8, NZ, NY), jnp.int32),
        ),
        in_specs=[ANY] * 6,
        out_specs=(VMEM, VMEM, ANY),
        scratch_shapes=[
            pltpu.VMEM(dir_maps.shape, f32),
            pltpu.VMEM(dir_coils.shape, f32),
            pltpu.VMEM((ITEMS, 8, NY), f32),
            pltpu.VMEM((ITEMS, 4, 8, NY), f32),
            pltpu.SMEM((2,), f32),
            SCRATCH_STACKED,
            SCRATCH_TURNED,
            pltpu.SemaphoreType.DMA((29,)),
        ],
        compiler_params=params(),
        cost_estimate=cost(4),
        name="pack",
    )(inversion_times, sampling_mask, dir_maps, dir_coils, pnt_maps, pnt_coils)

    def densify(maps, coils):
        return pl.pallas_call(
            dense_kernel,
            out_shape=struct(4, TILES, 8, LANES),
            in_specs=[VMEM] * 2,
            out_specs=VMEM,
            scratch_shapes=[SCRATCH_STACKED, SCRATCH_TURNED],
            compiler_params=params(),
            cost_estimate=cost(3),
            name="dense",
        )(maps, coils)

    res_dense = densify(res_maps, res_coils)
    own = by_parity(send)
    other = core_swap(own)
    mask_send, own = lax.optimization_barrier((mask_send, own))
    groups = [[8 * b + i for i in range(8)] for b in range(2)]
    masks = lax.all_to_all(mask_send, "ti", 0, 0, axis_index_groups=groups, tiled=True)

    spectrum, point, taus = pl.pallas_call(
        forward_kernel,
        grid=(8,),
        out_shape=(struct(8, 2, 2, NZ, NY), struct(2, FEATURES * NZ, LANES), struct(8, 8, LANES)),
        in_specs=[constant_block(a.shape) for a in (own, other, forward_y, forward_z)],
        out_specs=(
            stepping_block((2, 2, NZ, NY)),
            constant_block((2, FEATURES * NZ, LANES)),
            stepping_block((8, LANES)),
        ),
        scratch_shapes=[
            pltpu.VMEM((2, FEATURES * NZ, LANES), f32),
            pltpu.VMEM((MAIN * 64, LANES), f32),
            pltpu.VMEM((2, LANES, LANES), f32),
        ],
        compiler_params=params(),
        cost_estimate=cost(12),
        name="forward",
    )(own, other, forward_y, forward_z)

    mine, theirs = pl.pallas_call(
        backward_kernel,
        grid=(8,),
        out_shape=(struct(64, MSG), struct(64, MSG)),
        in_specs=[
            stepping_block((NZ, NY)),
            stepping_block((2, 2, NZ, NY)),
            constant_block((2, FEATURES * NZ, LANES)),
            stepping_block((8, LANES)),
        ]
        + [constant_block(a.shape) for a in (backward_y, backward_z, order)],
        out_specs=(constant_block((64, MSG)),) * 2,
        scratch_shapes=[
            pltpu.VMEM((2, FEATURES * NZ, LANES), f32),
            pltpu.VMEM((2, TILES * 64, LANES), f32),
            pltpu.VMEM((2, LANES, LANES), f32),
        ],
        compiler_params=params(),
        cost_estimate=cost(12),
        name="backward",
    )(masks, spectrum, point, taus, backward_y, backward_z, order)

    received = by_parity(mine + core_swap(theirs))
    app_dense, sums = pl.pallas_call(
        sums_kernel,
        out_shape=(struct(4, TILES, 8, LANES), struct(128, LANES)),
        in_specs=[VMEM] * 3,
        out_specs=(VMEM,) * 2,
        compiler_params=params(),
        cost_estimate=cost(1),
        name="sums",
    )(received, dir_dense, res_dense)
    all_sums = lax.all_to_all(sums.reshape(128, 1, LANES), AXES, 0, 0).reshape(128, LANES)

    maps_shape, coils_shape = struct(*dir_maps.shape), struct(*dir_coils.shape)
    app_maps, app_coils = pl.pallas_call(
        native_kernel,
        out_shape=(maps_shape, coils_shape),
        in_specs=[VMEM],
        out_specs=(VMEM,) * 2,
        scratch_shapes=[SCRATCH_STACKED, SCRATCH_TURNED],
        compiler_params=params(),
        cost_estimate=cost(3),
        name="native",
    )(app_dense)

    outs = pl.pallas_call(
        step_kernel,
        out_shape=(maps_shape, coils_shape, maps_shape, coils_shape),
        in_specs=[VMEM] * 7,
        out_specs=(VMEM,) * 4,
        compiler_params=params(),
        cost_estimate=cost(2),
        name="step",
    )(all_sums, app_maps, app_coils, dir_maps, dir_coils, res_maps, res_coils)
    return tuple(jnp.swapaxes(out, -2, -1) for out in outs)


def solution(mesh):
    in_specs = (
        P(None, None, "kz", None),
        P(None, None, None, "kz", None),
        P(None, None, "kz", "ti"),
        P(None, None, None, "kz", "ti"),
        P(None, None, "kz", "ti"),
        P(None, None, None, "kz", "ti"),
        P("ti"),
        P("ti", None, None),
    )
    out_specs = (
        P(None, None, "kz", "ti"),
        P(None, None, None, "kz", "ti"),
        P(None, None, "kz", "ti"),
        P(None, None, None, "kz", "ti"),
    )
    return jax.shard_map(shards, mesh=mesh, in_specs=in_specs, out_specs=out_specs, check_vma=False)
```

time: 133 us -> 124 us (0.932)
  blocking collectives: 64.5 us -> 30.2 us
  waiting for transfers between devices: 5.31 us -> 23 us
  local copies, waits for them, and re-layouts: 6.91 us -> 23.8 us
  Pallas kernels: 42.3 us -> 27.5 us
  starting transfers between devices: 12.8 us -> 17.8 us
    all_to_all x3 -> x1, blocking collectives: 64.5 us -> 30.2 us  [by_parity(): lax.all_to_all(values, AXES, 0, 0, axis_index_groups=groups, tiled=True)]
    all_to_all x0 -> x3, waiting for transfers between devices: none -> 21.4 us  [the longest x1 11.4 us: by_parity(): lax.all_to_all(values, AXES, 0, 0, axis_index_groups=groups, tiled=True)]
    unnamed x32 -> x54, local copies, waits for them, and re-layouts: 5.07 us -> 21.1 us
    all_to_all x0 -> x3, starting transfers between devices: none -> 14.4 us  [the longest x1 5.39 us: shards(): lax.all_to_all(sums.reshape(128, 1, LANES), AXES, 0, 0).reshape(128, LANES)]
    pallas_call x3 -> x5, Pallas kernels: 26.5 us -> 16 us  [the longest x1 9.63 us: shards(): pl.pallas_call(backward_kernel, grid=(8,), out_shape=(struct(64, MSG), st...]
    ppermute x7 -> x0, starting transfers between devices: 9.57 us -> none  [shards(): masks.append(lax.ppermute(own_mask, 'ti', pairs))]
    pallas_call x1, Pallas kernels: 14.2 us -> 9.8 us  [shards(): pl.pallas_call(forward_kernel, grid=(8,), out_shape=(struct(8, 2, 2, NZ,...]
    ppermute x7 -> x0, waiting for transfers between devices: 3.68 us -> none  [shards(): masks.append(lax.ppermute(own_mask, 'ti', pairs))]
  transfers between devices with their start and end apart: 9 -> 5, of which waited for: 3 -> 4; matrix products, arithmetic and copies ran while one was open for 0% -> 0% of each run, Pallas kernels for 11% -> 10%
where the time goes in v2:
time: 124 us; the launch traced here: 123 us
  blocking collectives  30.2 us (24%)
  Pallas kernels  27.5 us (22%)
  local copies, waits for them, and re-layouts  23.8 us (19%)
  waiting for transfers between devices  23 us (19%)
  starting transfers between devices  17.8 us (14%)
    all_to_all x1, blocking collectives, by_parity(): lax.all_to_all(values, AXES, 0, 0, axis_index_groups=groups, tiled=True)  30.2 us
    unnamed x54, local copies, waits for them, and re-layouts  21.1 us
    all_to_all x1, waiting for transfers between devices, by_parity(): lax.all_to_all(values, AXES, 0, 0, axis_index_groups=groups, tiled=True)  11.4 us
    pallas_call x1, Pallas kernels, shards(): pl.pallas_call(forward_kernel, grid=(8,), out_shape=(struct(8, 2, 2, NZ,...  9.8 us
    pallas_call x1, Pallas kernels, shards(): pl.pallas_call(backward_kernel, grid=(8,), out_shape=(struct(64, MSG), st...  9.63 us
    all_to_all x1, waiting for transfers between devices, shards(): lax.all_to_all(sums.reshape(128, 1, LANES), AXES, 0, 0).reshape(128, LANES)  6.58 us
    all_to_all x1, starting transfers between devices, shards(): lax.all_to_all(sums.reshape(128, 1, LANES), AXES, 0, 0).reshape(128, LANES)  5.39 us
    all_to_all x1, starting transfers between devices, by_parity(): lax.all_to_all(values, AXES, 0, 0, axis_index_groups=groups, tiled=True)  5.39 us
  transfers between devices with their start and end apart: 5, of which 4 were waited for; matrix products, arithmetic and copies ran while one was open for 0% of the time, Pallas kernels for 10%

profile of v2, /device:TPU:1, one launch (start us, length us, event | category | flops | bytes accessed | tf_op | source)
XLA Modules:
  0.0 123.2 jit_solution(459946919050462777)
XLA Ops:
  0.6 1.2 copy-done
  2.8 1.7 %copy-done.9 = f32[2,8,8,20,256]{4,2,3,1,0:T(8,128)S(1)} copy-done((f32[2,8,8,20,256]{4,2,3,1,0:T(8,128)S(1)}, f32[2,8,8,20,256]{4,2,3,1,0:T(8,128)}, u32[]{:S(2)}) %copy-start.9) | copy-done | bytes 2621464
  4.5 1.0 copy-done.10
  7.2 2.6 %pack.1 = (f32[64,4608]{1,0:T(8,128)S(1)}, f32[4,18,8,128]{3,2,1,0:T(8,128)S(1)}, s32[8,160,256]{2,1,0:T(8,128)}) custom-call(f32[2]{0:T(128)S(1)} %copy-done.12, s32[2,160,256]{2,1,0:T(8,128)S(1)} %copy-done.11, f32[3,8,16,20]{3,2,1,0:T(8,128)S(1)} %bitcast.34, f32[2,8,8,16,20]{4,3,2,1,0:T(8,128)S(1)} %bitcast.28, f32[3,20,8,256]{3,2,1,0:T(8,128)S(1)} %bitcast.39, ...), custom_call_target="tpu_custom_call" | custom-call | flops 1600000000 | bytes 8000000 | tf_op jit(solution)/shard_map/pack/pallas_call | solution.py:475
  9.8 1.2 copy.17
  11.1 30.2 %all_to_all.33 = f32[64,1,4608]{2,1,0:T(1,128)S(1)} all-to-all(f32[64,1,4608]{2,1,0:T(1,128)S(1)} %copy.17), channel_id=1, replica_groups={{0,2,4,6,8,10,12,14,16,18,20,22,24,26,28,30,32,34,36,38,40,42,44,46,48,..., dimensions={0} | all-to-all | bytes 2359296 | tf_op jit(solution)/shard_map/all_to_all | solution.py:456
  41.4 2.6 %collective-permute-start = (f32[64,4608]{1,0:T(8,128)S(1)}, f32[64,4608]{1,0:T(8,128)}, u32[]{:S(2)}, u32[]{:S(2)}) collective-permute-start(f32[64,4608]{1,0:T(8,128)S(1)} %bitcast.25), channel_id=1, source_target_pairs={{0,1},{1,0},{2,3},{3,2},{4,5},{5,4},{6,7},{7,6},{8,9},{9,8},{10,11... | collective-permute-start | bytes 3538952 | tf_op jit(solution)/shard_map/ppermute | solution.py:451
  44.0 3.6 %all-to-all-start.1 = ((s32[8,160,256]{2,1,0:T(8,128)}), s32[8,160,256]{2,1,0:T(8,128)S(1)}, u32[]{:S(2)}, u32[]{:S(2)}) async-start(s32[8,160,256]{2,1,0:T(8,128)} %get-tuple-element.24), calls=%async_computation.1 | async-start | bytes 2621440 | tf_op jit(solution)/shard_map/all_to_all | solution.py:516
  47.6 1.2 copy-done.14
  49.8 9.8 %forward.1 = (f32[8,2,2,160,256]{4,3,2,1,0:T(8,128)S(1)}, f32[2,1120,128]{2,1,0:T(8,128)S(1)}, f32[8,8,128]{2,1,0:T(8,128)S(1)}) custom-call(f32[64,4608]{1,0:T(8,128)S(1)} %bitcast.26, f32[64,4608]{1,0:T(8,128)} %collective-permute-done.other, bf16[2,768,256]{2,1,0:T(8,128)(2,1)S(1)} %copy-done.14, bf16[2,160,512]{2,1,0:T(8,128)(2,1)S(1)} %copy-done.16), custom_call_target="tpu_custom_call" | custom-call | flops 4800000000 | bytes 24000000 | tf_op jit(solution)/shard_map/forward/pallas_call | solution.py:518
  59.6 2.3 %copy-done.22 = f32[8,2,2,160,256]{4,3,2,1,0:T(8,128)} copy-done((f32[8,2,2,160,256]{4,3,2,1,0:T(8,128)}, f32[8,2,2,160,256]{4,3,2,1,0:T(8,128)S(1)}, u32[]{:S(2)}) %copy-start.22) | copy-done | bytes 5242904
  62.9 3.3 %all-to-all-done.1.mask = s32[8,160,256]{2,1,0:T(8,128)S(1)} async-done(((s32[8,160,256]{2,1,0:T(8,128)}), s32[8,160,256]{2,1,0:T(8,128)S(1)}, u32[]{:S(2)}, u32[]{:S(2)}) %all-to-all-start.1) | async-done | bytes 1310752 | tf_op jit(solution)/shard_map/all_to_all | solution.py:516
  67.3 2.5 %copy-done.23 = f32[8,2,2,160,256]{4,3,2,1,0:T(8,128)S(1)} copy-done((f32[8,2,2,160,256]{4,3,2,1,0:T(8,128)S(1)}, f32[8,2,2,160,256]{4,3,2,1,0:T(8,128)}, u32[]{:S(2)}) %copy-start.23) | copy-done | bytes 5242904
  69.8 1.3 %copy-done.25 = f32[2,1120,128]{2,1,0:T(8,128)S(1)} copy-done((f32[2,1120,128]{2,1,0:T(8,128)S(1)}, f32[2,1120,128]{2,1,0:T(8,128)}, u32[]{:S(2)}) %copy-start.25) | copy-done | bytes 1146904
  71.0 9.6 %backward.1 = (f32[64,2304]{1,0:T(8,128)S(1)}, f32[64,2304]{1,0:T(8,128)S(1)}) custom-call(s32[8,160,256]{2,1,0:T(8,128)S(1)} %all-to-all-done.1.mask, f32[8,2,2,160,256]{4,3,2,1,0:T(8,128)S(1)} %copy-done.23, f32[2,1120,128]{2,1,0:T(8,128)S(1)} %copy-done.25, f32[8,8,128]{2,1,0:T(8,128)S(1)} %get-tuple-element.28.taus, bf16[2,768,256]{2,1,0:T(8,128)(2,1)S(1)} %copy-done.13, ...), custom_call_target="tpu_custom_call" | custom-call | flops 4800000000 | bytes 24000000 | tf_op jit(solution)/shard_map/backward/pallas_call | solution.py:538
  81.4 1.6 %collective-permute-done.1 = f32[64,2304]{1,0:T(8,128)S(1)} collective-permute-done((f32[64,2304]{1,0:T(8,128)S(1)}, f32[64,2304]{1,0:T(8,128)S(1)}, u32[]{:S(2)}, u32[]{:S(2)}) %collective-permute-start.1) | collective-permute-done | bytes 589856 | tf_op jit(solution)/shard_map/ppermute | solution.py:451
  83.2 1.4 %copy.18 = f32[64,1,2304]{2,1,0:T(1,128)} copy(f32[64,1,2304]{2,0,1:T(8,128)S(1)} %add_bitcast_fusion) | data formatting | bytes 1179648 | tf_op jit(solution)/shard_map/all_to_all | solution.py:456
  84.6 5.4 %all-to-all-start.2 = ((f32[64,1,2304]{2,1,0:T(1,128)}), f32[64,1,2304]{2,1,0:T(1,128)S(1)}, u32[]{:S(2)}, u32[]{:S(2)}) async-start(f32[64,1,2304]{2,1,0:T(1,128)} %copy.18), calls=%async_computation.2 | async-start | bytes 1179648 | tf_op jit(solution)/shard_map/all_to_all | solution.py:456
  90.0 1.4 %dense.1.residual = f32[4,18,8,128]{3,2,1,0:T(8,128)S(1)} custom-call(f32[3,8,16,20]{3,2,1,0:T(8,128)S(1)} %bitcast.36, f32[2,8,8,16,20]{4,3,2,1,0:T(8,128)S(1)} %bitcast.30), custom_call_target="tpu_custom_call" | custom-call | flops 1200000000 | bytes 6000000 | tf_op jit(solution)/shard_map/dense/pallas_call | solution.py:500
  91.4 11.4 %all-to-all-done.2 = f32[64,1,2304]{2,1,0:T(1,128)S(1)} async-done(((f32[64,1,2304]{2,1,0:T(1,128)}), f32[64,1,2304]{2,1,0:T(1,128)S(1)}, u32[]{:S(2)}, u32[]{:S(2)}) %all-to-all-start.2) | async-done | bytes 589856 | tf_op jit(solution)/shard_map/all_to_all | solution.py:456
  104.6 5.4 %all-to-all-start.3 = ((f32[128,1,128]{2,1,0:T(1,128)}), f32[128,1,128]{2,1,0:T(1,128)S(1)}, u32[]{:S(2)}, u32[]{:S(2)}) async-start(f32[128,1,128]{2,1,0:T(1,128)} %bitcast.10), calls=%async_computation.3 | async-start | bytes 131072 | tf_op jit(solution)/shard_map/all_to_all | solution.py:570
  111.0 1.4 %native.1 = (f32[3,8,16,20]{3,2,1,0:T(8,128)S(1)}, f32[2,8,8,16,20]{4,3,2,1,0:T(8,128)S(1)}) custom-call(f32[4,18,8,128]{3,2,1,0:T(8,128)S(1)} %copy-done.21), custom_call_target="tpu_custom_call" | custom-call | flops 1200000000 | bytes 6000000 | tf_op jit(solution)/shard_map/native/pallas_call | solution.py:573
  113.1 6.6 %all-to-all-done.3 = f32[128,1,128]{2,1,0:T(1,128)S(1)} async-done(((f32[128,1,128]{2,1,0:T(1,128)}), f32[128,1,128]{2,1,0:T(1,128)S(1)}, u32[]{:S(2)}, u32[]{:S(2)}) %all-to-all-start.3) | async-done | bytes 65568 | tf_op jit(solution)/shard_map/all_to_all | solution.py:570
  121.5 1.7 %step.1 = (f32[3,8,16,20]{3,2,1,0:T(8,128)}, f32[2,8,8,16,20]{4,3,2,1,0:T(8,128)}, f32[3,8,16,20]{3,2,1,0:T(8,128)}, f32[2,8,8,16,20]{4,3,2,1,0:T(8,128)}) custom-call(f32[128,128]{1,0:T(8,128)S(1)} %bitcast.33, f32[3,8,16,20]{3,2,1,0:T(8,128)S(1)} %copy-done.8, f32[2,8,8,16,20]{4,3,2,1,0:T(8,128)S(1)} %get-tuple-element.35.app_coils, ...), custom_call_target="tpu_custom_call" | custom-call | flops 800000000 | bytes 4000000 | tf_op jit(solution)/shard_map/step/pallas_call | solution.py:584
  (51 shorter events, 11.7 us)
Async XLA Ops:
  0.6 1.2 copy-start
  2.8 1.7 %copy-start.9 = (f32[2,8,8,20,256]{4,2,3,1,0:T(8,128)S(1)}, f32[2,8,8,20,256]{4,2,3,1,0:T(8,128)}, u32[]{:S(2)}) copy-start(f32[2,8,8,20,256]{4,2,3,1,0:T(8,128)} %param.14) | copy-start | bytes 7864324
  4.5 1.0 copy-start.10
  5.6 1.0 copy-start.11
  9.8 1.2 %copy-start.18 = (f32[4,18,8,128]{3,2,1,0:T(8,128)}, f32[4,18,8,128]{3,2,1,0:T(8,128)S(1)}, u32[]{:S(2)}) copy-start(f32[4,18,8,128]{3,2,1,0:T(8,128)S(1)} %get-tuple-element.31.direction) | copy-start | bytes 884740
  41.4 6.2 %collective-permute-start = (f32[64,4608]{1,0:T(8,128)S(1)}, f32[64,4608]{1,0:T(8,128)}, u32[]{:S(2)}, u32[]{:S(2)}) collective-permute-start(f32[64,4608]{1,0:T(8,128)S(1)} %bitcast.25), channel_id=1, source_target_pairs={{0,1},{1,0},{2,3},{3,2},{4,5},{5,4},{6,7},{7,6},{8,9},{9,8},{10,11... | collective-permute-start | bytes 3538952 | tf_op jit(solution)/shard_map/ppermute | solution.py:451
  44.0 22.3 %all-to-all-start.1 = ((s32[8,160,256]{2,1,0:T(8,128)}), s32[8,160,256]{2,1,0:T(8,128)S(1)}, u32[]{:S(2)}, u32[]{:S(2)}) async-start(s32[8,160,256]{2,1,0:T(8,128)} %get-tuple-element.24), calls=%async_computation.1 | async-start | bytes 2621440 | tf_op jit(solution)/shard_map/all_to_all | solution.py:516
  47.6 18.7 %copy-start.13 = (bf16[2,768,256]{2,1,0:T(8,128)(2,1)S(1)}, bf16[2,768,256]{2,1,0:T(8,128)(2,1)}, u32[]{:S(2)}) copy-start(bf16[2,768,256]{2,1,0:T(8,128)(2,1)} %constant.12.clone.table_y) | copy-start | bytes 2359300
  47.6 1.2 copy-start.14
  48.8 1.0 copy-start.16
  49.8 16.5 %copy-start.17 = (bf16[256,256]{1,0:T(8,128)(2,1)S(1)}, bf16[256,256]{1,0:T(8,128)(2,1)}, u32[]{:S(2)}) copy-start(bf16[256,256]{1,0:T(8,128)(2,1)} %constant.14.clone.order) | copy-start | bytes 393220
  59.6 2.3 %copy-start.22 = (f32[8,2,2,160,256]{4,3,2,1,0:T(8,128)}, f32[8,2,2,160,256]{4,3,2,1,0:T(8,128)S(1)}, u32[]{:S(2)}) copy-start(f32[8,2,2,160,256]{4,3,2,1,0:T(8,128)S(1)} %get-tuple-element.26.spectrum) | copy-start | bytes 15728644
  61.9 1.0 copy-start.24
  66.3 1.0 copy-start.15
  67.3 2.5 %copy-start.23 = (f32[8,2,2,160,256]{4,3,2,1,0:T(8,128)S(1)}, f32[8,2,2,160,256]{4,3,2,1,0:T(8,128)}, u32[]{:S(2)}) copy-start(f32[8,2,2,160,256]{4,3,2,1,0:T(8,128)} %copy-done.22) | copy-start | bytes 15728644
  69.8 1.3 %copy-start.25 = (f32[2,1120,128]{2,1,0:T(8,128)S(1)}, f32[2,1120,128]{2,1,0:T(8,128)}, u32[]{:S(2)}) copy-start(f32[2,1120,128]{2,1,0:T(8,128)} %copy-done.24) | copy-start | bytes 3440644
  80.7 2.4 %collective-permute-start.1 = (f32[64,2304]{1,0:T(8,128)S(1)}, f32[64,2304]{1,0:T(8,128)S(1)}, u32[]{:S(2)}, u32[]{:S(2)}) collective-permute-start(f32[64,2304]{1,0:T(8,128)S(1)} %get-tuple-element.30), channel_id=1, source_target_pairs={{0,1},{1,0},{2,3},{3,2},{4,5},{5,4},{6,7},{7,6},{8,9},{9,8},{10,11... | collective-permute-start | bytes 1769480 | tf_op jit(solution)/shard_map/ppermute | solution.py:451
  83.1 6.8 %copy-start.2 = (f32[2,8,8,20,16]{3,4,2,1,0:T(8,128)S(1)}, f32[2,8,8,20,16]{3,4,2,1,0:T(8,128)}, u32[]{:S(2)}) copy-start(f32[2,8,8,20,16]{3,4,2,1,0:T(8,128)} %param.18) | copy-start | bytes 491524
  83.1 6.8 %copy-start.5 = (f32[3,8,20,16]{2,3,1,0:T(8,128)S(1)}, f32[3,8,20,16]{2,3,1,0:T(8,128)}, u32[]{:S(2)}) copy-start(f32[3,8,20,16]{2,3,1,0:T(8,128)} %param.17) | copy-start | bytes 92164
  84.6 18.3 %all-to-all-start.2 = ((f32[64,1,2304]{2,1,0:T(1,128)}), f32[64,1,2304]{2,1,0:T(1,128)S(1)}, u32[]{:S(2)}, u32[]{:S(2)}) async-start(f32[64,1,2304]{2,1,0:T(1,128)} %copy.18), calls=%async_computation.2 | async-start | bytes 1179648 | tf_op jit(solution)/shard_map/all_to_all | solution.py:456
  91.4 11.5 %copy-start.19 = (f32[4,18,8,128]{3,2,1,0:T(8,128)S(1)}, f32[4,18,8,128]{3,2,1,0:T(8,128)}, u32[]{:S(2)}) copy-start(f32[4,18,8,128]{3,2,1,0:T(8,128)} %copy-done.18) | copy-start | bytes 884740
  104.6 15.1 %all-to-all-start.3 = ((f32[128,1,128]{2,1,0:T(1,128)}), f32[128,1,128]{2,1,0:T(1,128)S(1)}, u32[]{:S(2)}, u32[]{:S(2)}) async-start(f32[128,1,128]{2,1,0:T(1,128)} %bitcast.10), calls=%async_computation.3 | async-start | bytes 131072 | tf_op jit(solution)/shard_map/all_to_all | solution.py:570
  111.0 8.7 %copy-start.1 = (f32[2,8,8,20,16]{3,4,2,1,0:T(8,128)S(1)}, f32[2,8,8,20,16]{3,4,2,1,0:T(8,128)}, u32[]{:S(2)}) copy-start(f32[2,8,8,20,16]{3,4,2,1,0:T(8,128)} %param.16) | copy-start | bytes 491524
  111.0 8.7 %copy-start.4 = (f32[3,8,20,16]{2,3,1,0:T(8,128)S(1)}, f32[3,8,20,16]{2,3,1,0:T(8,128)}, u32[]{:S(2)}) copy-start(f32[3,8,20,16]{2,3,1,0:T(8,128)} %param.15) | copy-start | bytes 92164
  (7 other events, 5.8 us)

commit v3 on v2

--- a/solution.py
+++ b/solution.py
@@ -19,6 +19,7 @@
 TILES = 18
 MSG = TILES * LANES
 ITEMS = 9
+WHOLE = 2 * TILES
 VMEM_LIMIT = 32 * 1024 * 1024
 f32 = jnp.float32
 bf16 = jnp.bfloat16
@@ -129,9 +130,11 @@
     return [0, 1, 2] + [3 + 8 * p + 2 * g + e for p in range(2) for e in range(2)]
 
 
-def dense_tiles(maps, coils, stacked, turned, emit):
+def dense_tiles(maps, coils, stacked, turned, emit, arrive=None):
     blank = jnp.zeros((8, LANES), f32)
     for g in range(4):
+        if arrive is not None:
+            arrive(g)
         stacked[g, 136:144] = blank
         for i, name in enumerate(names_of(g)):
             if name < 3:
@@ -152,15 +155,22 @@
 def pack_kernel(
     times, mask, maps_in, coils_in, point_maps, point_coils,
     send, dense, mask_send,
-    maps, coils, of_maps, of_coils, stamp, stacked, turned, sems,
+    maps, coils, of_maps, of_coils, stamp, own_mask, stacked, turned, sems,
 ):
     t, core = lax.axis_index("ti"), lax.axis_index("kz") & 1
-    copies = [
-        pltpu.make_async_copy(maps_in, maps, sems.at[0]),
-        pltpu.make_async_copy(coils_in, coils, sems.at[1]),
-        pltpu.make_async_copy(times, stamp, sems.at[2]),
+    mask_copy = pltpu.make_async_copy(mask.at[core], own_mask, sems.at[0])
+    mask_copies = [pltpu.make_async_copy(own_mask, mask_send.at[s], sems.at[1 + s]) for s in range(8)]
+    maps_copies = [
+        pltpu.make_async_copy(maps_in, maps, sems.at[9]),
+        pltpu.make_async_copy(times, stamp, sems.at[10]),
     ]
-    mask_copies = [pltpu.make_async_copy(mask.at[core], mask_send.at[s], sems.at[3 + s]) for s in range(8)]
+    coils_copies = [
+        pltpu.make_async_copy(
+            coils_in.at[p, pl.ds(2 * g, 2)], coils.at[p, pl.ds(2 * g, 2)], sems.at[11 + 2 * g + p]
+        )
+        for g in range(4)
+        for p in range(2)
+    ]
     point_copies = []
     items = []
     for i in range(ITEMS):
@@ -170,71 +180,99 @@
         q = jnp.maximum(f - 3, 0)
         items.append(f)
         point_copies.append(
-            pltpu.make_async_copy(point_maps.at[jnp.minimum(f, 2), z], of_maps.at[i], sems.at[11 + i])
+            pltpu.make_async_copy(point_maps.at[jnp.minimum(f, 2), z], of_maps.at[i], sems.at[19 + i])
         )
         point_copies.append(
-            pltpu.make_async_copy(point_coils.at[q >> 1, :, q & 1, z], of_coils.at[i], sems.at[20 + i])
+            pltpu.make_async_copy(point_coils.at[q >> 1, :, q & 1, z], of_coils.at[i], sems.at[28 + i])
         )
-    for copy in copies + point_copies + mask_copies:
+    for copy in point_copies + maps_copies + coils_copies + [mask_copy]:
         copy.start()
-    for copy in copies:
-        copy.wait()
-    lane = iota((8, LANES), 1)
-    spare = jnp.where(lane == 64, stamp[0], jnp.where(lane == 65, stamp[1], 0.0))
-
-    def emit(g, u, tile):
-        dense[g, u] = tile
-        if u == TILES - 1:
-            tile = jnp.where(lane < 64, tile, spare)
-        for m in (g, g + 4):
-            send[8 * m : 8 * m + 8, u * LANES : (u + 1) * LANES] = tile
-
-    dense_tiles(maps, coils, stacked, turned, emit)
     for copy in point_copies:
         copy.wait()
     for i in range(ITEMS):
         for g in range(4):
             tile = jnp.where(items[i] < 3, of_maps[i], of_coils[i, g])
             for m in (g, g + 4):
-                send[8 * m : 8 * m + 8, MSG + i * NY : MSG + (i + 1) * NY] = tile
+                for half in range(2):
+                    first = 8 * m * WHOLE + TILES + 2 * i + half
+                    send[pl.ds(first, 8, stride=WHOLE), :] = tile[:, half * LANES : (half + 1) * LANES]
+    for copy in maps_copies:
+        copy.wait()
+    lane = iota((8, LANES), 1)
+    spare = jnp.where(lane == 64, stamp[0], jnp.where(lane == 65, stamp[1], 0.0))
+
+    def emit(g, u, tile):
+        dense[g, u] = tile
+        if u == TILES - 1:
+            tile = jnp.where(lane < 64, tile, spare)
+        for m in (g, g + 4):
+            send[pl.ds(8 * m * WHOLE + u, 8, stride=WHOLE), :] = tile
+
+    def arrive(g):
+        if g == 1:
+            mask_copy.wait()
+            for copy in mask_copies:
+                copy.start()
+        for copy in coils_copies[2 * g : 2 * g + 2]:
+            copy.wait()
+
+    dense_tiles(maps, coils, stacked, turned, emit, arrive)
     for copy in mask_copies:
         copy.wait()
 
 
-def dense_kernel(maps, coils, dense, stacked, turned):
+def dense_kernel(maps_in, coils_in, dense, maps, coils, stacked, turned, sems):
+    copies = [
+        pltpu.make_async_copy(maps_in, maps, sems.at[0]),
+        pltpu.make_async_copy(coils_in, coils, sems.at[1]),
+    ]
+    for copy in copies:
+        copy.start()
+    for copy in copies:
+        copy.wait()
+
     def emit(g, u, tile):
         dense[g, u] = tile
 
     dense_tiles(maps, coils, stacked, turned, emit)
 
 
-def forward_kernel(own, other, table_y, table_z, spectrum, point, taus, direction, main, rest):
+def forward_kernel(
+    own, other, table_y_in, table_z_in,
+    spectrum, point, taus,
+    direction, rest, table_y, table_z, kept, sems,
+):
     step = pl.program_id(0)
     t, core = lax.axis_index("ti"), lax.axis_index("kz") & 1
+    slot = step & 1
+    tables = [
+        pltpu.make_async_copy(table_y_in, table_y, sems.at[2]),
+        pltpu.make_async_copy(table_z_in, table_z, sems.at[3]),
+    ]
+
+    def store(at, side):
+        return pltpu.make_async_copy(kept.at[side], spectrum.at[at], sems.at[side])
 
     @pl.when(step == 0)
     def _():
+        for copy in tables:
+            copy.start()
         for part, c in ((own, core), (other, 1 - core)):
-            for j in range(MAIN):
-                main[j * 64 : (j + 1) * 64, :] = part[:, j * LANES : (j + 1) * LANES]
             for y in range(4):
                 for half in range(2):
-                    rows = [
-                        main[pl.ds(8 * 64 * side + 4 * (8 * half + i) + y, 8, stride=64), :]
-                        for i in range(8)
-                        for side in range(2)
-                    ]
+                    firsts = [WHOLE * (4 * (8 * half + i) + y) for i in range(8)]
+                    rows = [part[first : first + MAIN, :] for first in firsts]
                     pairs = jnp.swapaxes(jnp.concatenate(rows, axis=0), 0, 1)
                     direction[half, pl.ds(2 * y + c, LANES, stride=8), :] = pairs
             for v in range(2):
-                rest[v, pl.ds(c, 64, stride=2), :] = part[:, (MAIN + v) * LANES : (MAIN + v + 1) * LANES]
+                rest[v, pl.ds(c, 64, stride=2), :] = part[pl.ds(MAIN + v, 64, stride=WHOLE), :]
             for i in range(ITEMS):
                 for half in range(2):
-                    side = slice(MSG + i * NY + half * LANES, MSG + i * NY + (half + 1) * LANES)
                     for m in range(8):
                         n = 18 * m + 2 * i
                         if n < PAIRS:
-                            point[half, pl.ds(8 * n + c, 8, stride=2), :] = part[8 * m : 8 * m + 8, side]
+                            first = 8 * m * WHOLE + TILES + 2 * i + half
+                            point[half, pl.ds(8 * n + c, 8, stride=2), :] = part[pl.ds(first, 8, stride=WHOLE), :]
         for v in range(2):
             for half in range(2):
                 tiles = [rest[v, 8 * (8 * half + i) : 8 * (8 * half + i) + 8] for i in range(8)]
@@ -242,6 +280,12 @@
                     n = LANES + 8 * v + member
                     if n < PAIRS:
                         direction[half, 8 * n : 8 * n + 8] = tile
+        for copy in tables:
+            copy.wait()
+
+    @pl.when(step >= 2)
+    def _():
+        store(step - 2, slot).wait()
 
     block = rest[1, pl.ds(pl.multiple_of(((t & 8) + step) * 8, 8), 8), :]
     chosen = (iota((8, LANES), 0) == 0) & (iota((8, LANES), 1) == 64 + core)
@@ -271,17 +315,47 @@
         ]
         for part in range(2):
             a, b = (side[part * HALF_Z : (part + 1) * HALF_Z] for side in parts)
-            spectrum[0, c, part, :HALF_Z] = a + b
-            spectrum[0, c, part, HALF_Z:] = a - b
-
-
-def backward_kernel(mask, spectrum, point, taus, table_y, table_z, order, mine, theirs, total, sent, rest):
+            kept[slot, c, part, :HALF_Z] = a + b
+            kept[slot, c, part, HALF_Z:] = a - b
+    store(step, slot).start()
+
+    @pl.when(step == 7)
+    def _():
+        store(6, 0).wait()
+        store(7, 1).wait()
+
+
+def backward_kernel(
+    mask, spectrum, point, taus, table_y_in, table_z_in, order_in,
+    mine, theirs,
+    total, sent, rest, table_y, table_z, order, kept, sems,
+):
     step = pl.program_id(0)
     core = lax.axis_index("kz") & 1
+    slot = step & 1
+    tables = [
+        pltpu.make_async_copy(order_in, order, sems.at[4]),
+        pltpu.make_async_copy(table_z_in, table_z, sems.at[3]),
+        pltpu.make_async_copy(table_y_in, table_y, sems.at[2]),
+    ]
+
+    def load(at, side):
+        return pltpu.make_async_copy(spectrum.at[at], kept.at[side], sems.at[side])
 
     @pl.when(step == 0)
     def _():
+        load(0, 0).start()
+        for copy in tables:
+            copy.start()
         total[...] = jnp.zeros_like(total)
+        for copy in tables:
+            copy.wait()
+
+    @pl.when(step < 7)
+    def _():
+        load(step + 1, 1 - slot).start()
+
+    load(step, slot).wait()
 
     tau = taus[0, 0:1, 0:1]
     weights = jnp.dot(mask[0].astype(f32).astype(bf16), order[...], preferred_element_type=f32)
@@ -289,7 +363,7 @@
     for c in range(2):
         plus, minus = [], []
         for part in range(2):
-            values = spectrum[0, c, part] * weights
+            values = kept[slot, c, part] * weights
             plus.append(values[:HALF_Z] + values[HALF_Z:])
             minus.append(values[:HALF_Z] - values[HALF_Z:])
         for parity, side in enumerate((plus, minus)):
@@ -328,14 +402,12 @@
     @pl.when(step == 7)
     def _():
         for k in range(8):
-            slot = (k & 1) ^ core
+            place = (k & 1) ^ core
             for half in range(2):
                 pairs = jnp.swapaxes(total[half, pl.ds(k, LANES, stride=8), :], 0, 1)
                 for i in range(8):
-                    for side in range(2):
-                        first = 8 * 64 * side + 4 * (8 * half + i) + (k >> 1)
-                        rows = slice(16 * i + 8 * side, 16 * i + 8 * side + 8)
-                        sent[slot, pl.ds(first, 8, stride=64), :] = pairs[rows]
+                    first = TILES * (4 * (8 * half + i) + (k >> 1))
+                    sent[place, first : first + MAIN, :] = pairs[YB * i : YB * (i + 1)]
         for v in range(2):
             for half in range(2):
                 tiles = []
@@ -345,11 +417,10 @@
                 for i, tile in enumerate(block_transpose(tiles)):
                     rest[v, 8 * (8 * half + i) : 8 * (8 * half + i) + 8] = tile
             for c in range(2):
-                rows = pl.ds((MAIN + v) * 64, 64)
+                rows = pl.ds(MAIN + v, 64, stride=TILES)
                 sent[c ^ core, rows, :] = rest[v, pl.ds(c, 64, stride=2), :]
-        for u in range(TILES):
-            mine[:, u * LANES : (u + 1) * LANES] = sent[0, u * 64 : (u + 1) * 64]
-            theirs[:, u * LANES : (u + 1) * LANES] = sent[1, u * 64 : (u + 1) * 64]
+        mine[...] = sent[0]
+        theirs[...] = sent[1]
 
 
 def sums_kernel(received, direction, residual, applied, out_sums):
@@ -358,7 +429,7 @@
     for u in range(TILES):
         sides = []
         for g in range(4):
-            upper, lower = (received[8 * m : 8 * m + 8, u * LANES : (u + 1) * LANES] for m in (g, g + 4))
+            upper, lower = (received[pl.ds(8 * m * TILES + u, 8, stride=TILES), :] for m in (g, g + 4))
             sides.append(upper + lower)
         if u < MAIN:
             maps = sides[0] + sides[1] + sides[2] + sides[3]
@@ -383,7 +454,16 @@
     out_sums[...] = jnp.broadcast_to(line, (LANES, LANES))
 
 
-def native_kernel(dense, maps, coils, stacked, turned):
+def native_kernel(
+    dense, dir_coils, res_coils, maps_out, fields, maps, stacked, turned, sems
+):
+    copies = [
+        pltpu.make_async_copy(source.at[p], fields.at[pl.ds(first + 8 * p, 8)], sems.at[2 * i + p])
+        for i, (source, first) in enumerate(((dir_coils, 16), (res_coils, 32)))
+        for p in range(2)
+    ]
+    for copy in copies:
+        copy.start()
     for g in range(4):
         for j in range(MAIN):
             turned[g, pl.ds(j, 8, stride=YB), :] = dense[g, j]
@@ -397,10 +477,21 @@
             if name < 3:
                 maps[name] = block
             else:
-                coils[(name - 3) // 8, (name - 3) % 8] = block
-
-
-def step_kernel(sums, app_maps, app_coils, dir_maps, dir_coils, res_maps, res_coils, *outs):
+                fields[name - 3] = block
+    copies.append(pltpu.make_async_copy(maps, maps_out, sems.at[4]))
+    copies[-1].start()
+    for copy in copies:
+        copy.wait()
+
+
+def step_kernel(sums, fields, app_maps, dir_maps, res_maps, *refs):
+    outs, (maps, sems) = refs[:4], refs[4:]
+    copies = [
+        pltpu.make_async_copy(source, maps.at[i], sems.at[i])
+        for i, source in enumerate((app_maps, dir_maps, res_maps))
+    ]
+    for copy in copies:
+        copy.start()
     line = jnp.sum(sums[...], axis=0, keepdims=True)
     lane = iota((1, LANES), 1)
     old, curve, cross, square = (
@@ -410,22 +501,23 @@
     new = old - 2.0 * size * cross + size * size * square
     ratio = (new / old).reshape(1, 1, 1)
     size = size.reshape(1, 1, 1)
+    for coil in range(16):
+        fresh = fields[32 + coil] - size * fields[coil]
+        outs[1][coil // 8, coil % 8] = fresh
+        outs[3][coil // 8, coil % 8] = fresh + ratio * fields[16 + coil]
+    for copy in copies:
+        copy.wait()
     for f in range(3):
-        fresh = res_maps[f] - size * app_maps[f]
+        fresh = maps[2, f] - size * maps[0, f]
         outs[0][f] = fresh
-        outs[2][f] = fresh + ratio * dir_maps[f]
-    for part in range(2):
-        for coil in range(8):
-            fresh = res_coils[part, coil] - size * app_coils[part, coil]
-            outs[1][part, coil] = fresh
-            outs[3][part, coil] = fresh + ratio * dir_coils[part, coil]
+        outs[2][f] = fresh + ratio * maps[1, f]
 
 
 def struct(*shape):
     return jax.ShapeDtypeStruct(shape, f32)
 
 
-ANY = pl.BlockSpec(memory_space=pl.ANY)
+HBM = pl.BlockSpec(memory_space=pltpu.HBM)
 VMEM = pl.BlockSpec(memory_space=pltpu.VMEM)
 SCRATCH_STACKED = pltpu.VMEM((4, 144, LANES), f32)
 SCRATCH_TURNED = pltpu.VMEM((4, LANES, LANES), f32)
@@ -447,13 +539,30 @@
     return pl.BlockSpec((1,) + shape, lambda s: (s,) + (0,) * len(shape))
 
 
+def in_hbm(*values):
+    return tuple(pltpu.with_memory_space_constraint(value, pltpu.HBM) for value in values)
+
+
+def in_vmem(*values):
+    return tuple(pltpu.with_memory_space_constraint(value, pltpu.VMEM) for value in values)
+
+
+def far(*shape):
+    return pltpu.HBM(shape, f32)
+
+
+def near(*shape):
+    return pltpu.VMEM(shape, f32)
+
+
 def core_swap(values):
     return lax.ppermute(values, "kz", [(i, i ^ 1) for i in range(8)])
 
 
 def by_parity(values):
     groups = [[i for i in range(128) if i & 1 == c] for c in range(2)]
-    return lax.all_to_all(values, AXES, 0, 0, axis_index_groups=groups, tiled=True)
+    messages = values.reshape(64, 1, values.shape[0] // 64 * LANES)
+    return lax.all_to_all(messages, AXES, 0, 0, axis_index_groups=groups).reshape(values.shape)
 
 
 def shards(
@@ -475,121 +584,148 @@
     send, dir_dense, mask_send = pl.pallas_call(
         pack_kernel,
         out_shape=(
-            struct(64, 2 * MSG),
-            struct(4, TILES, 8, LANES),
-            jax.ShapeDtypeStruct((8, NZ, NY), jnp.int32),
+            struct(64 * WHOLE, LANES),
+            near(4, TILES, 8, LANES),
+            pltpu.HBM((8, NZ, NY), jnp.int32),
         ),
-        in_specs=[ANY] * 6,
-        out_specs=(VMEM, VMEM, ANY),
+        in_specs=[HBM] * 6,
+        out_specs=(VMEM, VMEM, HBM),
         scratch_shapes=[
             pltpu.VMEM(dir_maps.shape, f32),
             pltpu.VMEM(dir_coils.shape, f32),
             pltpu.VMEM((ITEMS, 8, NY), f32),
             pltpu.VMEM((ITEMS, 4, 8, NY), f32),
             pltpu.SMEM((2,), f32),
+            pltpu.VMEM((NZ, NY), jnp.int32),
             SCRATCH_STACKED,
             SCRATCH_TURNED,
-            pltpu.SemaphoreType.DMA((29,)),
+            pltpu.SemaphoreType.DMA((37,)),
         ],
         compiler_params=params(),
         cost_estimate=cost(4),
         name="pack",
-    )(inversion_times, sampling_mask, dir_maps, dir_coils, pnt_maps, pnt_coils)
+    )(*in_hbm(inversion_times, sampling_mask, dir_maps, dir_coils, pnt_maps, pnt_coils))
 
     def densify(maps, coils):
         return pl.pallas_call(
             dense_kernel,
-            out_shape=struct(4, TILES, 8, LANES),
-            in_specs=[VMEM] * 2,
+            out_shape=near(4, TILES, 8, LANES),
+            in_specs=[HBM] * 2,
             out_specs=VMEM,
-            scratch_shapes=[SCRATCH_STACKED, SCRATCH_TURNED],
+            scratch_shapes=[
+                pltpu.VMEM(maps.shape, f32),
+                pltpu.VMEM(coils.shape, f32),
+                SCRATCH_STACKED,
+                SCRATCH_TURNED,
+                pltpu.SemaphoreType.DMA((2,)),
+            ],
             compiler_params=params(),
             cost_estimate=cost(3),
             name="dense",
-        )(maps, coils)
-
-    res_dense = densify(res_maps, res_coils)
+        )(*in_hbm(maps, coils))
+
     own = by_parity(send)
     other = core_swap(own)
-    mask_send, own = lax.optimization_barrier((mask_send, own))
     groups = [[8 * b + i for i in range(8)] for b in range(2)]
     masks = lax.all_to_all(mask_send, "ti", 0, 0, axis_index_groups=groups, tiled=True)
 
     spectrum, point, taus = pl.pallas_call(
         forward_kernel,
         grid=(8,),
-        out_shape=(struct(8, 2, 2, NZ, NY), struct(2, FEATURES * NZ, LANES), struct(8, 8, LANES)),
-        in_specs=[constant_block(a.shape) for a in (own, other, forward_y, forward_z)],
+        out_shape=(
+            far(8, 2, 2, NZ, NY),
+            near(2, FEATURES * NZ, LANES),
+            near(8, 8, LANES),
+        ),
+        in_specs=[constant_block(own.shape)] * 2 + [HBM] * 2,
         out_specs=(
-            stepping_block((2, 2, NZ, NY)),
+            HBM,
             constant_block((2, FEATURES * NZ, LANES)),
             stepping_block((8, LANES)),
         ),
         scratch_shapes=[
             pltpu.VMEM((2, FEATURES * NZ, LANES), f32),
-            pltpu.VMEM((MAIN * 64, LANES), f32),
             pltpu.VMEM((2, LANES, LANES), f32),
+            pltpu.VMEM(forward_y.shape, bf16),
+            pltpu.VMEM(forward_z.shape, bf16),
+            pltpu.VMEM((2, 2, 2, NZ, NY), f32),
+            pltpu.SemaphoreType.DMA((4,)),
         ],
         compiler_params=params(),
         cost_estimate=cost(12),
         name="forward",
-    )(own, other, forward_y, forward_z)
+    )(own, other, *in_hbm(forward_y, forward_z))
+
+    after = lax.optimization_barrier((res_maps, res_coils, taus))
+    res_dense = densify(*after[:2])
+    masks, res_dense = lax.optimization_barrier((masks, res_dense))
 
     mine, theirs = pl.pallas_call(
         backward_kernel,
         grid=(8,),
-        out_shape=(struct(64, MSG), struct(64, MSG)),
+        out_shape=(struct(64 * TILES, LANES), struct(64 * TILES, LANES)),
         in_specs=[
             stepping_block((NZ, NY)),
-            stepping_block((2, 2, NZ, NY)),
+            HBM,
             constant_block((2, FEATURES * NZ, LANES)),
             stepping_block((8, LANES)),
         ]
-        + [constant_block(a.shape) for a in (backward_y, backward_z, order)],
-        out_specs=(constant_block((64, MSG)),) * 2,
+        + [HBM] * 3,
+        out_specs=(constant_block((64 * TILES, LANES)),) * 2,
         scratch_shapes=[
             pltpu.VMEM((2, FEATURES * NZ, LANES), f32),
-            pltpu.VMEM((2, TILES * 64, LANES), f32),
+            pltpu.VMEM((2, 64 * TILES, LANES), f32),
             pltpu.VMEM((2, LANES, LANES), f32),
+            pltpu.VMEM(backward_y.shape, bf16),
+            pltpu.VMEM(backward_z.shape, bf16),
+            pltpu.VMEM(order.shape, bf16),
+            pltpu.VMEM((2, 2, 2, NZ, NY), f32),
+            pltpu.SemaphoreType.DMA((5,)),
         ],
         compiler_params=params(),
         cost_estimate=cost(12),
         name="backward",
-    )(masks, spectrum, point, taus, backward_y, backward_z, order)
+    )(*in_hbm(masks, spectrum), *in_vmem(point, taus), *in_hbm(backward_y, backward_z, order))
 
     received = by_parity(mine + core_swap(theirs))
     app_dense, sums = pl.pallas_call(
         sums_kernel,
-        out_shape=(struct(4, TILES, 8, LANES), struct(128, LANES)),
+        out_shape=(near(4, TILES, 8, LANES), near(128, LANES)),
         in_specs=[VMEM] * 3,
-        out_specs=(VMEM,) * 2,
+        out_specs=(VMEM, VMEM),
         compiler_params=params(),
         cost_estimate=cost(1),
         name="sums",
-    )(received, dir_dense, res_dense)
+    )(received, *in_vmem(dir_dense, res_dense))
     all_sums = lax.all_to_all(sums.reshape(128, 1, LANES), AXES, 0, 0).reshape(128, LANES)
 
     maps_shape, coils_shape = struct(*dir_maps.shape), struct(*dir_coils.shape)
-    app_maps, app_coils = pl.pallas_call(
+    app_maps, fields = pl.pallas_call(
         native_kernel,
-        out_shape=(maps_shape, coils_shape),
-        in_specs=[VMEM],
-        out_specs=(VMEM,) * 2,
-        scratch_shapes=[SCRATCH_STACKED, SCRATCH_TURNED],
+        out_shape=(far(*dir_maps.shape), near(48, XS, YB, ZB)),
+        in_specs=[VMEM] + [HBM] * 2,
+        out_specs=(HBM, VMEM),
+        scratch_shapes=[
+            pltpu.VMEM(dir_maps.shape, f32),
+            SCRATCH_STACKED,
+            SCRATCH_TURNED,
+            pltpu.SemaphoreType.DMA((5,)),
+        ],
         compiler_params=params(),
         cost_estimate=cost(3),
         name="native",
-    )(app_dense)
+    )(*in_vmem(app_dense), *in_hbm(dir_coils, res_coils))
 
     outs = pl.pallas_call(
         step_kernel,
         out_shape=(maps_shape, coils_shape, maps_shape, coils_shape),
-        in_specs=[VMEM] * 7,
+        in_specs=[VMEM] * 2 + [HBM] * 3,
         out_specs=(VMEM,) * 4,
+        scratch_shapes=[pltpu.VMEM((3,) + dir_maps.shape, f32), pltpu.SemaphoreType.DMA((3,))],
         compiler_params=params(),
         cost_estimate=cost(2),
         name="step",
-    )(all_sums, app_maps, app_coils, dir_maps, dir_coils, res_maps, res_coils)
+    )(all_sums, *in_vmem(fields), *in_hbm(app_maps, dir_maps, res_maps))
     return tuple(jnp.swapaxes(out, -2, -1) for out in outs)
 
 

time: 124 us -> 111 us (0.90)
  local copies, waits for them, and re-layouts: 23.8 us -> 1.07 us
  blocking collectives: 30.2 us -> 48.4 us
  waiting for transfers between devices: 23 us -> 14.6 us
  Pallas kernels: 27.5 us -> 32.7 us
  starting transfers between devices: 17.8 us -> 13 us
    unnamed x54 -> x4, local copies, waits for them, and re-layouts: 21.1 us -> 1.07 us
    all_to_all x1 -> x2, blocking collectives: 30.2 us -> 48.4 us  [by_parity(): lax.all_to_all(messages, AXES, 0, 0, axis_index_groups=groups)]
    all_to_all x1 -> x0, waiting for transfers between devices: 11.4 us -> none  [by_parity(): lax.all_to_all(values, AXES, 0, 0, axis_index_groups=groups, tiled=True)]
    all_to_all x1 -> x0, starting transfers between devices: 5.39 us -> none  [by_parity(): lax.all_to_all(values, AXES, 0, 0, axis_index_groups=groups, tiled=True)]
    pallas_call x6, Pallas kernels: 25.8 us -> 30.1 us  [the longest x1 11.7 us: shards(): pl.pallas_call(backward_kernel, grid=(8,), out_shape=(struct(64 * TILES,...]
    all_to_all x2 -> x0, local copies, waits for them, and re-layouts: 2.64 us -> none  [by_parity(): lax.all_to_all(values, AXES, 0, 0, axis_index_groups=groups, tiled=True)]
    all_to_all x1, waiting for transfers between devices: 3.34 us -> 5.09 us  [shards(): lax.all_to_all(mask_send, 'ti', 0, 0, axis_index_groups=groups, tiled=True)]
    all_to_all x1, waiting for transfers between devices: 6.58 us -> 7.89 us  [shards(): lax.all_to_all(sums.reshape(128, 1, LANES), AXES, 0, 0).reshape(128, LANES)]
  transfers between devices with their start and end apart: 5 -> 4, of which waited for: 4 -> 3; matrix products, arithmetic and copies ran while one was open for 0% -> 0% of each run, Pallas kernels for 10% -> 13%
where the time goes in v3:
time: 111 us
  blocking collectives  48.4 us (44%)
  Pallas kernels  32.7 us (29%)
  waiting for transfers between devices  14.6 us (13%)
  starting transfers between devices  13 us (12%)
    all_to_all x2, blocking collectives, by_parity(): lax.all_to_all(messages, AXES, 0, 0, axis_index_groups=groups)  48.4 us
    pallas_call x1, Pallas kernels, shards(): pl.pallas_call(backward_kernel, grid=(8,), out_shape=(struct(64 * TILES,...  11.7 us
    pallas_call x1, Pallas kernels, shards(): pl.pallas_call(forward_kernel, grid=(8,), out_shape=(far(8, 2, 2, NZ, NY)...  9.74 us
    all_to_all x1, waiting for transfers between devices, shards(): lax.all_to_all(sums.reshape(128, 1, LANES), AXES, 0, 0).reshape(128, LANES)  7.89 us
    all_to_all x1, starting transfers between devices, shards(): lax.all_to_all(sums.reshape(128, 1, LANES), AXES, 0, 0).reshape(128, LANES)  5.39 us
    all_to_all x1, waiting for transfers between devices, shards(): lax.all_to_all(mask_send, 'ti', 0, 0, axis_index_groups=groups, tiled=True)  5.09 us
    all_to_all x1, starting transfers between devices, shards(): lax.all_to_all(mask_send, 'ti', 0, 0, axis_index_groups=groups, tiled=True)  4.28 us
    ppermute x2, starting transfers between devices, core_swap(): return lax.ppermute(values, 'kz', [(i, i ^ 1) for i in range(8)])  3.33 us
  transfers between devices with their start and end apart: 4, of which 3 were waited for; matrix products, arithmetic and copies ran while one was open for 0% of the time, Pallas kernels for 13%

profile of v3, /device:TPU:1, one launch (start us, length us, event | category | flops | bytes accessed | tf_op | source)
XLA Modules:
  0.0 110.5 jit_solution(6618118979640247502)
XLA Ops:
  0.6 3.1 %pack.1 = (f32[2304,128]{1,0:T(8,128)S(1)}, f32[4,18,8,128]{3,2,1,0:T(8,128)S(1)}, s32[8,160,256]{2,1,0:T(8,128)}) custom-call(f32[2]{0:T(128)} %times.1, s32[2,160,256]{2,1,0:T(8,128)} %mask.1, f32[3,8,16,20]{3,2,1,0:T(8,128)} %bitcast.26, f32[2,8,8,16,20]{4,3,2,1,0:T(8,128)} %bitcast.31, f32[3,20,8,256]{3,2,1,0:T(8,128)} %bitcast.37, ...), custom_call_target="tpu_custom_call" | custom-call | flops 1600000000 | bytes 8000000 | tf_op jit(solution)/shard_map/pack/pallas_call | solution.py:584
  3.8 30.2 %all_to_all.20 = f32[64,1,4608]{2,1,0:T(1,128)S(1)} all-to-all(f32[64,1,4608]{2,1,0:T(1,128)S(1)} %bitcast.22), channel_id=1, replica_groups={{0,2,4,6,8,10,12,14,16,18,20,22,24,26,28,30,32,34,36,38,40,42,44,46,48,..., dimensions={0} | all-to-all | bytes 2359296 | tf_op jit(solution)/shard_map/all_to_all | solution.py:565
  34.0 2.6 %collective-permute-start = (f32[2304,128]{1,0:T(8,128)S(1)}, f32[2304,128]{1,0:T(8,128)S(1)}, u32[]{:S(2)}, u32[]{:S(2)}) collective-permute-start(f32[2304,128]{1,0:T(8,128)S(1)} %bitcast.20), channel_id=1, source_target_pairs={{0,1},{1,0},{2,3},{3,2},{4,5},{5,4},{6,7},{7,6},{8,9},{9,8},{10,11... | collective-permute-start | bytes 3538952 | tf_op jit(solution)/shard_map/ppermute | solution.py:559
  36.6 4.3 %all-to-all-start = ((s32[8,160,256]{2,1,0:T(8,128)}), s32[8,160,256]{2,1,0:T(8,128)}, u32[]{:S(2)}, u32[]{:S(2)}) async-start(s32[8,160,256]{2,1,0:T(8,128)} %get-tuple-element.24), calls=%async_computation | async-start | bytes 2621440 | tf_op jit(solution)/shard_map/all_to_all | solution.py:630
  40.9 0.0 collective-permute-done.other
  40.9 9.7 %forward.1 = (f32[8,2,2,160,256]{4,3,2,1,0:T(8,128)}, f32[2,1120,128]{2,1,0:T(8,128)S(1)}, f32[8,8,128]{2,1,0:T(8,128)S(1)}) custom-call(f32[2304,128]{1,0:T(8,128)S(1)} %bitcast.21, f32[2304,128]{1,0:T(8,128)S(1)} %collective-permute-done.other, bf16[2,768,256]{2,1,0:T(8,128)(2,1)} %constant.10.clone.table_y_in, bf16[2,160,512]{2,1,0:T(8,128)(2,1)} %constant.11.clone.table_z_in), custom_call_target="tpu_custom_call" | custom-call | flops 4800000000 | bytes 24000000 | tf_op jit(solution)/shard_map/forward/pallas_call | solution.py:632
  50.6 0.0 copy-start
  50.6 1.1 copy-done
  51.7 0.0 copy-start.1
  51.7 2.8 %dense.1.residual = f32[4,18,8,128]{3,2,1,0:T(8,128)S(1)} custom-call(f32[3,8,16,20]{3,2,1,0:T(8,128)} %bitcast.28, f32[2,8,8,16,20]{4,3,2,1,0:T(8,128)} %bitcast.33), custom_call_target="tpu_custom_call" | custom-call | flops 1200000000 | bytes 6000000 | tf_op jit(solution)/shard_map/dense/pallas_call | solution.py:610
  54.5 5.1 %all-to-all-done.mask = s32[8,160,256]{2,1,0:T(8,128)} async-done(((s32[8,160,256]{2,1,0:T(8,128)}), s32[8,160,256]{2,1,0:T(8,128)}, u32[]{:S(2)}, u32[]{:S(2)}) %all-to-all-start) | async-done | bytes 1310752 | tf_op jit(solution)/shard_map/all_to_all | solution.py:630
  59.6 0.0 copy-done.1
  59.6 11.7 %backward.1 = (f32[1152,128]{1,0:T(8,128)S(1)}, f32[1152,128]{1,0:T(8,128)S(1)}) custom-call(s32[8,160,256]{2,1,0:T(8,128)} %all-to-all-done.mask, f32[8,2,2,160,256]{4,3,2,1,0:T(8,128)} %get-tuple-element.30.spectrum, f32[2,1120,128]{2,1,0:T(8,128)S(1)} %copy-done.1, f32[8,8,128]{2,1,0:T(8,128)S(1)} %get-tuple-element.26.taus, ...), custom_call_target="tpu_custom_call" | custom-call | flops 4800000000 | bytes 24000000 | tf_op jit(solution)/shard_map/backward/pallas_call | solution.py:663
  71.3 0.8 collective-permute-start.1
  72.1 1.6 %collective-permute-done.1 = f32[1152,128]{1,0:T(8,128)S(1)} collective-permute-done((f32[1152,128]{1,0:T(8,128)S(1)}, f32[1152,128]{1,0:T(8,128)S(1)}, u32[]{:S(2)}, u32[]{:S(2)}) %collective-permute-start.1) | collective-permute-done | bytes 589856 | tf_op jit(solution)/shard_map/ppermute | solution.py:559
  73.7 0.1 add.3
  73.8 18.1 %all_to_all.21 = f32[64,1,2304]{2,1,0:T(1,128)S(1)} all-to-all(f32[64,1,2304]{2,1,0:T(1,128)S(1)} %bitcast.25), channel_id=1, replica_groups={{0,2,4,6,8,10,12,14,16,18,20,22,24,26,28,30,32,34,36,38,40,42,44,46,48,..., dimensions={0} | all-to-all | bytes 1179648 | tf_op jit(solution)/shard_map/all_to_all | solution.py:565
  91.9 0.9 sums.1
  92.9 5.4 %all-to-all-start.3 = ((f32[128,1,128]{2,1,0:T(1,128)}), f32[128,1,128]{2,1,0:T(1,128)S(1)}, u32[]{:S(2)}, u32[]{:S(2)}) async-start(f32[128,1,128]{2,1,0:T(1,128)} %bitcast.12), calls=%async_computation.3 | async-start | bytes 131072 | tf_op jit(solution)/shard_map/all_to_all | solution.py:700
  98.3 1.8 %native.1 = (f32[3,8,16,20]{3,2,1,0:T(8,128)}, f32[48,8,16,20]{3,2,1,0:T(8,128)S(1)}) custom-call(f32[4,18,8,128]{3,2,1,0:T(8,128)S(1)} %get-tuple-element.37.dense, f32[2,8,8,16,20]{4,3,2,1,0:T(8,128)} %bitcast.32, f32[2,8,8,16,20]{4,3,2,1,0:T(8,128)} %bitcast.34), custom_call_target="tpu_custom_call" | custom-call | flops 1200000000 | bytes 6000000 | tf_op jit(solution)/shard_map/native/pallas_call | solution.py:703
  100.1 7.9 %all-to-all-done.3 = f32[128,1,128]{2,1,0:T(1,128)S(1)} async-done(((f32[128,1,128]{2,1,0:T(1,128)}), f32[128,1,128]{2,1,0:T(1,128)S(1)}, u32[]{:S(2)}, u32[]{:S(2)}) %all-to-all-start.3) | async-done | bytes 65568 | tf_op jit(solution)/shard_map/all_to_all | solution.py:700
  107.9 2.6 %step.1 = (f32[3,8,16,20]{3,2,1,0:T(8,128)}, f32[2,8,8,16,20]{4,3,2,1,0:T(8,128)}, f32[3,8,16,20]{3,2,1,0:T(8,128)}, f32[2,8,8,16,20]{4,3,2,1,0:T(8,128)}) custom-call(f32[128,128]{1,0:T(8,128)S(1)} %bitcast.24, f32[48,8,16,20]{3,2,1,0:T(8,128)S(1)} %get-tuple-element.38.fields, f32[3,8,16,20]{3,2,1,0:T(8,128)} %get-tuple-element.39.app_maps, ...), custom_call_target="tpu_custom_call" | custom-call | flops 800000000 | bytes 4000000 | tf_op jit(solution)/shard_map/step/pallas_call | solution.py:719
Async XLA Ops:
  34.0 6.8 %collective-permute-start = (f32[2304,128]{1,0:T(8,128)S(1)}, f32[2304,128]{1,0:T(8,128)S(1)}, u32[]{:S(2)}, u32[]{:S(2)}) collective-permute-start(f32[2304,128]{1,0:T(8,128)S(1)} %bitcast.20), channel_id=1, source_target_pairs={{0,1},{1,0},{2,3},{3,2},{4,5},{5,4},{6,7},{7,6},{8,9},{9,8},{10,11... | collective-permute-start | bytes 3538952 | tf_op jit(solution)/shard_map/ppermute | solution.py:559
  36.6 23.1 %all-to-all-start = ((s32[8,160,256]{2,1,0:T(8,128)}), s32[8,160,256]{2,1,0:T(8,128)}, u32[]{:S(2)}, u32[]{:S(2)}) async-start(s32[8,160,256]{2,1,0:T(8,128)} %get-tuple-element.24), calls=%async_computation | async-start | bytes 2621440 | tf_op jit(solution)/shard_map/all_to_all | solution.py:630
  50.6 1.1 copy-start
  51.7 7.9 %copy-start.1 = (f32[2,1120,128]{2,1,0:T(8,128)S(1)}, f32[2,1120,128]{2,1,0:T(8,128)}, u32[]{:S(2)}) copy-start(f32[2,1120,128]{2,1,0:T(8,128)} %copy-done) | copy-start | bytes 3440644
  71.3 2.4 %collective-permute-start.1 = (f32[1152,128]{1,0:T(8,128)S(1)}, f32[1152,128]{1,0:T(8,128)S(1)}, u32[]{:S(2)}, u32[]{:S(2)}) collective-permute-start(f32[1152,128]{1,0:T(8,128)S(1)} %get-tuple-element.33), channel_id=1, source_target_pairs={{0,1},{1,0},{2,3},{3,2},{4,5},{5,4},{6,7},{7,6},{8,9},{9,8},{10,11... | collective-permute-start | bytes 1769480 | tf_op jit(solution)/shard_map/ppermute | solution.py:559
  92.9 15.1 %all-to-all-start.3 = ((f32[128,1,128]{2,1,0:T(1,128)}), f32[128,1,128]{2,1,0:T(1,128)S(1)}, u32[]{:S(2)}, u32[]{:S(2)}) async-start(f32[128,1,128]{2,1,0:T(1,128)} %bitcast.12), calls=%async_computation.3 | async-start | bytes 131072 | tf_op jit(solution)/shard_map/all_to_all | solution.py:700

commit v4 on v3

--- a/solution.py
+++ b/solution.py
@@ -19,6 +19,8 @@
 TILES = 18
 MSG = TILES * LANES
 ITEMS = 9
+BINS = 8
+FULL = 4
 WHOLE = 2 * TILES
 VMEM_LIMIT = 32 * 1024 * 1024
 f32 = jnp.float32
@@ -153,13 +155,11 @@
 
 
 def pack_kernel(
-    times, mask, maps_in, coils_in, point_maps, point_coils,
-    send, dense, mask_send,
-    maps, coils, of_maps, of_coils, stamp, own_mask, stacked, turned, sems,
+    times, maps_in, coils_in, point_maps, point_coils,
+    send, dense,
+    maps, coils, of_maps, of_coils, stamp, stacked, turned, sems,
 ):
-    t, core = lax.axis_index("ti"), lax.axis_index("kz") & 1
-    mask_copy = pltpu.make_async_copy(mask.at[core], own_mask, sems.at[0])
-    mask_copies = [pltpu.make_async_copy(own_mask, mask_send.at[s], sems.at[1 + s]) for s in range(8)]
+    t = lax.axis_index("ti")
     maps_copies = [
         pltpu.make_async_copy(maps_in, maps, sems.at[9]),
         pltpu.make_async_copy(times, stamp, sems.at[10]),
@@ -185,7 +185,7 @@
         point_copies.append(
             pltpu.make_async_copy(point_coils.at[q >> 1, :, q & 1, z], of_coils.at[i], sems.at[28 + i])
         )
-    for copy in point_copies + maps_copies + coils_copies + [mask_copy]:
+    for copy in point_copies + maps_copies + coils_copies:
         copy.start()
     for copy in point_copies:
         copy.wait()
@@ -209,16 +209,10 @@
             send[pl.ds(8 * m * WHOLE + u, 8, stride=WHOLE), :] = tile
 
     def arrive(g):
-        if g == 1:
-            mask_copy.wait()
-            for copy in mask_copies:
-                copy.start()
         for copy in coils_copies[2 * g : 2 * g + 2]:
             copy.wait()
 
     dense_tiles(maps, coils, stacked, turned, emit, arrive)
-    for copy in mask_copies:
-        copy.wait()
 
 
 def dense_kernel(maps_in, coils_in, dense, maps, coils, stacked, turned, sems):
@@ -237,61 +231,35 @@
     dense_tiles(maps, coils, stacked, turned, emit)
 
 
-def forward_kernel(
-    own, other, table_y_in, table_z_in,
-    spectrum, point, taus,
-    direction, rest, table_y, table_z, kept, sems,
-):
-    step = pl.program_id(0)
-    t, core = lax.axis_index("ti"), lax.axis_index("kz") & 1
-    slot = step & 1
-    tables = [
-        pltpu.make_async_copy(table_y_in, table_y, sems.at[2]),
-        pltpu.make_async_copy(table_z_in, table_z, sems.at[3]),
-    ]
-
-    def store(at, side):
-        return pltpu.make_async_copy(kept.at[side], spectrum.at[at], sems.at[side])
-
-    @pl.when(step == 0)
-    def _():
-        for copy in tables:
-            copy.start()
-        for part, c in ((own, core), (other, 1 - core)):
-            for y in range(4):
-                for half in range(2):
-                    firsts = [WHOLE * (4 * (8 * half + i) + y) for i in range(8)]
-                    rows = [part[first : first + MAIN, :] for first in firsts]
-                    pairs = jnp.swapaxes(jnp.concatenate(rows, axis=0), 0, 1)
-                    direction[half, pl.ds(2 * y + c, LANES, stride=8), :] = pairs
-            for v in range(2):
-                rest[v, pl.ds(c, 64, stride=2), :] = part[pl.ds(MAIN + v, 64, stride=WHOLE), :]
-            for i in range(ITEMS):
-                for half in range(2):
-                    for m in range(8):
-                        n = 18 * m + 2 * i
-                        if n < PAIRS:
-                            first = 8 * m * WHOLE + TILES + 2 * i + half
-                            point[half, pl.ds(8 * n + c, 8, stride=2), :] = part[pl.ds(first, 8, stride=WHOLE), :]
-        for v in range(2):
-            for half in range(2):
-                tiles = [rest[v, 8 * (8 * half + i) : 8 * (8 * half + i) + 8] for i in range(8)]
-                for member, tile in enumerate(block_transpose(tiles)):
-                    n = LANES + 8 * v + member
-                    if n < PAIRS:
-                        direction[half, 8 * n : 8 * n + 8] = tile
-        for copy in tables:
-            copy.wait()
-
-    @pl.when(step >= 2)
-    def _():
-        store(step - 2, slot).wait()
-
-    block = rest[1, pl.ds(pl.multiple_of(((t & 8) + step) * 8, 8), 8), :]
-    chosen = (iota((8, LANES), 0) == 0) & (iota((8, LANES), 1) == 64 + core)
-    tau = jnp.sum(jnp.where(chosen, block, 0.0), axis=(0, 1), keepdims=True)
-    taus[0] = jnp.broadcast_to(tau, (8, LANES))
-
+def unpack(part, c, point, direction, rest):
+    for y in range(4):
+        for half in range(2):
+            firsts = [WHOLE * (4 * (8 * half + i) + y) for i in range(8)]
+            rows = [part[first : first + MAIN, :] for first in firsts]
+            pairs = jnp.swapaxes(jnp.concatenate(rows, axis=0), 0, 1)
+            direction[half, pl.ds(2 * y + c, LANES, stride=8), :] = pairs
+    for v in range(2):
+        rest[v, pl.ds(c, 64, stride=2), :] = part[pl.ds(MAIN + v, 64, stride=WHOLE), :]
+    for i in range(ITEMS):
+        for half in range(2):
+            for m in range(8):
+                n = 18 * m + 2 * i
+                if n < PAIRS:
+                    first = 8 * m * WHOLE + TILES + 2 * i + half
+                    point[half, pl.ds(8 * n + c, 8, stride=2), :] = part[pl.ds(first, 8, stride=WHOLE), :]
+
+
+def unpack_rest(direction, rest):
+    for v in range(2):
+        for half in range(2):
+            tiles = [rest[v, 8 * (8 * half + i) : 8 * (8 * half + i) + 8] for i in range(8)]
+            for member, tile in enumerate(block_transpose(tiles)):
+                n = LANES + 8 * v + member
+                if n < PAIRS:
+                    direction[half, 8 * n : 8 * n + 8] = tile
+
+
+def forward_bin(tau, point, direction, table_y, table_z, spectrum):
     amplitude = plane(point, 1)
     decays = jnp.exp(-tau * plane(point, 2))
     signal = plane(point, 0) - amplitude * decays
@@ -315,55 +283,17 @@
         ]
         for part in range(2):
             a, b = (side[part * HALF_Z : (part + 1) * HALF_Z] for side in parts)
-            kept[slot, c, part, :HALF_Z] = a + b
-            kept[slot, c, part, HALF_Z:] = a - b
-    store(step, slot).start()
-
-    @pl.when(step == 7)
-    def _():
-        store(6, 0).wait()
-        store(7, 1).wait()
-
-
-def backward_kernel(
-    mask, spectrum, point, taus, table_y_in, table_z_in, order_in,
-    mine, theirs,
-    total, sent, rest, table_y, table_z, order, kept, sems,
-):
-    step = pl.program_id(0)
-    core = lax.axis_index("kz") & 1
-    slot = step & 1
-    tables = [
-        pltpu.make_async_copy(order_in, order, sems.at[4]),
-        pltpu.make_async_copy(table_z_in, table_z, sems.at[3]),
-        pltpu.make_async_copy(table_y_in, table_y, sems.at[2]),
-    ]
-
-    def load(at, side):
-        return pltpu.make_async_copy(spectrum.at[at], kept.at[side], sems.at[side])
-
-    @pl.when(step == 0)
-    def _():
-        load(0, 0).start()
-        for copy in tables:
-            copy.start()
-        total[...] = jnp.zeros_like(total)
-        for copy in tables:
-            copy.wait()
-
-    @pl.when(step < 7)
-    def _():
-        load(step + 1, 1 - slot).start()
-
-    load(step, slot).wait()
-
-    tau = taus[0, 0:1, 0:1]
-    weights = jnp.dot(mask[0].astype(f32).astype(bf16), order[...], preferred_element_type=f32)
+            spectrum[c, part, :HALF_Z] = a + b
+            spectrum[c, part, HALF_Z:] = a - b
+
+
+def backward_bin(tau, mask, spectrum, point, table_y, table_z, order, total):
+    weights = jnp.dot(mask.astype(f32).astype(bf16), order[...], preferred_element_type=f32)
     evens, odds = [], []
     for c in range(2):
         plus, minus = [], []
         for part in range(2):
-            values = kept[slot, c, part] * weights
+            values = spectrum[c, part] * weights
             plus.append(values[:HALF_Z] + values[HALF_Z:])
             minus.append(values[:HALF_Z] - values[HALF_Z:])
         for parity, side in enumerate((plus, minus)):
@@ -399,33 +329,121 @@
     add(1, -faded)
     add(2, amplitude * (tau * faded))
 
-    @pl.when(step == 7)
-    def _():
-        for k in range(8):
-            place = (k & 1) ^ core
-            for half in range(2):
-                pairs = jnp.swapaxes(total[half, pl.ds(k, LANES, stride=8), :], 0, 1)
-                for i in range(8):
-                    first = TILES * (4 * (8 * half + i) + (k >> 1))
-                    sent[place, first : first + MAIN, :] = pairs[YB * i : YB * (i + 1)]
-        for v in range(2):
-            for half in range(2):
-                tiles = []
-                for member in range(8):
-                    n = min(LANES + 8 * v + member, PAIRS - 1)
-                    tiles.append(total[half, 8 * n : 8 * n + 8])
-                for i, tile in enumerate(block_transpose(tiles)):
-                    rest[v, 8 * (8 * half + i) : 8 * (8 * half + i) + 8] = tile
-            for c in range(2):
-                rows = pl.ds(MAIN + v, 64, stride=TILES)
-                sent[c ^ core, rows, :] = rest[v, pl.ds(c, 64, stride=2), :]
-        mine[...] = sent[0]
-        theirs[...] = sent[1]
-
-
-def sums_kernel(received, direction, residual, applied, out_sums):
+
+def pack_sums(core, total, sent, rest, mine, theirs):
+    for k in range(8):
+        place = (k & 1) ^ core
+        for half in range(2):
+            pairs = jnp.swapaxes(total[half, pl.ds(k, LANES, stride=8), :], 0, 1)
+            for i in range(8):
+                first = TILES * (4 * (8 * half + i) + (k >> 1))
+                sent[place, first : first + MAIN, :] = pairs[YB * i : YB * (i + 1)]
+    for v in range(2):
+        for half in range(2):
+            tiles = []
+            for member in range(8):
+                n = min(LANES + 8 * v + member, PAIRS - 1)
+                tiles.append(total[half, 8 * n : 8 * n + 8])
+            for i, tile in enumerate(block_transpose(tiles)):
+                rest[v, 8 * (8 * half + i) : 8 * (8 * half + i) + 8] = tile
+        for c in range(2):
+            rows = pl.ds(MAIN + v, 64, stride=TILES)
+            sent[c ^ core, rows, :] = rest[v, pl.ds(c, 64, stride=2), :]
+    mine[...] = sent[0]
+    theirs[...] = sent[1]
+
+
+def first_kernel(*refs):
+    own, other, mask, *tables_in = refs[:8]
+    spectrum, last, point, taus, total, backward_y, backward_z, order = refs[8:16]
+    direction, rest, forward_y, forward_z, kept, sems = refs[16:]
+    step = pl.program_id(0)
+    t, core = lax.axis_index("ti"), lax.axis_index("kz") & 1
+    slot = step & 1
+    tables = (forward_y, forward_z, backward_y, backward_z, order)
+    copies = [pltpu.make_async_copy(a, b, sems.at[2 + i]) for i, (a, b) in enumerate(zip(tables_in, tables))]
+
+    def store(at, side):
+        return pltpu.make_async_copy(kept.at[side], spectrum.at[at - FULL], sems.at[side])
+
+    @pl.when(step == 0)
+    def _():
+        for copy in copies:
+            copy.start()
+        total[...] = jnp.zeros_like(total)
+        unpack(own, core, point, direction, rest)
+        unpack(other, 1 - core, point, direction, rest)
+        unpack_rest(direction, rest)
+        for copy in copies:
+            copy.wait()
+
+    @pl.when(step >= FULL + 2)
+    def _():
+        store(step - 2, slot).wait()
+
+    spread = (step & 3) ^ ((step & 2) >> 1)
+    bin_of = ((t & 12) | ((t + spread) & 3)) ^ (step & 4)
+    block = rest[1, pl.ds(pl.multiple_of(bin_of * 8, 8), 8), :]
+    chosen = (iota((8, LANES), 0) == 0) & (iota((8, LANES), 1) == 64 + core)
+    tau = jnp.sum(jnp.where(chosen, block, 0.0), axis=(0, 1), keepdims=True)
+
+    taus[0] = jnp.broadcast_to(tau, (8, LANES))
+
+    @pl.when(step < BINS - 1)
+    def _():
+        forward_bin(tau, point, direction, forward_y, forward_z, kept.at[slot])
+
+    @pl.when(step < FULL)
+    def _():
+        backward_bin(tau, mask[0], kept.at[slot], point, backward_y, backward_z, order, total)
+
+    @pl.when((step >= FULL) & (step < BINS - 1))
+    def _():
+        store(step, slot).start()
+
+    @pl.when(step == BINS - 1)
+    def _():
+        forward_bin(tau, point, direction, forward_y, forward_z, last)
+        store(BINS - 2, BINS & 1).wait()
+
+
+def second_kernel(
+    mask, spectrum, last, point, taus, total_in, table_y, table_z, order,
+    mine, theirs,
+    total, sent, rest, kept, sems,
+):
+    step = pl.program_id(0)
+    core = lax.axis_index("kz") & 1
+    slot = step & 1
+
+    def load(at):
+        return pltpu.make_async_copy(spectrum.at[at - 1], kept.at[at & 1], sems.at[at & 1])
+
+    @pl.when(step == 0)
+    def _():
+        total[...] = total_in[...]
+        kept[0] = last[...]
+
+    @pl.when(step < BINS - FULL - 1)
+    def _():
+        load(step + 1).start()
+
+    @pl.when(step > 0)
+    def _():
+        load(step).wait()
+
+    tau = taus[0, 0:1, 0:1]
+    backward_bin(tau, mask[0], kept.at[slot], point, table_y, table_z, order, total)
+
+    @pl.when(step == BINS - FULL - 1)
+    def _():
+        pack_sums(core, total, sent, rest, mine, theirs)
+
+
+def sums_kernel(received, direction, residual, applied_out, out_sums, applied, sems):
     lane = iota((8, LANES), 1)
     sums = [jnp.zeros((8, LANES), f32) for _ in range(4)]
+    copies = []
     for u in range(TILES):
         sides = []
         for g in range(4):
@@ -444,32 +462,41 @@
             elif u == TILES - 1:
                 d, r, value = (jnp.where(lane < 64, a, 0.0) for a in (d, r, value))
             q = value + regular_weight * d
-            applied[g, u] = q
+            applied[u, g] = q
             for i, (a, b) in enumerate(((r, r), (d, q), (r, q), (q, q))):
                 sums[i] = sums[i] + a * b
+        if u % 6 == 5:
+            part = pl.ds(u - 5, 6)
+            copies.append(pltpu.make_async_copy(applied.at[part], applied_out.at[part], sems.at[u // 6]))
+            copies[-1].start()
     line = jnp.zeros((1, LANES), f32)
     for i in range(4):
         value = jnp.sum(sums[i], axis=(0, 1), keepdims=True)
         line = jnp.where(iota((1, LANES), 1) == i, value, line)
     out_sums[...] = jnp.broadcast_to(line, (LANES, LANES))
+    for copy in copies:
+        copy.wait()
 
 
 def native_kernel(
-    dense, dir_coils, res_coils, maps_out, fields, maps, stacked, turned, sems
+    dense_in, dir_coils, res_coils, maps_out, fields, dense, maps, stacked, turned, sems
 ):
     copies = [
         pltpu.make_async_copy(source.at[p], fields.at[pl.ds(first + 8 * p, 8)], sems.at[2 * i + p])
         for i, (source, first) in enumerate(((dir_coils, 16), (res_coils, 32)))
         for p in range(2)
     ]
-    for copy in copies:
+    copies.append(pltpu.make_async_copy(dense_in, dense, sems.at[5]))
+    copies[-1].start()
+    for copy in copies[:-1]:
         copy.start()
+    copies.pop().wait()
     for g in range(4):
         for j in range(MAIN):
-            turned[g, pl.ds(j, 8, stride=YB), :] = dense[g, j]
+            turned[g, pl.ds(j, 8, stride=YB), :] = dense[j, g]
         stacked[g, :LANES] = jnp.swapaxes(turned[g], 0, 1)
         for v in range(2):
-            stacked[g, LANES + 8 * v : LANES + 8 * v + 8] = inner_transpose(dense[g, MAIN + v])
+            stacked[g, LANES + 8 * v : LANES + 8 * v + 8] = inner_transpose(dense[MAIN + v, g])
         for i, name in enumerate(names_of(g)):
             if name < 3 and g:
                 continue
@@ -485,7 +512,7 @@
 
 
 def step_kernel(sums, fields, app_maps, dir_maps, res_maps, *refs):
-    outs, (maps, sems) = refs[:4], refs[4:]
+    outs, (maps, made_maps, made_coils, sems) = refs[:4], refs[4:]
     copies = [
         pltpu.make_async_copy(source, maps.at[i], sems.at[i])
         for i, source in enumerate((app_maps, dir_maps, res_maps))
@@ -501,16 +528,31 @@
     new = old - 2.0 * size * cross + size * size * square
     ratio = (new / old).reshape(1, 1, 1)
     size = size.reshape(1, 1, 1)
-    for coil in range(16):
-        fresh = fields[32 + coil] - size * fields[coil]
-        outs[1][coil // 8, coil % 8] = fresh
-        outs[3][coil // 8, coil % 8] = fresh + ratio * fields[16 + coil]
+    stores = []
+    for first in range(0, 16, 4):
+        for coil in range(first, first + 4):
+            fresh = fields[32 + coil] - size * fields[coil]
+            made_coils[0, coil] = fresh
+            made_coils[1, coil] = fresh + ratio * fields[16 + coil]
+        part, rows = first // 8, pl.ds(first % 8, 4)
+        for i in range(2):
+            stores.append(
+                pltpu.make_async_copy(
+                    made_coils.at[i, pl.ds(first, 4)], outs[1 + 2 * i].at[part, rows], sems.at[3 + len(stores)]
+                )
+            )
+            stores[-1].start()
     for copy in copies:
         copy.wait()
     for f in range(3):
         fresh = maps[2, f] - size * maps[0, f]
-        outs[0][f] = fresh
-        outs[2][f] = fresh + ratio * maps[1, f]
+        made_maps[0, f] = fresh
+        made_maps[1, f] = fresh + ratio * maps[1, f]
+    for i in range(2):
+        stores.append(pltpu.make_async_copy(made_maps.at[i], outs[2 * i], sems.at[3 + len(stores)]))
+        stores[-1].start()
+    for copy in stores:
+        copy.wait()
 
 
 def struct(*shape):
@@ -581,22 +623,20 @@
     pnt_maps = jnp.swapaxes(point_maps, 1, 2)
     pnt_coils = jnp.swapaxes(point_coils, 2, 3).reshape(2, 4, 2, ZB, XS, NY)
 
-    send, dir_dense, mask_send = pl.pallas_call(
+    send, dir_dense = pl.pallas_call(
         pack_kernel,
         out_shape=(
             struct(64 * WHOLE, LANES),
             near(4, TILES, 8, LANES),
-            pltpu.HBM((8, NZ, NY), jnp.int32),
         ),
-        in_specs=[HBM] * 6,
-        out_specs=(VMEM, VMEM, HBM),
+        in_specs=[HBM] * 5,
+        out_specs=(VMEM, VMEM),
         scratch_shapes=[
             pltpu.VMEM(dir_maps.shape, f32),
             pltpu.VMEM(dir_coils.shape, f32),
             pltpu.VMEM((ITEMS, 8, NY), f32),
             pltpu.VMEM((ITEMS, 4, 8, NY), f32),
             pltpu.SMEM((2,), f32),
-            pltpu.VMEM((NZ, NY), jnp.int32),
             SCRATCH_STACKED,
             SCRATCH_TURNED,
             pltpu.SemaphoreType.DMA((37,)),
@@ -604,7 +644,7 @@
         compiler_params=params(),
         cost_estimate=cost(4),
         name="pack",
-    )(*in_hbm(inversion_times, sampling_mask, dir_maps, dir_coils, pnt_maps, pnt_coils))
+    )(*in_hbm(inversion_times, dir_maps, dir_coils, pnt_maps, pnt_coils))
 
     def densify(maps, coils):
         return pl.pallas_call(
@@ -625,103 +665,127 @@
         )(*in_hbm(maps, coils))
 
     own = by_parity(send)
+    res_dense = densify(res_maps, res_coils)
+    own_mask = lax.dynamic_index_in_dim(sampling_mask, lax.axis_index("kz") & 1, 0, keepdims=False)
+    own_mask, res_dense = lax.optimization_barrier((own_mask, res_dense))
+
+    def from_ti(values, shift, flip):
+        return lax.ppermute(values, "ti", [(((i & 12) | ((i + shift) & 3)) ^ flip, i) for i in range(16)])
+
+    near_masks = jnp.stack([own_mask] + [from_ti(own_mask, shift, 0) for shift in (1, 3, 2)])
+    own, near_masks = lax.optimization_barrier((own, near_masks))
     other = core_swap(own)
-    groups = [[8 * b + i for i in range(8)] for b in range(2)]
-    masks = lax.all_to_all(mask_send, "ti", 0, 0, axis_index_groups=groups, tiled=True)
-
-    spectrum, point, taus = pl.pallas_call(
-        forward_kernel,
-        grid=(8,),
+    far_masks = from_ti(near_masks, 0, 4)
+    planes = (2, FEATURES * NZ, LANES)
+    tables = (forward_y, forward_z, backward_y, backward_z, order)
+    sums_shape = struct(64 * TILES, LANES)
+    sent_scratch = pltpu.VMEM((2, 64 * TILES, LANES), f32)
+    spectrum, last, point, taus, total, *near_tables = pl.pallas_call(
+        first_kernel,
+        grid=(BINS,),
         out_shape=(
-            far(8, 2, 2, NZ, NY),
-            near(2, FEATURES * NZ, LANES),
-            near(8, 8, LANES),
+            far(BINS - FULL - 1, 2, 2, NZ, NY),
+            near(2, 2, NZ, NY),
+            near(*planes),
+            near(BINS, 8, LANES),
+            near(*planes),
+            *[pltpu.VMEM(table.shape, bf16) for table in tables[2:]],
         ),
-        in_specs=[constant_block(own.shape)] * 2 + [HBM] * 2,
+        in_specs=[constant_block(own.shape)] * 2
+        + [pl.BlockSpec((1, NZ, NY), lambda s: (jnp.minimum(s, FULL - 1), 0, 0))]
+        + [HBM] * 5,
         out_specs=(
             HBM,
-            constant_block((2, FEATURES * NZ, LANES)),
+            constant_block((2, 2, NZ, NY)),
+            constant_block(planes),
             stepping_block((8, LANES)),
+            constant_block(planes),
+            *[constant_block(table.shape) for table in tables[2:]],
         ),
         scratch_shapes=[
-            pltpu.VMEM((2, FEATURES * NZ, LANES), f32),
+            pltpu.VMEM(planes, f32),
             pltpu.VMEM((2, LANES, LANES), f32),
             pltpu.VMEM(forward_y.shape, bf16),
             pltpu.VMEM(forward_z.shape, bf16),
             pltpu.VMEM((2, 2, 2, NZ, NY), f32),
-            pltpu.SemaphoreType.DMA((4,)),
+            pltpu.SemaphoreType.DMA((7,)),
         ],
         compiler_params=params(),
-        cost_estimate=cost(12),
-        name="forward",
-    )(own, other, *in_hbm(forward_y, forward_z))
-
-    after = lax.optimization_barrier((res_maps, res_coils, taus))
-    res_dense = densify(*after[:2])
-    masks, res_dense = lax.optimization_barrier((masks, res_dense))
+        cost_estimate=cost(15),
+        name="first",
+    )(own, other, near_masks, *in_hbm(*tables))
+
+    def bin_block(shape, first):
+        return pl.BlockSpec((1,) + shape, lambda s: (jnp.where(s == 0, BINS - 1, s + FULL - 1) - first, 0, 0))
 
     mine, theirs = pl.pallas_call(
-        backward_kernel,
-        grid=(8,),
-        out_shape=(struct(64 * TILES, LANES), struct(64 * TILES, LANES)),
+        second_kernel,
+        grid=(BINS - FULL,),
+        out_shape=(sums_shape, sums_shape),
         in_specs=[
-            stepping_block((NZ, NY)),
+            bin_block((NZ, NY), FULL),
             HBM,
-            constant_block((2, FEATURES * NZ, LANES)),
-            stepping_block((8, LANES)),
+            constant_block((2, 2, NZ, NY)),
+            constant_block(planes),
+            bin_block((8, LANES), 0),
+            constant_block(planes),
         ]
-        + [HBM] * 3,
+        + [constant_block(table.shape) for table in tables[2:]],
         out_specs=(constant_block((64 * TILES, LANES)),) * 2,
         scratch_shapes=[
-            pltpu.VMEM((2, FEATURES * NZ, LANES), f32),
-            pltpu.VMEM((2, 64 * TILES, LANES), f32),
+            pltpu.VMEM(planes, f32),
+            sent_scratch,
             pltpu.VMEM((2, LANES, LANES), f32),
-            pltpu.VMEM(backward_y.shape, bf16),
-            pltpu.VMEM(backward_z.shape, bf16),
-            pltpu.VMEM(order.shape, bf16),
             pltpu.VMEM((2, 2, 2, NZ, NY), f32),
-            pltpu.SemaphoreType.DMA((5,)),
+            pltpu.SemaphoreType.DMA((2,)),
         ],
         compiler_params=params(),
-        cost_estimate=cost(12),
-        name="backward",
-    )(*in_hbm(masks, spectrum), *in_vmem(point, taus), *in_hbm(backward_y, backward_z, order))
+        cost_estimate=cost(8),
+        name="second",
+    )(far_masks, *in_hbm(spectrum), *in_vmem(last, point, taus, total, *near_tables))
 
     received = by_parity(mine + core_swap(theirs))
     app_dense, sums = pl.pallas_call(
         sums_kernel,
-        out_shape=(near(4, TILES, 8, LANES), near(128, LANES)),
+        out_shape=(far(TILES, 4, 8, LANES), near(128, LANES)),
         in_specs=[VMEM] * 3,
-        out_specs=(VMEM, VMEM),
+        out_specs=(HBM, VMEM),
+        scratch_shapes=[pltpu.VMEM((TILES, 4, 8, LANES), f32), pltpu.SemaphoreType.DMA((3,))],
         compiler_params=params(),
         cost_estimate=cost(1),
         name="sums",
     )(received, *in_vmem(dir_dense, res_dense))
     all_sums = lax.all_to_all(sums.reshape(128, 1, LANES), AXES, 0, 0).reshape(128, LANES)
 
-    maps_shape, coils_shape = struct(*dir_maps.shape), struct(*dir_coils.shape)
+    maps_shape, coils_shape = far(*dir_maps.shape), far(*dir_coils.shape)
     app_maps, fields = pl.pallas_call(
         native_kernel,
         out_shape=(far(*dir_maps.shape), near(48, XS, YB, ZB)),
-        in_specs=[VMEM] + [HBM] * 2,
+        in_specs=[HBM] * 3,
         out_specs=(HBM, VMEM),
         scratch_shapes=[
+            pltpu.VMEM((TILES, 4, 8, LANES), f32),
             pltpu.VMEM(dir_maps.shape, f32),
             SCRATCH_STACKED,
             SCRATCH_TURNED,
-            pltpu.SemaphoreType.DMA((5,)),
+            pltpu.SemaphoreType.DMA((6,)),
         ],
         compiler_params=params(),
         cost_estimate=cost(3),
         name="native",
-    )(*in_vmem(app_dense), *in_hbm(dir_coils, res_coils))
+    )(*in_hbm(app_dense, dir_coils, res_coils))
 
     outs = pl.pallas_call(
         step_kernel,
         out_shape=(maps_shape, coils_shape, maps_shape, coils_shape),
         in_specs=[VMEM] * 2 + [HBM] * 3,
-        out_specs=(VMEM,) * 4,
-        scratch_shapes=[pltpu.VMEM((3,) + dir_maps.shape, f32), pltpu.SemaphoreType.DMA((3,))],
+        out_specs=(HBM,) * 4,
+        scratch_shapes=[
+            pltpu.VMEM((3,) + dir_maps.shape, f32),
+            pltpu.VMEM((2,) + dir_maps.shape, f32),
+            pltpu.VMEM((2, 16, XS, YB, ZB), f32),
+            pltpu.SemaphoreType.DMA((13,)),
+        ],
         compiler_params=params(),
         cost_estimate=cost(2),
         name="step",

time: 111 us -> 105 us (0.946)
  blocking collectives: 48.4 us -> 20.8 us
  starting transfers between devices: 13 us -> 25.6 us
  waiting for transfers between devices: 14.6 us -> 25 us
    all_to_all x2 -> x1, blocking collectives: 48.4 us -> 20.8 us  [by_parity(): lax.all_to_all(messages, AXES, 0, 0, axis_index_groups=groups)]
    ppermute x0 -> x4, waiting for transfers between devices: none -> 15 us  [from_ti(): lax.ppermute(values, 'ti', [((i & 12 | i + shift & 3) ^ flip, i) for i in...]
    all_to_all x1, starting transfers between devices: 4.28 us -> 12 us  [by_parity(): lax.all_to_all(messages, AXES, 0, 0, axis_index_groups=groups)]
    ppermute x0 -> x4, starting transfers between devices: none -> 5.29 us  [from_ti(): lax.ppermute(values, 'ti', [((i & 12 | i + shift & 3) ^ flip, i) for i in...]
    all_to_all x1, waiting for transfers between devices: 5.09 us -> 0.01 us  [by_parity(): lax.all_to_all(messages, AXES, 0, 0, axis_index_groups=groups)]
    pallas_call x3, Pallas kernels: 22.4 us -> 20.2 us  [the longest x1 13.7 us: shards(): pl.pallas_call(first_kernel, grid=(BINS,), out_shape=(far(BINS - FULL - 1...]
    ppermute x2, waiting for transfers between devices: 1.63 us -> 2.87 us  [core_swap(): return lax.ppermute(values, 'kz', [(i, i ^ 1) for i in range(8)])]
  transfers between devices with their start and end apart: 4 -> 8, of which waited for: 3 -> 7; matrix products, arithmetic and copies ran while one was open for 0% -> 0% of each run, Pallas kernels for 13% -> 18%
where the time goes in v4:
time: 105 us; the launch traced here: 104 us
  Pallas kernels  31.9 us (30%)
  starting transfers between devices  25.6 us (24%)
  waiting for transfers between devices  25 us (24%)
  blocking collectives  20.8 us (20%)
    all_to_all x1, blocking collectives, by_parity(): lax.all_to_all(messages, AXES, 0, 0, axis_index_groups=groups)  20.8 us
    ppermute x4, waiting for transfers between devices, from_ti(): lax.ppermute(values, 'ti', [((i & 12 | i + shift & 3) ^ flip, i) for i in...  15 us
    pallas_call x1, Pallas kernels, shards(): pl.pallas_call(first_kernel, grid=(BINS,), out_shape=(far(BINS - FULL - 1...  13.7 us
    all_to_all x1, starting transfers between devices, by_parity(): lax.all_to_all(messages, AXES, 0, 0, axis_index_groups=groups)  12 us
    all_to_all x1, waiting for transfers between devices, shards(): lax.all_to_all(sums.reshape(128, 1, LANES), AXES, 0, 0).reshape(128, LANES)  7.19 us
    all_to_all x1, starting transfers between devices, shards(): lax.all_to_all(sums.reshape(128, 1, LANES), AXES, 0, 0).reshape(128, LANES)  5.41 us
    ppermute x4, starting transfers between devices, from_ti(): lax.ppermute(values, 'ti', [((i & 12 | i + shift & 3) ^ flip, i) for i in...  5.29 us
    pallas_call x1, Pallas kernels, shards(): pl.pallas_call(second_kernel, grid=(BINS - FULL,), out_shape=(sums_shape,...  4.98 us
  transfers between devices with their start and end apart: 8, of which 7 were waited for; matrix products, arithmetic and copies ran while one was open for 0% of the time, Pallas kernels for 18%

profile of v4, /device:TPU:1, one launch (start us, length us, event | category | flops | bytes accessed | tf_op | source)
XLA Modules:
  0.0 104.2 jit_solution(8223589817738959712)
XLA Ops:
  0.6 0.0 copy-start
  0.6 4.1 %pack.1 = (f32[2304,128]{1,0:T(8,128)}, f32[4,18,8,128]{3,2,1,0:T(8,128)S(1)}) custom-call(f32[2]{0:T(128)} %times.1, f32[3,8,16,20]{3,2,1,0:T(8,128)} %bitcast.32, f32[2,8,8,16,20]{4,3,2,1,0:T(8,128)} %bitcast.40, f32[3,20,8,256]{3,2,1,0:T(8,128)} %bitcast.46, f32[2,4,2,20,8,256]{5,4,3,2,1,0:T(8,128)} %bitcast.39), custom_call_target="tpu_custom_call" | custom-call | flops 1600000000 | bytes 8000000 | tf_op jit(solution)/shard_map/pack/pallas_call | solution.py:626
  4.8 12.0 %all-to-all-start = ((f32[64,1,4608]{2,1,0:T(1,128)}), f32[64,1,4608]{2,1,0:T(1,128)S(1)}, u32[]{:S(2)}, u32[]{:S(2)}) async-start(f32[64,1,4608]{2,1,0:T(1,128)} %bitcast.5), calls=%async_computation | async-start | bytes 2359296 | tf_op jit(solution)/shard_map/all_to_all | solution.py:607
  16.8 2.8 %dense.1.residual = f32[4,18,8,128]{3,2,1,0:T(8,128)S(1)} custom-call(f32[3,8,16,20]{3,2,1,0:T(8,128)} %bitcast.34, f32[2,8,8,16,20]{4,3,2,1,0:T(8,128)} %bitcast.42), custom_call_target="tpu_custom_call" | custom-call | flops 1200000000 | bytes 6000000 | tf_op jit(solution)/shard_map/dense/pallas_call | solution.py:650
  19.6 2.3 %collective-permute-start = (s32[160,256]{1,0:T(8,128)S(1)}, s32[160,256]{1,0:T(8,128)S(1)}, u32[]{:S(2)}, u32[]{:S(2)}) collective-permute-start(s32[160,256]{1,0:T(8,128)S(1)} %dynamic-slice_bitcast_fusion), channel_id=1, source_target_pairs={{8,0},{16,8},{24,16},{0,24},{40,32},{48,40},{56,48},{32,56},{72,64... | collective-permute-start | bytes 491528 | tf_op jit(solution)/shard_map/ppermute | solution.py:673
  21.9 1.8 %collective-permute-start.2 = (s32[160,256]{1,0:T(8,128)S(1)}, s32[160,256]{1,0:T(8,128)S(1)}, u32[]{:S(2)}, u32[]{:S(2)}) collective-permute-start(s32[160,256]{1,0:T(8,128)S(1)} %dynamic-slice_bitcast_fusion), channel_id=1, source_target_pairs={{16,0},{24,8},{0,16},{8,24},{48,32},{56,40},{32,48},{40,56},{80,64... | collective-permute-start | bytes 491528 | tf_op jit(solution)/shard_map/ppermute | solution.py:673
  23.7 9.9 %collective-permute-done = s32[160,256]{1,0:T(8,128)S(1)} collective-permute-done((s32[160,256]{1,0:T(8,128)S(1)}, s32[160,256]{1,0:T(8,128)S(1)}, u32[]{:S(2)}, u32[]{:S(2)}) %collective-permute-start) | collective-permute-done | bytes 163872 | tf_op jit(solution)/shard_map/ppermute | solution.py:673
  33.6 2.0 %collective-permute-done.1 = s32[160,256]{1,0:T(8,128)S(1)} collective-permute-done((s32[160,256]{1,0:T(8,128)S(1)}, s32[160,256]{1,0:T(8,128)S(1)}, u32[]{:S(2)}, u32[]{:S(2)}) %collective-permute-start.1) | collective-permute-done | bytes 163872 | tf_op jit(solution)/shard_map/ppermute | solution.py:673
  35.5 3.1 %collective-permute-done.2 = s32[160,256]{1,0:T(8,128)S(1)} collective-permute-done((s32[160,256]{1,0:T(8,128)S(1)}, s32[160,256]{1,0:T(8,128)S(1)}, u32[]{:S(2)}, u32[]{:S(2)}) %collective-permute-start.2) | collective-permute-done | bytes 163872 | tf_op jit(solution)/shard_map/ppermute | solution.py:673
  38.6 1.9 %collective-permute-start.4 = (f32[2304,128]{1,0:T(8,128)S(1)}, f32[2304,128]{1,0:T(8,128)S(1)}, u32[]{:S(2)}, u32[]{:S(2)}) collective-permute-start(f32[2304,128]{1,0:T(8,128)S(1)} %bitcast.26), channel_id=1, source_target_pairs={{0,1},{1,0},{2,3},{3,2},{4,5},{5,4},{6,7},{7,6},{8,9},{9,8},{10,11... | collective-permute-start | bytes 3538952 | tf_op jit(solution)/shard_map/ppermute | solution.py:601
  40.6 1.2 %collective-permute-start.3 = (s32[4,160,256]{2,1,0:T(8,128)S(1)}, s32[4,160,256]{2,1,0:T(8,128)S(1)}, u32[]{:S(2)}, u32[]{:S(2)}) collective-permute-start(s32[4,160,256]{2,1,0:T(8,128)S(1)} %pad_add_fusion.refs_2_), channel_id=1, source_target_pairs={{32,0},{40,8},{48,16},{56,24},{0,32},{8,40},{16,48},{24,56},{96,64... | collective-permute-start | bytes 1966088 | tf_op jit(solution)/shard_map/ppermute | solution.py:673
  41.8 1.2 %collective-permute-done.4.refs_1_ = f32[2304,128]{1,0:T(8,128)S(1)} collective-permute-done((f32[2304,128]{1,0:T(8,128)S(1)}, f32[2304,128]{1,0:T(8,128)S(1)}, u32[]{:S(2)}, u32[]{:S(2)}) %collective-permute-start.4) | collective-permute-done | bytes 1179680 | tf_op jit(solution)/shard_map/ppermute | solution.py:601
  43.1 13.7 %first.1 = (f32[3,2,2,160,256]{4,3,2,1,0:T(8,128)}, f32[2,2,160,256]{3,2,1,0:T(8,128)S(1)}, f32[2,1120,128]{2,1,0:T(8,128)S(1)}, f32[8,8,128]{2,1,0:T(8,128)S(1)...) custom-call(f32[2304,128]{1,0:T(8,128)S(1)} %bitcast.27, ...), custom_call_target="tpu_custom_call" | custom-call | flops 6000000000 | bytes 30000000 | tf_op jit(solution)/shard_map/first/pallas_call | solution.py:683
  56.8 0.1 collective-permute-done.3.mask
  56.9 5.0 %second.1 = (f32[1152,128]{1,0:T(8,128)S(1)}, f32[1152,128]{1,0:T(8,128)S(1)}) custom-call(s32[4,160,256]{2,1,0:T(8,128)S(1)} %collective-permute-done.3.mask, f32[3,2,2,160,256]{4,3,2,1,0:T(8,128)} %get-tuple-element.32.spectrum, f32[2,2,160,256]{3,2,1,0:T(8,128)S(1)} %get-tuple-element.33.last, f32[2,1120,128]{2,1,0:T(8,128)S(1)} %get-tuple-element.34.point, ...), custom_call_target="tpu_custom_call" | custom-call | flops 3200000000 | bytes 16000000 | tf_op jit(solution)/shard_map/second/pallas_call | solution.py:721
  61.9 0.9 collective-permute-start.5
  62.8 1.6 %collective-permute-done.5 = f32[1152,128]{1,0:T(8,128)S(1)} collective-permute-done((f32[1152,128]{1,0:T(8,128)S(1)}, f32[1152,128]{1,0:T(8,128)S(1)}, u32[]{:S(2)}, u32[]{:S(2)}) %collective-permute-start.5) | collective-permute-done | bytes 589856 | tf_op jit(solution)/shard_map/ppermute | solution.py:601
  64.4 0.1 add.8
  64.5 20.8 %all_to_all.15 = f32[64,1,2304]{2,1,0:T(1,128)S(1)} all-to-all(f32[64,1,2304]{2,1,0:T(1,128)S(1)} %bitcast.30), channel_id=1, replica_groups={{0,2,4,6,8,10,12,14,16,18,20,22,24,26,28,30,32,34,36,38,40,42,44,46,48,..., dimensions={0} | all-to-all | bytes 1179648 | tf_op jit(solution)/shard_map/all_to_all | solution.py:607
  85.3 1.5 %sums.1 = (f32[18,4,8,128]{3,2,1,0:T(8,128)}, f32[128,128]{1,0:T(8,128)}) custom-call(f32[1152,128]{1,0:T(8,128)S(1)} %bitcast.28, f32[4,18,8,128]{3,2,1,0:T(8,128)S(1)} %get-tuple-element.42.direction, f32[4,18,8,128]{3,2,1,0:T(8,128)S(1)} %dense.1.residual), custom_call_target="tpu_custom_call" | custom-call | flops 400000000 | bytes 2000000 | tf_op jit(solution)/shard_map/sums/pallas_call | solution.py:748
  86.8 5.4 %all-to-all-start.2 = ((f32[128,1,128]{2,1,0:T(1,128)}), f32[128,1,128]{2,1,0:T(1,128)S(1)}, u32[]{:S(2)}, u32[]{:S(2)}) async-start(f32[128,1,128]{2,1,0:T(1,128)} %bitcast.17), calls=%async_computation.2 | async-start | bytes 131072 | tf_op jit(solution)/shard_map/all_to_all | solution.py:758
  92.2 2.5 %native.1 = (f32[3,8,16,20]{3,2,1,0:T(8,128)}, f32[48,8,16,20]{3,2,1,0:T(8,128)S(1)}) custom-call(f32[18,4,8,128]{3,2,1,0:T(8,128)} %get-tuple-element.45.dense_in, f32[2,8,8,16,20]{4,3,2,1,0:T(8,128)} %bitcast.41, f32[2,8,8,16,20]{4,3,2,1,0:T(8,128)} %bitcast.43), custom_call_target="tpu_custom_call" | custom-call | flops 1200000000 | bytes 6000000 | tf_op jit(solution)/shard_map/native/pallas_call | solution.py:761
  94.7 7.2 %all-to-all-done.2 = f32[128,1,128]{2,1,0:T(1,128)S(1)} async-done(((f32[128,1,128]{2,1,0:T(1,128)}), f32[128,1,128]{2,1,0:T(1,128)S(1)}, u32[]{:S(2)}, u32[]{:S(2)}) %all-to-all-start.2) | async-done | bytes 65568 | tf_op jit(solution)/shard_map/all_to_all | solution.py:758
  101.9 2.3 %step.1 = (f32[3,8,16,20]{3,2,1,0:T(8,128)}, f32[2,8,8,16,20]{4,3,2,1,0:T(8,128)}, f32[3,8,16,20]{3,2,1,0:T(8,128)}, f32[2,8,8,16,20]{4,3,2,1,0:T(8,128)}) custom-call(f32[128,128]{1,0:T(8,128)S(1)} %bitcast.29, f32[48,8,16,20]{3,2,1,0:T(8,128)S(1)} %get-tuple-element.46.fields, f32[3,8,16,20]{3,2,1,0:T(8,128)} %get-tuple-element.47.app_maps, ...), custom_call_target="tpu_custom_call" | custom-call | flops 800000000 | bytes 4000000 | tf_op jit(solution)/shard_map/step/pallas_call | solution.py:778
  (5 shorter events, 0.1 us)
Async XLA Ops:
  0.6 18.9 %copy-start = (s32[2,160,256]{2,1,0:T(8,128)S(1)}, s32[2,160,256]{2,1,0:T(8,128)}, u32[]{:S(2)}) copy-start(s32[2,160,256]{2,1,0:T(8,128)} %param.20) | copy-start | bytes 983044
  4.8 33.8 %all-to-all-start = ((f32[64,1,4608]{2,1,0:T(1,128)}), f32[64,1,4608]{2,1,0:T(1,128)S(1)}, u32[]{:S(2)}, u32[]{:S(2)}) async-start(f32[64,1,4608]{2,1,0:T(1,128)} %bitcast.5), calls=%async_computation | async-start | bytes 2359296 | tf_op jit(solution)/shard_map/all_to_all | solution.py:607
  19.6 14.0 %collective-permute-start = (s32[160,256]{1,0:T(8,128)S(1)}, s32[160,256]{1,0:T(8,128)S(1)}, u32[]{:S(2)}, u32[]{:S(2)}) collective-permute-start(s32[160,256]{1,0:T(8,128)S(1)} %dynamic-slice_bitcast_fusion), channel_id=1, source_target_pairs={{8,0},{16,8},{24,16},{0,24},{40,32},{48,40},{56,48},{32,56},{72,64... | collective-permute-start | bytes 491528 | tf_op jit(solution)/shard_map/ppermute | solution.py:673
  21.9 13.6 %collective-permute-start.1 = (s32[160,256]{1,0:T(8,128)S(1)}, s32[160,256]{1,0:T(8,128)S(1)}, u32[]{:S(2)}, u32[]{:S(2)}) collective-permute-start(s32[160,256]{1,0:T(8,128)S(1)} %dynamic-slice_bitcast_fusion), channel_id=1, source_target_pairs={{24,0},{0,8},{8,16},{16,24},{56,32},{32,40},{40,48},{48,56},{88,64... | collective-permute-start | bytes 491528 | tf_op jit(solution)/shard_map/ppermute | solution.py:673
  21.9 16.7 %collective-permute-start.2 = (s32[160,256]{1,0:T(8,128)S(1)}, s32[160,256]{1,0:T(8,128)S(1)}, u32[]{:S(2)}, u32[]{:S(2)}) collective-permute-start(s32[160,256]{1,0:T(8,128)S(1)} %dynamic-slice_bitcast_fusion), channel_id=1, source_target_pairs={{16,0},{24,8},{0,16},{8,24},{48,32},{56,40},{32,48},{40,56},{80,64... | collective-permute-start | bytes 491528 | tf_op jit(solution)/shard_map/ppermute | solution.py:673
  38.6 4.4 %collective-permute-start.4 = (f32[2304,128]{1,0:T(8,128)S(1)}, f32[2304,128]{1,0:T(8,128)S(1)}, u32[]{:S(2)}, u32[]{:S(2)}) collective-permute-start(f32[2304,128]{1,0:T(8,128)S(1)} %bitcast.26), channel_id=1, source_target_pairs={{0,1},{1,0},{2,3},{3,2},{4,5},{5,4},{6,7},{7,6},{8,9},{9,8},{10,11... | collective-permute-start | bytes 3538952 | tf_op jit(solution)/shard_map/ppermute | solution.py:601
  40.6 16.3 %collective-permute-start.3 = (s32[4,160,256]{2,1,0:T(8,128)S(1)}, s32[4,160,256]{2,1,0:T(8,128)S(1)}, u32[]{:S(2)}, u32[]{:S(2)}) collective-permute-start(s32[4,160,256]{2,1,0:T(8,128)S(1)} %pad_add_fusion.refs_2_), channel_id=1, source_target_pairs={{32,0},{40,8},{48,16},{56,24},{0,32},{8,40},{16,48},{24,56},{96,64... | collective-permute-start | bytes 1966088 | tf_op jit(solution)/shard_map/ppermute | solution.py:673
  61.9 2.6 %collective-permute-start.5 = (f32[1152,128]{1,0:T(8,128)S(1)}, f32[1152,128]{1,0:T(8,128)S(1)}, u32[]{:S(2)}, u32[]{:S(2)}) collective-permute-start(f32[1152,128]{1,0:T(8,128)S(1)} %get-tuple-element.41), channel_id=1, source_target_pairs={{0,1},{1,0},{2,3},{3,2},{4,5},{5,4},{6,7},{7,6},{8,9},{9,8},{10,11... | collective-permute-start | bytes 1769480 | tf_op jit(solution)/shard_map/ppermute | solution.py:601
  86.8 15.1 %all-to-all-start.2 = ((f32[128,1,128]{2,1,0:T(1,128)}), f32[128,1,128]{2,1,0:T(1,128)S(1)}, u32[]{:S(2)}, u32[]{:S(2)}) async-start(f32[128,1,128]{2,1,0:T(1,128)} %bitcast.17), calls=%async_computation.2 | async-start | bytes 131072 | tf_op jit(solution)/shard_map/all_to_all | solution.py:758

commit v5 on v4

--- a/solution.py
+++ b/solution.py
@@ -20,7 +20,8 @@
 MSG = TILES * LANES
 ITEMS = 9
 BINS = 8
-FULL = 4
+NEAR = 5
+STEPS = ((0, 0), (0, 1), (0, 3), (1, 0), (3, 0), (1, 1), (1, 3), (2, 0))
 WHOLE = 2 * TILES
 VMEM_LIMIT = 32 * 1024 * 1024
 f32 = jnp.float32
@@ -126,6 +127,10 @@
 
 def plane(ref, f):
     return jnp.concatenate([ref[0, f * NZ : (f + 1) * NZ], ref[1, f * NZ : (f + 1) * NZ]], axis=1)
+
+
+def pairs_of(g):
+    return (g, 4 + (g ^ 1))
 
 
 def names_of(g):
@@ -156,8 +161,8 @@
 
 def pack_kernel(
     times, maps_in, coils_in, point_maps, point_coils,
-    send, dense,
-    maps, coils, of_maps, of_coils, stamp, stacked, turned, sems,
+    send_out, dense,
+    send, maps, coils, of_maps, of_coils, stamp, stacked, turned, sems,
 ):
     t = lax.axis_index("ti")
     maps_copies = [
@@ -189,30 +194,38 @@
         copy.start()
     for copy in point_copies:
         copy.wait()
-    for i in range(ITEMS):
-        for g in range(4):
-            tile = jnp.where(items[i] < 3, of_maps[i], of_coils[i, g])
-            for m in (g, g + 4):
-                for half in range(2):
-                    first = 8 * m * WHOLE + TILES + 2 * i + half
-                    send[pl.ds(first, 8, stride=WHOLE), :] = tile[:, half * LANES : (half + 1) * LANES]
     for copy in maps_copies:
         copy.wait()
     lane = iota((8, LANES), 1)
     spare = jnp.where(lane == 64, stamp[0], jnp.where(lane == 65, stamp[1], 0.0))
 
+    stores = []
+
     def emit(g, u, tile):
         dense[g, u] = tile
         if u == TILES - 1:
             tile = jnp.where(lane < 64, tile, spare)
-        for m in (g, g + 4):
+        for m in pairs_of(g):
             send[pl.ds(8 * m * WHOLE + u, 8, stride=WHOLE), :] = tile
+        if u == TILES - 1:
+            for m in pairs_of(g):
+                rows = pl.ds(8 * m * WHOLE, 8 * WHOLE)
+                stores.append(pltpu.make_async_copy(send.at[rows], send_out.at[rows], sems.at[len(stores)]))
+                stores[-1].start()
 
     def arrive(g):
+        for i in range(ITEMS):
+            tile = jnp.where(items[i] < 3, of_maps[i], of_coils[i, g])
+            for m in pairs_of(g):
+                for half in range(2):
+                    first = 8 * m * WHOLE + TILES + 2 * i + half
+                    send[pl.ds(first, 8, stride=WHOLE), :] = tile[:, half * LANES : (half + 1) * LANES]
         for copy in coils_copies[2 * g : 2 * g + 2]:
             copy.wait()
 
     dense_tiles(maps, coils, stacked, turned, emit, arrive)
+    for copy in stores:
+        copy.wait()
 
 
 def dense_kernel(maps_in, coils_in, dense, maps, coils, stacked, turned, sems):
@@ -259,10 +272,14 @@
                     direction[half, 8 * n : 8 * n + 8] = tile
 
 
+def model_terms(tau, point):
+    decays = jnp.exp(-tau * plane(point, 2))
+    return decays, plane(point, 0) - plane(point, 1) * decays
+
+
 def forward_bin(tau, point, direction, table_y, table_z, spectrum):
     amplitude = plane(point, 1)
-    decays = jnp.exp(-tau * plane(point, 2))
-    signal = plane(point, 0) - amplitude * decays
+    decays, signal = model_terms(tau, point)
     change = plane(direction, 0) - plane(direction, 1) * decays + amplitude * tau * decays * plane(direction, 2)
     evens, odds = [], []
     for c in range(2):
@@ -285,9 +302,10 @@
             a, b = (side[part * HALF_Z : (part + 1) * HALF_Z] for side in parts)
             spectrum[c, part, :HALF_Z] = a + b
             spectrum[c, part, HALF_Z:] = a - b
-
-
-def backward_bin(tau, mask, spectrum, point, table_y, table_z, order, total):
+    return decays, signal
+
+
+def backward_bin(tau, decays, signal, mask, spectrum, point, table_y, table_z, order, total):
     weights = jnp.dot(mask.astype(f32).astype(bf16), order[...], preferred_element_type=f32)
     evens, odds = [], []
     for c in range(2):
@@ -309,9 +327,6 @@
         for half in range(2):
             total[half, f * NZ : (f + 1) * NZ] += values[:, half * LANES : (half + 1) * LANES]
 
-    amplitude = plane(point, 1)
-    decays = jnp.exp(-tau * plane(point, 2))
-    signal = plane(point, 0) - amplitude * decays
     projected = None
     for c in range(2):
         sides = []
@@ -327,7 +342,7 @@
     add(0, projected)
     faded = decays * projected
     add(1, -faded)
-    add(2, amplitude * (tau * faded))
+    add(2, plane(point, 1) * (tau * faded))
 
 
 def pack_sums(core, total, sent, rest, mine, theirs):
@@ -354,20 +369,21 @@
 
 
 def first_kernel(*refs):
-    own, other, mask, *tables_in = refs[:8]
-    spectrum, last, point, taus, total, backward_y, backward_z, order = refs[8:16]
-    direction, rest, forward_y, forward_z, kept, sems = refs[16:]
+    own, other, *masks = refs[: 2 + NEAR]
+    tables_in, refs = refs[2 + NEAR : 7 + NEAR], refs[7 + NEAR :]
+    spectrum, last, point, taus, total, backward_y, backward_z, order = refs[:8]
+    direction, rest, forward_y, forward_z, kept, mask, sems = refs[8:]
     step = pl.program_id(0)
     t, core = lax.axis_index("ti"), lax.axis_index("kz") & 1
     slot = step & 1
-    tables = (forward_y, forward_z, backward_y, backward_z, order)
-    copies = [pltpu.make_async_copy(a, b, sems.at[2 + i]) for i, (a, b) in enumerate(zip(tables_in, tables))]
 
     def store(at, side):
-        return pltpu.make_async_copy(kept.at[side], spectrum.at[at - FULL], sems.at[side])
+        return pltpu.make_async_copy(kept.at[side], spectrum.at[at - NEAR], sems.at[side])
 
     @pl.when(step == 0)
     def _():
+        tables = (forward_y, forward_z, backward_y, backward_z, order)
+        copies = [pltpu.make_async_copy(a, b, sems.at[2 + i]) for i, (a, b) in enumerate(zip(tables_in, tables))]
         for copy in copies:
             copy.start()
         total[...] = jnp.zeros_like(total)
@@ -377,28 +393,33 @@
         for copy in copies:
             copy.wait()
 
-    @pl.when(step >= FULL + 2)
+    @pl.when(step >= NEAR + 2)
     def _():
         store(step - 2, slot).wait()
 
-    spread = (step & 3) ^ ((step & 2) >> 1)
-    bin_of = ((t & 12) | ((t + spread) & 3)) ^ (step & 4)
+    for n in range(NEAR):
+
+        @pl.when(step == n)
+        def _():
+            mask[...] = masks[n][...]
+
+    along_z, along_x = (
+        sum(jnp.where(step == n, moves[axis], 0) for n, moves in enumerate(STEPS)) for axis in range(2)
+    )
+    bin_of = (((t >> 2) + along_z) & 3) * 4 + ((t + along_x) & 3)
     block = rest[1, pl.ds(pl.multiple_of(bin_of * 8, 8), 8), :]
     chosen = (iota((8, LANES), 0) == 0) & (iota((8, LANES), 1) == 64 + core)
     tau = jnp.sum(jnp.where(chosen, block, 0.0), axis=(0, 1), keepdims=True)
-
     taus[0] = jnp.broadcast_to(tau, (8, LANES))
 
-    @pl.when(step < BINS - 1)
+    @pl.when(step < NEAR)
+    def _():
+        decays, signal = forward_bin(tau, point, direction, forward_y, forward_z, kept.at[slot])
+        backward_bin(tau, decays, signal, mask[...], kept.at[slot], point, backward_y, backward_z, order, total)
+
+    @pl.when((step >= NEAR) & (step < BINS - 1))
     def _():
         forward_bin(tau, point, direction, forward_y, forward_z, kept.at[slot])
-
-    @pl.when(step < FULL)
-    def _():
-        backward_bin(tau, mask[0], kept.at[slot], point, backward_y, backward_z, order, total)
-
-    @pl.when((step >= FULL) & (step < BINS - 1))
-    def _():
         store(step, slot).start()
 
     @pl.when(step == BINS - 1)
@@ -424,7 +445,7 @@
         total[...] = total_in[...]
         kept[0] = last[...]
 
-    @pl.when(step < BINS - FULL - 1)
+    @pl.when(step < BINS - NEAR - 1)
     def _():
         load(step + 1).start()
 
@@ -433,9 +454,10 @@
         load(step).wait()
 
     tau = taus[0, 0:1, 0:1]
-    backward_bin(tau, mask[0], kept.at[slot], point, table_y, table_z, order, total)
-
-    @pl.when(step == BINS - FULL - 1)
+    decays, signal = model_terms(tau, point)
+    backward_bin(tau, decays, signal, mask[0], kept.at[slot], point, table_y, table_z, order, total)
+
+    @pl.when(step == BINS - NEAR - 1)
     def _():
         pack_sums(core, total, sent, rest, mine, theirs)
 
@@ -447,7 +469,7 @@
     for u in range(TILES):
         sides = []
         for g in range(4):
-            upper, lower = (received[pl.ds(8 * m * TILES + u, 8, stride=TILES), :] for m in (g, g + 4))
+            upper, lower = (received[pl.ds(8 * m * TILES + u, 8, stride=TILES), :] for m in pairs_of(g))
             sides.append(upper + lower)
         if u < MAIN:
             maps = sides[0] + sides[1] + sides[2] + sides[3]
@@ -626,12 +648,13 @@
     send, dir_dense = pl.pallas_call(
         pack_kernel,
         out_shape=(
-            struct(64 * WHOLE, LANES),
+            far(64 * WHOLE, LANES),
             near(4, TILES, 8, LANES),
         ),
         in_specs=[HBM] * 5,
-        out_specs=(VMEM, VMEM),
+        out_specs=(HBM, VMEM),
         scratch_shapes=[
+            pltpu.VMEM((64 * WHOLE, LANES), f32),
             pltpu.VMEM(dir_maps.shape, f32),
             pltpu.VMEM(dir_coils.shape, f32),
             pltpu.VMEM((ITEMS, 8, NY), f32),
@@ -664,18 +687,20 @@
             name="dense",
         )(*in_hbm(maps, coils))
 
+    own_mask = lax.dynamic_index_in_dim(sampling_mask, lax.axis_index("kz") & 1, 0, keepdims=False)
+
+    def from_ti(values, move):
+        pairs = [((((i >> 2) + move[0]) & 3) * 4 + ((i + move[1]) & 3), i) for i in range(16)]
+        return lax.ppermute(values, "ti", pairs)
+
+    masks = [own_mask] + [from_ti(own_mask, move) for move in STEPS[1:NEAR]]
+    send, *masks = lax.optimization_barrier((send, *masks))
     own = by_parity(send)
-    res_dense = densify(res_maps, res_coils)
-    own_mask = lax.dynamic_index_in_dim(sampling_mask, lax.axis_index("kz") & 1, 0, keepdims=False)
-    own_mask, res_dense = lax.optimization_barrier((own_mask, res_dense))
-
-    def from_ti(values, shift, flip):
-        return lax.ppermute(values, "ti", [(((i & 12) | ((i + shift) & 3)) ^ flip, i) for i in range(16)])
-
-    near_masks = jnp.stack([own_mask] + [from_ti(own_mask, shift, 0) for shift in (1, 3, 2)])
-    own, near_masks = lax.optimization_barrier((own, near_masks))
+    res_dense = densify(*lax.optimization_barrier((res_maps, res_coils, dir_dense))[:2])
+    stack = jnp.stack(masks[1:4])
+    own, res_dense, stack = lax.optimization_barrier((own, res_dense, stack))
     other = core_swap(own)
-    far_masks = from_ti(near_masks, 0, 4)
+    far_masks = from_ti(stack, STEPS[3])
     planes = (2, FEATURES * NZ, LANES)
     tables = (forward_y, forward_z, backward_y, backward_z, order)
     sums_shape = struct(64 * TILES, LANES)
@@ -684,7 +709,7 @@
         first_kernel,
         grid=(BINS,),
         out_shape=(
-            far(BINS - FULL - 1, 2, 2, NZ, NY),
+            far(BINS - NEAR - 1, 2, 2, NZ, NY),
             near(2, 2, NZ, NY),
             near(*planes),
             near(BINS, 8, LANES),
@@ -692,7 +717,7 @@
             *[pltpu.VMEM(table.shape, bf16) for table in tables[2:]],
         ),
         in_specs=[constant_block(own.shape)] * 2
-        + [pl.BlockSpec((1, NZ, NY), lambda s: (jnp.minimum(s, FULL - 1), 0, 0))]
+        + [constant_block((NZ, NY))] * NEAR
         + [HBM] * 5,
         out_specs=(
             HBM,
@@ -708,22 +733,23 @@
             pltpu.VMEM(forward_y.shape, bf16),
             pltpu.VMEM(forward_z.shape, bf16),
             pltpu.VMEM((2, 2, 2, NZ, NY), f32),
+            pltpu.VMEM((NZ, NY), jnp.int32),
             pltpu.SemaphoreType.DMA((7,)),
         ],
         compiler_params=params(),
         cost_estimate=cost(15),
         name="first",
-    )(own, other, near_masks, *in_hbm(*tables))
+    )(own, other, *masks, *in_hbm(*tables))
 
     def bin_block(shape, first):
-        return pl.BlockSpec((1,) + shape, lambda s: (jnp.where(s == 0, BINS - 1, s + FULL - 1) - first, 0, 0))
+        return pl.BlockSpec((1,) + shape, lambda s: (jnp.where(s == 0, BINS - 1, s + NEAR - 1) - first, 0, 0))
 
     mine, theirs = pl.pallas_call(
         second_kernel,
-        grid=(BINS - FULL,),
+        grid=(BINS - NEAR,),
         out_shape=(sums_shape, sums_shape),
         in_specs=[
-            bin_block((NZ, NY), FULL),
+            bin_block((NZ, NY), NEAR),
             HBM,
             constant_block((2, 2, NZ, NY)),
             constant_block(planes),

time: 105 us -> 101 us (0.962)
  blocking collectives: 20.8 us -> 17.3 us
    ppermute x4 -> x5, waiting for transfers between devices: 15 us -> 0.01 us  [from_ti(): return lax.ppermute(values, 'ti', pairs)]
    all_to_all x1, waiting for transfers between devices: 0.01 us -> 14.2 us  [by_parity(): lax.all_to_all(messages, AXES, 0, 0, axis_index_groups=groups)]
    all_to_all x1, starting transfers between devices: 12 us -> 7.86 us  [by_parity(): lax.all_to_all(messages, AXES, 0, 0, axis_index_groups=groups)]
    all_to_all x1, blocking collectives: 20.8 us -> 17.3 us  [by_parity(): lax.all_to_all(messages, AXES, 0, 0, axis_index_groups=groups)]
    ppermute x4 -> x5, starting transfers between devices: 5.29 us -> 7.88 us  [from_ti(): return lax.ppermute(values, 'ti', pairs)]
    ppermute x2, starting transfers between devices: 2.89 us -> 4.47 us  [core_swap(): return lax.ppermute(values, 'kz', [(i, i ^ 1) for i in range(8)])]
  transfers between devices with their start and end apart: 8 -> 9, of which waited for: 7 -> 4; matrix products, arithmetic and copies ran while one was open for 0% -> 0% of each run, Pallas kernels for 18% -> 23%
where the time goes in v5:
time: 101 us
  Pallas kernels  31.1 us (31%)
  starting transfers between devices  25.6 us (25%)
  waiting for transfers between devices  25.1 us (25%)
  blocking collectives  17.3 us (17%)
    all_to_all x1, blocking collectives, by_parity(): lax.all_to_all(messages, AXES, 0, 0, axis_index_groups=groups)  17.3 us
    pallas_call x1, Pallas kernels, shards(): pl.pallas_call(first_kernel, grid=(BINS,), out_shape=(far(BINS - NEAR - 1...  14.3 us
    all_to_all x1, waiting for transfers between devices, by_parity(): lax.all_to_all(messages, AXES, 0, 0, axis_index_groups=groups)  14.2 us
    ppermute x5, starting transfers between devices, from_ti(): return lax.ppermute(values, 'ti', pairs)  7.88 us
    all_to_all x1, starting transfers between devices, by_parity(): lax.all_to_all(messages, AXES, 0, 0, axis_index_groups=groups)  7.86 us
    all_to_all x1, waiting for transfers between devices, shards(): lax.all_to_all(sums.reshape(128, 1, LANES), AXES, 0, 0).reshape(128, LANES)  7.19 us
    all_to_all x1, starting transfers between devices, shards(): lax.all_to_all(sums.reshape(128, 1, LANES), AXES, 0, 0).reshape(128, LANES)  5.41 us
    ppermute x2, starting transfers between devices, core_swap(): return lax.ppermute(values, 'kz', [(i, i ^ 1) for i in range(8)])  4.47 us
  transfers between devices with their start and end apart: 9, of which 4 were waited for; matrix products, arithmetic and copies ran while one was open for 0% of the time, Pallas kernels for 23%

profile of v5, /device:TPU:1, one launch (start us, length us, event | category | flops | bytes accessed | tf_op | source)
XLA Modules:
  0.0 100.9 jit_solution(6521555145975633256)
XLA Ops:
  0.6 0.0 copy-start
  0.6 1.0 copy-done
  1.6 2.5 %collective-permute-start.3 = (s32[160,256]{1,0:T(8,128)S(1)}, s32[160,256]{1,0:T(8,128)S(1)}, u32[]{:S(2)}, u32[]{:S(2)}) collective-permute-start(s32[160,256]{1,0:T(8,128)S(1)} %dynamic-slice_bitcast_fusion.refs_2_), channel_id=1, source_target_pairs={{96,0},{104,8},{112,16},{120,24},{0,32},{8,40},{16,48},{24,56},{32... | collective-permute-start | bytes 491528 | tf_op jit(solution)/shard_map/ppermute | solution.py:694
  4.2 2.2 %collective-permute-start.2 = (s32[160,256]{1,0:T(8,128)S(1)}, s32[160,256]{1,0:T(8,128)S(1)}, u32[]{:S(2)}, u32[]{:S(2)}) collective-permute-start(s32[160,256]{1,0:T(8,128)S(1)} %dynamic-slice_bitcast_fusion.refs_2_), channel_id=1, source_target_pairs={{32,0},{40,8},{48,16},{56,24},{64,32},{72,40},{80,48},{88,56},{96,... | collective-permute-start | bytes 491528 | tf_op jit(solution)/shard_map/ppermute | solution.py:694
  6.4 1.2 %collective-permute-start.1 = (s32[160,256]{1,0:T(8,128)S(1)}, s32[160,256]{1,0:T(8,128)S(1)}, u32[]{:S(2)}, u32[]{:S(2)}) collective-permute-start(s32[160,256]{1,0:T(8,128)S(1)} %dynamic-slice_bitcast_fusion.refs_2_), channel_id=1, source_target_pairs={{24,0},{0,8},{8,16},{16,24},{56,32},{32,40},{40,48},{48,56},{88,64... | collective-permute-start | bytes 491528 | tf_op jit(solution)/shard_map/ppermute | solution.py:694
  7.6 1.5 %collective-permute-start = (s32[160,256]{1,0:T(8,128)S(1)}, s32[160,256]{1,0:T(8,128)S(1)}, u32[]{:S(2)}, u32[]{:S(2)}) collective-permute-start(s32[160,256]{1,0:T(8,128)S(1)} %dynamic-slice_bitcast_fusion.refs_2_), channel_id=1, source_target_pairs={{8,0},{16,8},{24,16},{0,24},{40,32},{48,40},{56,48},{32,56},{72,64... | collective-permute-start | bytes 491528 | tf_op jit(solution)/shard_map/ppermute | solution.py:694
  9.0 3.8 %pack.1 = (f32[2304,128]{1,0:T(8,128)}, f32[4,18,8,128]{3,2,1,0:T(8,128)S(1)}) custom-call(f32[2]{0:T(128)} %times.1, f32[3,8,16,20]{3,2,1,0:T(8,128)} %bitcast.34, f32[2,8,8,16,20]{4,3,2,1,0:T(8,128)} %bitcast.39, f32[3,20,8,256]{3,2,1,0:T(8,128)} %bitcast.45, f32[2,4,2,20,8,256]{5,4,3,2,1,0:T(8,128)} %bitcast.38), custom_call_target="tpu_custom_call" | custom-call | flops 1600000000 | bytes 8000000 | tf_op jit(solution)/shard_map/pack/pallas_call | solution.py:648
  12.9 7.9 %all-to-all-start = ((f32[64,1,4608]{2,1,0:T(1,128)}), f32[64,1,4608]{2,1,0:T(1,128)S(1)}, u32[]{:S(2)}, u32[]{:S(2)}) async-start(f32[64,1,4608]{2,1,0:T(1,128)} %bitcast.33), calls=%async_computation | async-start | bytes 2359296 | tf_op jit(solution)/shard_map/all_to_all | solution.py:629
  20.7 2.8 %dense.1.residual = f32[4,18,8,128]{3,2,1,0:T(8,128)S(1)} custom-call(f32[3,8,16,20]{3,2,1,0:T(8,128)} %bitcast.36, f32[2,8,8,16,20]{4,3,2,1,0:T(8,128)} %bitcast.41), custom_call_target="tpu_custom_call" | custom-call | flops 1200000000 | bytes 6000000 | tf_op jit(solution)/shard_map/dense/pallas_call | solution.py:673
  23.6 14.2 %all-to-all-done = f32[64,1,4608]{2,1,0:T(1,128)S(1)} async-done(((f32[64,1,4608]{2,1,0:T(1,128)}), f32[64,1,4608]{2,1,0:T(1,128)S(1)}, u32[]{:S(2)}, u32[]{:S(2)}) %all-to-all-start) | async-done | bytes 1179680 | tf_op jit(solution)/shard_map/all_to_all | solution.py:629
  37.8 4.0 %collective-permute-start.5 = (f32[2304,128]{1,0:T(8,128)S(1)}, f32[2304,128]{1,0:T(8,128)S(1)}, u32[]{:S(2)}, u32[]{:S(2)}) collective-permute-start(f32[2304,128]{1,0:T(8,128)S(1)} %bitcast.25), channel_id=1, source_target_pairs={{0,1},{1,0},{2,3},{3,2},{4,5},{5,4},{6,7},{7,6},{8,9},{9,8},{10,11... | collective-permute-start | bytes 3538952 | tf_op jit(solution)/shard_map/ppermute | solution.py:623
  41.8 0.5 collective-permute-start.4
  42.2 2.0 %collective-permute-done.5.refs_1_ = f32[2304,128]{1,0:T(8,128)S(1)} collective-permute-done((f32[2304,128]{1,0:T(8,128)S(1)}, f32[2304,128]{1,0:T(8,128)S(1)}, u32[]{:S(2)}, u32[]{:S(2)}) %collective-permute-start.5) | collective-permute-done | bytes 1179680 | tf_op jit(solution)/shard_map/ppermute | solution.py:623
  44.2 14.3 %first.1 = (f32[2,2,2,160,256]{4,3,2,1,0:T(8,128)}, f32[2,2,160,256]{3,2,1,0:T(8,128)S(1)}, f32[2,1120,128]{2,1,0:T(8,128)S(1)}, f32[8,8,128]{2,1,0:T(8,128)S(1)...) custom-call(f32[2304,128]{1,0:T(8,128)S(1)} %bitcast.26, ...), custom_call_target="tpu_custom_call" | custom-call | flops 6000000000 | bytes 30000000 | tf_op jit(solution)/shard_map/first/pallas_call | solution.py:708
  58.6 3.9 %second.1 = (f32[1152,128]{1,0:T(8,128)S(1)}, f32[1152,128]{1,0:T(8,128)S(1)}) custom-call(s32[3,160,256]{2,1,0:T(8,128)S(1)} %collective-permute-done.4.mask, f32[2,2,2,160,256]{4,3,2,1,0:T(8,128)} %get-tuple-element.47.spectrum, f32[2,2,160,256]{3,2,1,0:T(8,128)S(1)} %get-tuple-element.48.last, f32[2,1120,128]{2,1,0:T(8,128)S(1)} %get-tuple-element.49.point, ...), custom_call_target="tpu_custom_call" | custom-call | flops 3200000000 | bytes 16000000 | tf_op jit(solution)/shard_map/second/pallas_call | solution.py:747
  62.5 0.5 collective-permute-start.6
  63.0 1.6 %collective-permute-done.6 = f32[1152,128]{1,0:T(8,128)S(1)} collective-permute-done((f32[1152,128]{1,0:T(8,128)S(1)}, f32[1152,128]{1,0:T(8,128)S(1)}, u32[]{:S(2)}, u32[]{:S(2)}) %collective-permute-start.6) | collective-permute-done | bytes 589856 | tf_op jit(solution)/shard_map/ppermute | solution.py:623
  64.7 0.1 add.8
  64.7 17.3 %all_to_all.15 = f32[64,1,2304]{2,1,0:T(1,128)S(1)} all-to-all(f32[64,1,2304]{2,1,0:T(1,128)S(1)} %bitcast.32), channel_id=1, replica_groups={{0,2,4,6,8,10,12,14,16,18,20,22,24,26,28,30,32,34,36,38,40,42,44,46,48,..., dimensions={0} | all-to-all | bytes 1179648 | tf_op jit(solution)/shard_map/all_to_all | solution.py:629
  82.0 1.5 %sums.1 = (f32[18,4,8,128]{3,2,1,0:T(8,128)}, f32[128,128]{1,0:T(8,128)}) custom-call(f32[1152,128]{1,0:T(8,128)S(1)} %bitcast.27, f32[4,18,8,128]{3,2,1,0:T(8,128)S(1)} %get-tuple-element.37.direction, f32[4,18,8,128]{3,2,1,0:T(8,128)S(1)} %dense.1.residual), custom_call_target="tpu_custom_call" | custom-call | flops 400000000 | bytes 2000000 | tf_op jit(solution)/shard_map/sums/pallas_call | solution.py:774
  83.5 5.4 %all-to-all-start.2 = ((f32[128,1,128]{2,1,0:T(1,128)}), f32[128,1,128]{2,1,0:T(1,128)S(1)}, u32[]{:S(2)}, u32[]{:S(2)}) async-start(f32[128,1,128]{2,1,0:T(1,128)} %bitcast.16), calls=%async_computation.2 | async-start | bytes 131072 | tf_op jit(solution)/shard_map/all_to_all | solution.py:784
  88.9 2.5 %native.1 = (f32[3,8,16,20]{3,2,1,0:T(8,128)}, f32[48,8,16,20]{3,2,1,0:T(8,128)S(1)}) custom-call(f32[18,4,8,128]{3,2,1,0:T(8,128)} %get-tuple-element.59.dense_in, f32[2,8,8,16,20]{4,3,2,1,0:T(8,128)} %bitcast.40, f32[2,8,8,16,20]{4,3,2,1,0:T(8,128)} %bitcast.42), custom_call_target="tpu_custom_call" | custom-call | flops 1200000000 | bytes 6000000 | tf_op jit(solution)/shard_map/native/pallas_call | solution.py:787
  91.4 7.2 %all-to-all-done.2 = f32[128,1,128]{2,1,0:T(1,128)S(1)} async-done(((f32[128,1,128]{2,1,0:T(1,128)}), f32[128,1,128]{2,1,0:T(1,128)S(1)}, u32[]{:S(2)}, u32[]{:S(2)}) %all-to-all-start.2) | async-done | bytes 65568 | tf_op jit(solution)/shard_map/all_to_all | solution.py:784
  98.6 2.3 %step.1 = (f32[3,8,16,20]{3,2,1,0:T(8,128)}, f32[2,8,8,16,20]{4,3,2,1,0:T(8,128)}, f32[3,8,16,20]{3,2,1,0:T(8,128)}, f32[2,8,8,16,20]{4,3,2,1,0:T(8,128)}) custom-call(f32[128,128]{1,0:T(8,128)S(1)} %bitcast.28, f32[48,8,16,20]{3,2,1,0:T(8,128)S(1)} %get-tuple-element.60.fields, f32[3,8,16,20]{3,2,1,0:T(8,128)} %get-tuple-element.61.app_maps, ...), custom_call_target="tpu_custom_call" | custom-call | flops 800000000 | bytes 4000000 | tf_op jit(solution)/shard_map/step/pallas_call | solution.py:804
  (7 shorter events, 0.1 us)
Async XLA Ops:
  0.6 1.0 copy-start
  1.6 11.2 %collective-permute-start.3 = (s32[160,256]{1,0:T(8,128)S(1)}, s32[160,256]{1,0:T(8,128)S(1)}, u32[]{:S(2)}, u32[]{:S(2)}) collective-permute-start(s32[160,256]{1,0:T(8,128)S(1)} %dynamic-slice_bitcast_fusion.refs_2_), channel_id=1, source_target_pairs={{96,0},{104,8},{112,16},{120,24},{0,32},{8,40},{16,48},{24,56},{32... | collective-permute-start | bytes 491528 | tf_op jit(solution)/shard_map/ppermute | solution.py:694
  4.2 8.7 %collective-permute-start.2 = (s32[160,256]{1,0:T(8,128)S(1)}, s32[160,256]{1,0:T(8,128)S(1)}, u32[]{:S(2)}, u32[]{:S(2)}) collective-permute-start(s32[160,256]{1,0:T(8,128)S(1)} %dynamic-slice_bitcast_fusion.refs_2_), channel_id=1, source_target_pairs={{32,0},{40,8},{48,16},{56,24},{64,32},{72,40},{80,48},{88,56},{96,... | collective-permute-start | bytes 491528 | tf_op jit(solution)/shard_map/ppermute | solution.py:694
  6.4 6.5 %collective-permute-start.1 = (s32[160,256]{1,0:T(8,128)S(1)}, s32[160,256]{1,0:T(8,128)S(1)}, u32[]{:S(2)}, u32[]{:S(2)}) collective-permute-start(s32[160,256]{1,0:T(8,128)S(1)} %dynamic-slice_bitcast_fusion.refs_2_), channel_id=1, source_target_pairs={{24,0},{0,8},{8,16},{16,24},{56,32},{32,40},{40,48},{48,56},{88,64... | collective-permute-start | bytes 491528 | tf_op jit(solution)/shard_map/ppermute | solution.py:694
  7.6 5.3 %collective-permute-start = (s32[160,256]{1,0:T(8,128)S(1)}, s32[160,256]{1,0:T(8,128)S(1)}, u32[]{:S(2)}, u32[]{:S(2)}) collective-permute-start(s32[160,256]{1,0:T(8,128)S(1)} %dynamic-slice_bitcast_fusion.refs_2_), channel_id=1, source_target_pairs={{8,0},{16,8},{24,16},{0,24},{40,32},{48,40},{56,48},{32,56},{72,64... | collective-permute-start | bytes 491528 | tf_op jit(solution)/shard_map/ppermute | solution.py:694
  12.9 24.9 %all-to-all-start = ((f32[64,1,4608]{2,1,0:T(1,128)}), f32[64,1,4608]{2,1,0:T(1,128)S(1)}, u32[]{:S(2)}, u32[]{:S(2)}) async-start(f32[64,1,4608]{2,1,0:T(1,128)} %bitcast.33), calls=%async_computation | async-start | bytes 2359296 | tf_op jit(solution)/shard_map/all_to_all | solution.py:629
  37.8 6.5 %collective-permute-start.5 = (f32[2304,128]{1,0:T(8,128)S(1)}, f32[2304,128]{1,0:T(8,128)S(1)}, u32[]{:S(2)}, u32[]{:S(2)}) collective-permute-start(f32[2304,128]{1,0:T(8,128)S(1)} %bitcast.25), channel_id=1, source_target_pairs={{0,1},{1,0},{2,3},{3,2},{4,5},{5,4},{6,7},{7,6},{8,9},{9,8},{10,11... | collective-permute-start | bytes 3538952 | tf_op jit(solution)/shard_map/ppermute | solution.py:623
  41.8 16.8 %collective-permute-start.4 = (s32[3,160,256]{2,1,0:T(8,128)S(1)}, s32[3,160,256]{2,1,0:T(8,128)S(1)}, u32[]{:S(2)}, u32[]{:S(2)}) collective-permute-start(s32[3,160,256]{2,1,0:T(8,128)S(1)} %pad_add_fusion), channel_id=1, source_target_pairs={{32,0},{40,8},{48,16},{56,24},{64,32},{72,40},{80,48},{88,56},{96,... | collective-permute-start | bytes 1474568 | tf_op jit(solution)/shard_map/ppermute | solution.py:694
  62.5 2.1 %collective-permute-start.6 = (f32[1152,128]{1,0:T(8,128)S(1)}, f32[1152,128]{1,0:T(8,128)S(1)}, u32[]{:S(2)}, u32[]{:S(2)}) collective-permute-start(f32[1152,128]{1,0:T(8,128)S(1)} %get-tuple-element.56), channel_id=1, source_target_pairs={{0,1},{1,0},{2,3},{3,2},{4,5},{5,4},{6,7},{7,6},{8,9},{9,8},{10,11... | collective-permute-start | bytes 1769480 | tf_op jit(solution)/shard_map/ppermute | solution.py:623
  83.5 15.1 %all-to-all-start.2 = ((f32[128,1,128]{2,1,0:T(1,128)}), f32[128,1,128]{2,1,0:T(1,128)S(1)}, u32[]{:S(2)}, u32[]{:S(2)}) async-start(f32[128,1,128]{2,1,0:T(1,128)} %bitcast.16), calls=%async_computation.2 | async-start | bytes 131072 | tf_op jit(solution)/shard_map/all_to_all | solution.py:784

commit v6 on v5

--- a/solution.py
+++ b/solution.py
@@ -371,19 +371,15 @@
 def first_kernel(*refs):
     own, other, *masks = refs[: 2 + NEAR]
     tables_in, refs = refs[2 + NEAR : 7 + NEAR], refs[7 + NEAR :]
-    spectrum, last, point, taus, total, backward_y, backward_z, order = refs[:8]
-    direction, rest, forward_y, forward_z, kept, mask, sems = refs[8:]
+    spectra, point, taus, total, backward_y, backward_z, order = refs[:7]
+    direction, rest, forward_y, forward_z, kept, sems = refs[7:]
     step = pl.program_id(0)
     t, core = lax.axis_index("ti"), lax.axis_index("kz") & 1
-    slot = step & 1
-
-    def store(at, side):
-        return pltpu.make_async_copy(kept.at[side], spectrum.at[at - NEAR], sems.at[side])
 
     @pl.when(step == 0)
     def _():
         tables = (forward_y, forward_z, backward_y, backward_z, order)
-        copies = [pltpu.make_async_copy(a, b, sems.at[2 + i]) for i, (a, b) in enumerate(zip(tables_in, tables))]
+        copies = [pltpu.make_async_copy(a, b, sems.at[i]) for i, (a, b) in enumerate(zip(tables_in, tables))]
         for copy in copies:
             copy.start()
         total[...] = jnp.zeros_like(total)
@@ -393,73 +389,37 @@
         for copy in copies:
             copy.wait()
 
-    @pl.when(step >= NEAR + 2)
-    def _():
-        store(step - 2, slot).wait()
-
-    for n in range(NEAR):
-
-        @pl.when(step == n)
+    def bin_time(n):
+        along_z, along_x = STEPS[n]
+        bin_of = (((t >> 2) + along_z) & 3) * 4 + ((t + along_x) & 3)
+        block = rest[1, pl.ds(pl.multiple_of(bin_of * 8, 8), 8), :]
+        chosen = (iota((8, LANES), 0) == 0) & (iota((8, LANES), 1) == 64 + core)
+        tau = jnp.sum(jnp.where(chosen, block, 0.0), axis=(0, 1), keepdims=True)
+        taus[n] = jnp.broadcast_to(tau, (8, LANES))
+        return tau
+
+    for first in range(0, BINS, 2):
+
+        @pl.when(step == first // 2)
         def _():
-            mask[...] = masks[n][...]
-
-    along_z, along_x = (
-        sum(jnp.where(step == n, moves[axis], 0) for n, moves in enumerate(STEPS)) for axis in range(2)
-    )
-    bin_of = (((t >> 2) + along_z) & 3) * 4 + ((t + along_x) & 3)
-    block = rest[1, pl.ds(pl.multiple_of(bin_of * 8, 8), 8), :]
-    chosen = (iota((8, LANES), 0) == 0) & (iota((8, LANES), 1) == 64 + core)
-    tau = jnp.sum(jnp.where(chosen, block, 0.0), axis=(0, 1), keepdims=True)
-    taus[0] = jnp.broadcast_to(tau, (8, LANES))
-
-    @pl.when(step < NEAR)
-    def _():
-        decays, signal = forward_bin(tau, point, direction, forward_y, forward_z, kept.at[slot])
-        backward_bin(tau, decays, signal, mask[...], kept.at[slot], point, backward_y, backward_z, order, total)
-
-    @pl.when((step >= NEAR) & (step < BINS - 1))
-    def _():
-        forward_bin(tau, point, direction, forward_y, forward_z, kept.at[slot])
-        store(step, slot).start()
-
-    @pl.when(step == BINS - 1)
-    def _():
-        forward_bin(tau, point, direction, forward_y, forward_z, last)
-        store(BINS - 2, BINS & 1).wait()
-
-
-def second_kernel(
-    mask, spectrum, last, point, taus, total_in, table_y, table_z, order,
-    mine, theirs,
-    total, sent, rest, kept, sems,
-):
-    step = pl.program_id(0)
+            done = []
+            for n in (first, first + 1):
+                tau = bin_time(n)
+                spectrum = kept.at[n & 1] if n < NEAR else spectra.at[n - NEAR]
+                done.append((n, tau, spectrum, forward_bin(tau, point, direction, forward_y, forward_z, spectrum)))
+            for n, tau, spectrum, terms in done:
+                if n < NEAR:
+                    backward_bin(tau, *terms, masks[n][...], spectrum, point, backward_y, backward_z, order, total)
+
+
+def second_kernel(mask, spectra, point, taus, total_in, table_y, table_z, order, mine, theirs, total, sent, rest):
     core = lax.axis_index("kz") & 1
-    slot = step & 1
-
-    def load(at):
-        return pltpu.make_async_copy(spectrum.at[at - 1], kept.at[at & 1], sems.at[at & 1])
-
-    @pl.when(step == 0)
-    def _():
-        total[...] = total_in[...]
-        kept[0] = last[...]
-
-    @pl.when(step < BINS - NEAR - 1)
-    def _():
-        load(step + 1).start()
-
-    @pl.when(step > 0)
-    def _():
-        load(step).wait()
-
-    tau = taus[0, 0:1, 0:1]
-    decays, signal = model_terms(tau, point)
-    backward_bin(tau, decays, signal, mask[0], kept.at[slot], point, table_y, table_z, order, total)
-
-    @pl.when(step == BINS - NEAR - 1)
-    def _():
-        pack_sums(core, total, sent, rest, mine, theirs)
+    total[...] = total_in[...]
+    for n in range(NEAR, BINS):
+        tau = taus[n, 0:1, 0:1]
+        terms = model_terms(tau, point)
+        backward_bin(tau, *terms, mask[n - NEAR], spectra.at[n - NEAR], point, table_y, table_z, order, total)
+    pack_sums(core, total, sent, rest, mine, theirs)
 
 
 def sums_kernel(received, direction, residual, applied_out, out_sums, applied, sems):
@@ -599,10 +559,6 @@
     return pl.BlockSpec(shape, lambda s: (0,) * len(shape))
 
 
-def stepping_block(shape):
-    return pl.BlockSpec((1,) + shape, lambda s: (s,) + (0,) * len(shape))
-
-
 def in_hbm(*values):
     return tuple(pltpu.with_memory_space_constraint(value, pltpu.HBM) for value in values)
 
@@ -705,12 +661,11 @@
     tables = (forward_y, forward_z, backward_y, backward_z, order)
     sums_shape = struct(64 * TILES, LANES)
     sent_scratch = pltpu.VMEM((2, 64 * TILES, LANES), f32)
-    spectrum, last, point, taus, total, *near_tables = pl.pallas_call(
+    spectra, point, taus, total, *near_tables = pl.pallas_call(
         first_kernel,
-        grid=(BINS,),
+        grid=(BINS // 2,),
         out_shape=(
-            far(BINS - NEAR - 1, 2, 2, NZ, NY),
-            near(2, 2, NZ, NY),
+            near(BINS - NEAR, 2, 2, NZ, NY),
             near(*planes),
             near(BINS, 8, LANES),
             near(*planes),
@@ -720,10 +675,9 @@
         + [constant_block((NZ, NY))] * NEAR
         + [HBM] * 5,
         out_specs=(
-            HBM,
-            constant_block((2, 2, NZ, NY)),
+            constant_block((BINS - NEAR, 2, 2, NZ, NY)),
             constant_block(planes),
-            stepping_block((8, LANES)),
+            constant_block((BINS, 8, LANES)),
             constant_block(planes),
             *[constant_block(table.shape) for table in tables[2:]],
         ),
@@ -733,42 +687,27 @@
             pltpu.VMEM(forward_y.shape, bf16),
             pltpu.VMEM(forward_z.shape, bf16),
             pltpu.VMEM((2, 2, 2, NZ, NY), f32),
-            pltpu.VMEM((NZ, NY), jnp.int32),
-            pltpu.SemaphoreType.DMA((7,)),
+            pltpu.SemaphoreType.DMA((5,)),
         ],
         compiler_params=params(),
         cost_estimate=cost(15),
         name="first",
     )(own, other, *masks, *in_hbm(*tables))
 
-    def bin_block(shape, first):
-        return pl.BlockSpec((1,) + shape, lambda s: (jnp.where(s == 0, BINS - 1, s + NEAR - 1) - first, 0, 0))
-
     mine, theirs = pl.pallas_call(
         second_kernel,
-        grid=(BINS - NEAR,),
         out_shape=(sums_shape, sums_shape),
-        in_specs=[
-            bin_block((NZ, NY), NEAR),
-            HBM,
-            constant_block((2, 2, NZ, NY)),
-            constant_block(planes),
-            bin_block((8, LANES), 0),
-            constant_block(planes),
-        ]
-        + [constant_block(table.shape) for table in tables[2:]],
-        out_specs=(constant_block((64 * TILES, LANES)),) * 2,
+        in_specs=[VMEM] * 8,
+        out_specs=(VMEM, VMEM),
         scratch_shapes=[
             pltpu.VMEM(planes, f32),
             sent_scratch,
             pltpu.VMEM((2, LANES, LANES), f32),
-            pltpu.VMEM((2, 2, 2, NZ, NY), f32),
-            pltpu.SemaphoreType.DMA((2,)),
         ],
         compiler_params=params(),
-        cost_estimate=cost(8),
+        cost_estimate=cost(4),
         name="second",
-    )(far_masks, *in_hbm(spectrum), *in_vmem(last, point, taus, total, *near_tables))
+    )(far_masks, *in_vmem(spectra, point, taus, total, *near_tables))
 
     received = by_parity(mine + core_swap(theirs))
     app_dense, sums = pl.pallas_call(

time: 101 us -> 98.8 us (0.978)
  Pallas kernels: 31.1 us -> 28.4 us
    pallas_call x2, Pallas kernels: 18.3 us -> 15.6 us  [the longest x1 12.3 us: shards(): pl.pallas_call(first_kernel, grid=(BINS // 2,), out_shape=(near(BINS - NE...]
  transfers between devices with their start and end apart: 9 -> 9, of which waited for: 4 -> 4; matrix products, arithmetic and copies ran while one was open for 0% -> 0% of each run, Pallas kernels for 23% -> 22%
where the time goes in v6:
time: 98.8 us; the launch traced here: 98.3 us
  Pallas kernels  28.4 us (29%)
  starting transfers between devices  25.6 us (26%)
  waiting for transfers between devices  25.1 us (25%)
  blocking collectives  17.3 us (18%)
    all_to_all x1, blocking collectives, by_parity(): lax.all_to_all(messages, AXES, 0, 0, axis_index_groups=groups)  17.3 us
    all_to_all x1, waiting for transfers between devices, by_parity(): lax.all_to_all(messages, AXES, 0, 0, axis_index_groups=groups)  14.2 us
    pallas_call x1, Pallas kernels, shards(): pl.pallas_call(first_kernel, grid=(BINS // 2,), out_shape=(near(BINS - NE...  12.3 us
    ppermute x5, starting transfers between devices, from_ti(): return lax.ppermute(values, 'ti', pairs)  7.88 us
    all_to_all x1, starting transfers between devices, by_parity(): lax.all_to_all(messages, AXES, 0, 0, axis_index_groups=groups)  7.86 us
    all_to_all x1, waiting for transfers between devices, shards(): lax.all_to_all(sums.reshape(128, 1, LANES), AXES, 0, 0).reshape(128, LANES)  7.19 us
    all_to_all x1, starting transfers between devices, shards(): lax.all_to_all(sums.reshape(128, 1, LANES), AXES, 0, 0).reshape(128, LANES)  5.41 us
    ppermute x2, starting transfers between devices, core_swap(): return lax.ppermute(values, 'kz', [(i, i ^ 1) for i in range(8)])  4.42 us
  transfers between devices with their start and end apart: 9, of which 4 were waited for; matrix products, arithmetic and copies ran while one was open for 0% of the time, Pallas kernels for 22%

profile of v6, /device:TPU:1, one launch (start us, length us, event | category | flops | bytes accessed | tf_op | source)
XLA Modules:
  0.0 98.3 jit_solution(578729247684355191)
XLA Ops:
  0.6 0.0 copy-start
  0.6 1.0 copy-done
  1.6 2.5 %collective-permute-start.3 = (s32[160,256]{1,0:T(8,128)S(1)}, s32[160,256]{1,0:T(8,128)S(1)}, u32[]{:S(2)}, u32[]{:S(2)}) collective-permute-start(s32[160,256]{1,0:T(8,128)S(1)} %dynamic-slice_bitcast_fusion.refs_2_), channel_id=1, source_target_pairs={{96,0},{104,8},{112,16},{120,24},{0,32},{8,40},{16,48},{24,56},{32... | collective-permute-start | bytes 491528 | tf_op jit(solution)/shard_map/ppermute | solution.py:650
  4.2 2.2 %collective-permute-start.2 = (s32[160,256]{1,0:T(8,128)S(1)}, s32[160,256]{1,0:T(8,128)S(1)}, u32[]{:S(2)}, u32[]{:S(2)}) collective-permute-start(s32[160,256]{1,0:T(8,128)S(1)} %dynamic-slice_bitcast_fusion.refs_2_), channel_id=1, source_target_pairs={{32,0},{40,8},{48,16},{56,24},{64,32},{72,40},{80,48},{88,56},{96,... | collective-permute-start | bytes 491528 | tf_op jit(solution)/shard_map/ppermute | solution.py:650
  6.4 1.2 %collective-permute-start.1 = (s32[160,256]{1,0:T(8,128)S(1)}, s32[160,256]{1,0:T(8,128)S(1)}, u32[]{:S(2)}, u32[]{:S(2)}) collective-permute-start(s32[160,256]{1,0:T(8,128)S(1)} %dynamic-slice_bitcast_fusion.refs_2_), channel_id=1, source_target_pairs={{24,0},{0,8},{8,16},{16,24},{56,32},{32,40},{40,48},{48,56},{88,64... | collective-permute-start | bytes 491528 | tf_op jit(solution)/shard_map/ppermute | solution.py:650
  7.6 1.5 %collective-permute-start = (s32[160,256]{1,0:T(8,128)S(1)}, s32[160,256]{1,0:T(8,128)S(1)}, u32[]{:S(2)}, u32[]{:S(2)}) collective-permute-start(s32[160,256]{1,0:T(8,128)S(1)} %dynamic-slice_bitcast_fusion.refs_2_), channel_id=1, source_target_pairs={{8,0},{16,8},{24,16},{0,24},{40,32},{48,40},{56,48},{32,56},{72,64... | collective-permute-start | bytes 491528 | tf_op jit(solution)/shard_map/ppermute | solution.py:650
  9.0 3.8 %pack.1 = (f32[2304,128]{1,0:T(8,128)}, f32[4,18,8,128]{3,2,1,0:T(8,128)S(1)}) custom-call(f32[2]{0:T(128)} %times.1, f32[3,8,16,20]{3,2,1,0:T(8,128)} %bitcast.34, f32[2,8,8,16,20]{4,3,2,1,0:T(8,128)} %bitcast.39, f32[3,20,8,256]{3,2,1,0:T(8,128)} %bitcast.45, f32[2,4,2,20,8,256]{5,4,3,2,1,0:T(8,128)} %bitcast.38), custom_call_target="tpu_custom_call" | custom-call | flops 1600000000 | bytes 8000000 | tf_op jit(solution)/shard_map/pack/pallas_call | solution.py:604
  12.9 7.9 %all-to-all-start = ((f32[64,1,4608]{2,1,0:T(1,128)}), f32[64,1,4608]{2,1,0:T(1,128)S(1)}, u32[]{:S(2)}, u32[]{:S(2)}) async-start(f32[64,1,4608]{2,1,0:T(1,128)} %bitcast.33), calls=%async_computation | async-start | bytes 2359296 | tf_op jit(solution)/shard_map/all_to_all | solution.py:585
  20.7 2.8 %dense.1.residual = f32[4,18,8,128]{3,2,1,0:T(8,128)S(1)} custom-call(f32[3,8,16,20]{3,2,1,0:T(8,128)} %bitcast.36, f32[2,8,8,16,20]{4,3,2,1,0:T(8,128)} %bitcast.41), custom_call_target="tpu_custom_call" | custom-call | flops 1200000000 | bytes 6000000 | tf_op jit(solution)/shard_map/dense/pallas_call | solution.py:629
  23.6 14.2 %all-to-all-done = f32[64,1,4608]{2,1,0:T(1,128)S(1)} async-done(((f32[64,1,4608]{2,1,0:T(1,128)}), f32[64,1,4608]{2,1,0:T(1,128)S(1)}, u32[]{:S(2)}, u32[]{:S(2)}) %all-to-all-start) | async-done | bytes 1179680 | tf_op jit(solution)/shard_map/all_to_all | solution.py:585
  37.8 4.0 %collective-permute-start.5 = (f32[2304,128]{1,0:T(8,128)S(1)}, f32[2304,128]{1,0:T(8,128)S(1)}, u32[]{:S(2)}, u32[]{:S(2)}) collective-permute-start(f32[2304,128]{1,0:T(8,128)S(1)} %bitcast.25), channel_id=1, source_target_pairs={{0,1},{1,0},{2,3},{3,2},{4,5},{5,4},{6,7},{7,6},{8,9},{9,8},{10,11... | collective-permute-start | bytes 3538952 | tf_op jit(solution)/shard_map/ppermute | solution.py:579
  41.8 0.5 collective-permute-start.4
  42.2 2.0 %collective-permute-done.5.refs_1_ = f32[2304,128]{1,0:T(8,128)S(1)} collective-permute-done((f32[2304,128]{1,0:T(8,128)S(1)}, f32[2304,128]{1,0:T(8,128)S(1)}, u32[]{:S(2)}, u32[]{:S(2)}) %collective-permute-start.5) | collective-permute-done | bytes 1179680 | tf_op jit(solution)/shard_map/ppermute | solution.py:579
  44.2 12.3 %first.1 = (f32[3,2,2,160,256]{4,3,2,1,0:T(8,128)S(1)}, f32[2,1120,128]{2,1,0:T(8,128)S(1)}, f32[8,8,128]{2,1,0:T(8,128)S(1)}, f32[2,1120,128]{2,1,0:T(8,128)S(1...) custom-call(f32[2304,128]{1,0:T(8,128)S(1)} %bitcast.26, ...), custom_call_target="tpu_custom_call" | custom-call | flops 6000000000 | bytes 30000000 | tf_op jit(solution)/shard_map/first/pallas_call | solution.py:664
  56.6 3.2 %second.1 = (f32[1152,128]{1,0:T(8,128)S(1)}, f32[1152,128]{1,0:T(8,128)S(1)}) custom-call(s32[3,160,256]{2,1,0:T(8,128)S(1)} %collective-permute-done.4.mask, f32[3,2,2,160,256]{4,3,2,1,0:T(8,128)S(1)} %get-tuple-element.46.spectra, f32[2,1120,128]{2,1,0:T(8,128)S(1)} %get-tuple-element.47.point, f32[8,8,128]{2,1,0:T(8,128)S(1)} %get-tuple-element.48.taus, ...), custom_call_target="tpu_custom_call" | custom-call | flops 1600000000 | bytes 8000000 | tf_op jit(solution)/shard_map/second/pallas_call | solution.py:697
  59.8 0.4 collective-permute-start.6
  60.3 1.6 %collective-permute-done.6 = f32[1152,128]{1,0:T(8,128)S(1)} collective-permute-done((f32[1152,128]{1,0:T(8,128)S(1)}, f32[1152,128]{1,0:T(8,128)S(1)}, u32[]{:S(2)}, u32[]{:S(2)}) %collective-permute-start.6) | collective-permute-done | bytes 589856 | tf_op jit(solution)/shard_map/ppermute | solution.py:579
  61.9 0.1 add.8
  62.0 17.3 %all_to_all.15 = f32[64,1,2304]{2,1,0:T(1,128)S(1)} all-to-all(f32[64,1,2304]{2,1,0:T(1,128)S(1)} %bitcast.32), channel_id=1, replica_groups={{0,2,4,6,8,10,12,14,16,18,20,22,24,26,28,30,32,34,36,38,40,42,44,46,48,..., dimensions={0} | all-to-all | bytes 1179648 | tf_op jit(solution)/shard_map/all_to_all | solution.py:585
  79.3 1.5 %sums.1 = (f32[18,4,8,128]{3,2,1,0:T(8,128)}, f32[128,128]{1,0:T(8,128)}) custom-call(f32[1152,128]{1,0:T(8,128)S(1)} %bitcast.27, f32[4,18,8,128]{3,2,1,0:T(8,128)S(1)} %get-tuple-element.36.direction, f32[4,18,8,128]{3,2,1,0:T(8,128)S(1)} %dense.1.residual), custom_call_target="tpu_custom_call" | custom-call | flops 400000000 | bytes 2000000 | tf_op jit(solution)/shard_map/sums/pallas_call | solution.py:713
  80.8 5.4 %all-to-all-start.2 = ((f32[128,1,128]{2,1,0:T(1,128)}), f32[128,1,128]{2,1,0:T(1,128)S(1)}, u32[]{:S(2)}, u32[]{:S(2)}) async-start(f32[128,1,128]{2,1,0:T(1,128)} %bitcast.16), calls=%async_computation.2 | async-start | bytes 131072 | tf_op jit(solution)/shard_map/all_to_all | solution.py:723
  86.2 2.5 %native.1 = (f32[3,8,16,20]{3,2,1,0:T(8,128)}, f32[48,8,16,20]{3,2,1,0:T(8,128)S(1)}) custom-call(f32[18,4,8,128]{3,2,1,0:T(8,128)} %get-tuple-element.57.dense_in, f32[2,8,8,16,20]{4,3,2,1,0:T(8,128)} %bitcast.40, f32[2,8,8,16,20]{4,3,2,1,0:T(8,128)} %bitcast.42), custom_call_target="tpu_custom_call" | custom-call | flops 1200000000 | bytes 6000000 | tf_op jit(solution)/shard_map/native/pallas_call | solution.py:726
  88.7 7.2 %all-to-all-done.2 = f32[128,1,128]{2,1,0:T(1,128)S(1)} async-done(((f32[128,1,128]{2,1,0:T(1,128)}), f32[128,1,128]{2,1,0:T(1,128)S(1)}, u32[]{:S(2)}, u32[]{:S(2)}) %all-to-all-start.2) | async-done | bytes 65568 | tf_op jit(solution)/shard_map/all_to_all | solution.py:723
  95.9 2.3 %step.1 = (f32[3,8,16,20]{3,2,1,0:T(8,128)}, f32[2,8,8,16,20]{4,3,2,1,0:T(8,128)}, f32[3,8,16,20]{3,2,1,0:T(8,128)}, f32[2,8,8,16,20]{4,3,2,1,0:T(8,128)}) custom-call(f32[128,128]{1,0:T(8,128)S(1)} %bitcast.28, f32[48,8,16,20]{3,2,1,0:T(8,128)S(1)} %get-tuple-element.58.fields, f32[3,8,16,20]{3,2,1,0:T(8,128)} %get-tuple-element.59.app_maps, ...), custom_call_target="tpu_custom_call" | custom-call | flops 800000000 | bytes 4000000 | tf_op jit(solution)/shard_map/step/pallas_call | solution.py:743
  (7 shorter events, 0.1 us)
Async XLA Ops:
  0.6 1.0 copy-start
  1.6 11.2 %collective-permute-start.3 = (s32[160,256]{1,0:T(8,128)S(1)}, s32[160,256]{1,0:T(8,128)S(1)}, u32[]{:S(2)}, u32[]{:S(2)}) collective-permute-start(s32[160,256]{1,0:T(8,128)S(1)} %dynamic-slice_bitcast_fusion.refs_2_), channel_id=1, source_target_pairs={{96,0},{104,8},{112,16},{120,24},{0,32},{8,40},{16,48},{24,56},{32... | collective-permute-start | bytes 491528 | tf_op jit(solution)/shard_map/ppermute | solution.py:650
  4.2 8.7 %collective-permute-start.2 = (s32[160,256]{1,0:T(8,128)S(1)}, s32[160,256]{1,0:T(8,128)S(1)}, u32[]{:S(2)}, u32[]{:S(2)}) collective-permute-start(s32[160,256]{1,0:T(8,128)S(1)} %dynamic-slice_bitcast_fusion.refs_2_), channel_id=1, source_target_pairs={{32,0},{40,8},{48,16},{56,24},{64,32},{72,40},{80,48},{88,56},{96,... | collective-permute-start | bytes 491528 | tf_op jit(solution)/shard_map/ppermute | solution.py:650
  6.4 6.5 %collective-permute-start.1 = (s32[160,256]{1,0:T(8,128)S(1)}, s32[160,256]{1,0:T(8,128)S(1)}, u32[]{:S(2)}, u32[]{:S(2)}) collective-permute-start(s32[160,256]{1,0:T(8,128)S(1)} %dynamic-slice_bitcast_fusion.refs_2_), channel_id=1, source_target_pairs={{24,0},{0,8},{8,16},{16,24},{56,32},{32,40},{40,48},{48,56},{88,64... | collective-permute-start | bytes 491528 | tf_op jit(solution)/shard_map/ppermute | solution.py:650
  7.6 5.3 %collective-permute-start = (s32[160,256]{1,0:T(8,128)S(1)}, s32[160,256]{1,0:T(8,128)S(1)}, u32[]{:S(2)}, u32[]{:S(2)}) collective-permute-start(s32[160,256]{1,0:T(8,128)S(1)} %dynamic-slice_bitcast_fusion.refs_2_), channel_id=1, source_target_pairs={{8,0},{16,8},{24,16},{0,24},{40,32},{48,40},{56,48},{32,56},{72,64... | collective-permute-start | bytes 491528 | tf_op jit(solution)/shard_map/ppermute | solution.py:650
  12.9 24.9 %all-to-all-start = ((f32[64,1,4608]{2,1,0:T(1,128)}), f32[64,1,4608]{2,1,0:T(1,128)S(1)}, u32[]{:S(2)}, u32[]{:S(2)}) async-start(f32[64,1,4608]{2,1,0:T(1,128)} %bitcast.33), calls=%async_computation | async-start | bytes 2359296 | tf_op jit(solution)/shard_map/all_to_all | solution.py:585
  37.8 6.5 %collective-permute-start.5 = (f32[2304,128]{1,0:T(8,128)S(1)}, f32[2304,128]{1,0:T(8,128)S(1)}, u32[]{:S(2)}, u32[]{:S(2)}) collective-permute-start(f32[2304,128]{1,0:T(8,128)S(1)} %bitcast.25), channel_id=1, source_target_pairs={{0,1},{1,0},{2,3},{3,2},{4,5},{5,4},{6,7},{7,6},{8,9},{9,8},{10,11... | collective-permute-start | bytes 3538952 | tf_op jit(solution)/shard_map/ppermute | solution.py:579
  41.8 14.8 %collective-permute-start.4 = (s32[3,160,256]{2,1,0:T(8,128)S(1)}, s32[3,160,256]{2,1,0:T(8,128)S(1)}, u32[]{:S(2)}, u32[]{:S(2)}) collective-permute-start(s32[3,160,256]{2,1,0:T(8,128)S(1)} %pad_add_fusion), channel_id=1, source_target_pairs={{32,0},{40,8},{48,16},{56,24},{64,32},{72,40},{80,48},{88,56},{96,... | collective-permute-start | bytes 1474568 | tf_op jit(solution)/shard_map/ppermute | solution.py:650
  59.8 2.1 %collective-permute-start.6 = (f32[1152,128]{1,0:T(8,128)S(1)}, f32[1152,128]{1,0:T(8,128)S(1)}, u32[]{:S(2)}, u32[]{:S(2)}) collective-permute-start(f32[1152,128]{1,0:T(8,128)S(1)} %get-tuple-element.54), channel_id=1, source_target_pairs={{0,1},{1,0},{2,3},{3,2},{4,5},{5,4},{6,7},{7,6},{8,9},{9,8},{10,11... | collective-permute-start | bytes 1769480 | tf_op jit(solution)/shard_map/ppermute | solution.py:579
  80.8 15.1 %all-to-all-start.2 = ((f32[128,1,128]{2,1,0:T(1,128)}), f32[128,1,128]{2,1,0:T(1,128)S(1)}, u32[]{:S(2)}, u32[]{:S(2)}) async-start(f32[128,1,128]{2,1,0:T(1,128)} %bitcast.16), calls=%async_computation.2 | async-start | bytes 131072 | tf_op jit(solution)/shard_map/all_to_all | solution.py:723

commit v7 on v6

--- a/solution.py
+++ b/solution.py
@@ -368,26 +368,28 @@
     theirs[...] = sent[1]
 
 
+def tables_kernel(after, *refs):
+    del after
+    sources, targets, sems = refs[:5], refs[5:10], refs[10]
+    copies = [pltpu.make_async_copy(a, b, sems.at[i]) for i, (a, b) in enumerate(zip(sources, targets))]
+    for copy in copies:
+        copy.start()
+    for copy in copies:
+        copy.wait()
+
+
 def first_kernel(*refs):
     own, other, *masks = refs[: 2 + NEAR]
-    tables_in, refs = refs[2 + NEAR : 7 + NEAR], refs[7 + NEAR :]
-    spectra, point, taus, total, backward_y, backward_z, order = refs[:7]
-    direction, rest, forward_y, forward_z, kept, sems = refs[7:]
+    forward_y, forward_z, backward_y, backward_z, order = refs[2 + NEAR : 7 + NEAR]
+    spectra, point, taus, total, direction, rest, kept = refs[7 + NEAR :]
     step = pl.program_id(0)
     t, core = lax.axis_index("ti"), lax.axis_index("kz") & 1
 
-    @pl.when(step == 0)
-    def _():
-        tables = (forward_y, forward_z, backward_y, backward_z, order)
-        copies = [pltpu.make_async_copy(a, b, sems.at[i]) for i, (a, b) in enumerate(zip(tables_in, tables))]
-        for copy in copies:
-            copy.start()
+    def prepare():
         total[...] = jnp.zeros_like(total)
         unpack(own, core, point, direction, rest)
         unpack(other, 1 - core, point, direction, rest)
         unpack_rest(direction, rest)
-        for copy in copies:
-            copy.wait()
 
     def bin_time(n):
         along_z, along_x = STEPS[n]
@@ -402,6 +404,8 @@
 
         @pl.when(step == first // 2)
         def _():
+            if first == 0:
+                prepare()
             done = []
             for n in (first, first + 1):
                 tau = bin_time(n)
@@ -661,7 +665,19 @@
     tables = (forward_y, forward_z, backward_y, backward_z, order)
     sums_shape = struct(64 * TILES, LANES)
     sent_scratch = pltpu.VMEM((2, 64 * TILES, LANES), f32)
-    spectra, point, taus, total, *near_tables = pl.pallas_call(
+    near_tables = in_vmem(
+        *pl.pallas_call(
+            tables_kernel,
+            out_shape=[pltpu.VMEM(table.shape, bf16) for table in tables],
+            in_specs=[pl.BlockSpec(memory_space=pl.ANY)] + [HBM] * 5,
+            out_specs=[VMEM] * 5,
+            scratch_shapes=[pltpu.SemaphoreType.DMA((5,))],
+            compiler_params=params(),
+            cost_estimate=cost(2),
+            name="tables",
+        )(own, *in_hbm(*tables))
+    )
+    spectra, point, taus, total = pl.pallas_call(
         first_kernel,
         grid=(BINS // 2,),
         out_shape=(
@@ -669,30 +685,25 @@
             near(*planes),
             near(BINS, 8, LANES),
             near(*planes),
-            *[pltpu.VMEM(table.shape, bf16) for table in tables[2:]],
         ),
         in_specs=[constant_block(own.shape)] * 2
         + [constant_block((NZ, NY))] * NEAR
-        + [HBM] * 5,
+        + [VMEM] * 5,
         out_specs=(
             constant_block((BINS - NEAR, 2, 2, NZ, NY)),
             constant_block(planes),
             constant_block((BINS, 8, LANES)),
             constant_block(planes),
-            *[constant_block(table.shape) for table in tables[2:]],
         ),
         scratch_shapes=[
             pltpu.VMEM(planes, f32),
             pltpu.VMEM((2, LANES, LANES), f32),
-            pltpu.VMEM(forward_y.shape, bf16),
-            pltpu.VMEM(forward_z.shape, bf16),
             pltpu.VMEM((2, 2, 2, NZ, NY), f32),
-            pltpu.SemaphoreType.DMA((5,)),
         ],
         compiler_params=params(),
         cost_estimate=cost(15),
         name="first",
-    )(own, other, *masks, *in_hbm(*tables))
+    )(own, other, *masks, *near_tables)
 
     mine, theirs = pl.pallas_call(
         second_kernel,
@@ -707,7 +718,7 @@
         compiler_params=params(),
         cost_estimate=cost(4),
         name="second",
-    )(far_masks, *in_vmem(spectra, point, taus, total, *near_tables))
+    )(far_masks, *in_vmem(spectra, point, taus, total), *near_tables[2:])
 
     received = by_parity(mine + core_swap(theirs))
     app_dense, sums = pl.pallas_call(

time: 98.8 us -> 98.2 us (level)
  waiting for transfers between devices: 25.1 us -> 23.4 us
  blocking collectives: 17.3 us -> 18.3 us
    ppermute x2, waiting for transfers between devices: 3.65 us -> 2.01 us  [core_swap(): return lax.ppermute(values, 'kz', [(i, i ^ 1) for i in range(8)])]
    pallas_call x0 -> x1, Pallas kernels: none -> 1.62 us  [shards(): pl.pallas_call(tables_kernel, out_shape=[pltpu.VMEM(table.shape, bf16) fo...]
    pallas_call x1, Pallas kernels: 12.3 us -> 10.8 us  [shards(): pl.pallas_call(first_kernel, grid=(BINS // 2,), out_shape=(near(BINS - NE...]
where the time goes in v7:
time: 98.2 us; the launch traced here: 97.7 us
  Pallas kernels  28.4 us (29%)
  starting transfers between devices  25.6 us (26%)
  waiting for transfers between devices  23.4 us (24%)
  blocking collectives  18.3 us (19%)
    all_to_all x1, blocking collectives, by_parity(): lax.all_to_all(messages, AXES, 0, 0, axis_index_groups=groups)  18.3 us
    all_to_all x1, waiting for transfers between devices, by_parity(): lax.all_to_all(messages, AXES, 0, 0, axis_index_groups=groups)  14.2 us
    pallas_call x1, Pallas kernels, shards(): pl.pallas_call(first_kernel, grid=(BINS // 2,), out_shape=(near(BINS - NE...  10.8 us
    ppermute x5, starting transfers between devices, from_ti(): return lax.ppermute(values, 'ti', pairs)  7.88 us
    all_to_all x1, starting transfers between devices, by_parity(): lax.all_to_all(messages, AXES, 0, 0, axis_index_groups=groups)  7.85 us
    all_to_all x1, waiting for transfers between devices, shards(): lax.all_to_all(sums.reshape(128, 1, LANES), AXES, 0, 0).reshape(128, LANES)  7.19 us
    all_to_all x1, starting transfers between devices, shards(): lax.all_to_all(sums.reshape(128, 1, LANES), AXES, 0, 0).reshape(128, LANES)  5.41 us
    ppermute x2, starting transfers between devices, core_swap(): return lax.ppermute(values, 'kz', [(i, i ^ 1) for i in range(8)])  4.44 us
  transfers between devices with their start and end apart: 9, of which 4 were waited for; matrix products, arithmetic and copies ran while one was open for 0% of the time, Pallas kernels for 22%

profile of v7, /device:TPU:1, one launch (start us, length us, event | category | flops | bytes accessed | tf_op | source)
XLA Modules:
  0.0 97.7 jit_solution(1431898178875539154)
XLA Ops:
  0.6 1.0 copy-done
  1.6 2.5 %collective-permute-start.3 = (s32[160,256]{1,0:T(8,128)S(1)}, s32[160,256]{1,0:T(8,128)S(1)}, u32[]{:S(2)}, u32[]{:S(2)}) collective-permute-start(s32[160,256]{1,0:T(8,128)S(1)} %dynamic-slice_bitcast_fusion.refs_2_), channel_id=1, source_target_pairs={{96,0},{104,8},{112,16},{120,24},{0,32},{8,40},{16,48},{24,56},{32... | collective-permute-start | bytes 491528 | tf_op jit(solution)/shard_map/ppermute | solution.py:654
  4.2 2.2 %collective-permute-start.2 = (s32[160,256]{1,0:T(8,128)S(1)}, s32[160,256]{1,0:T(8,128)S(1)}, u32[]{:S(2)}, u32[]{:S(2)}) collective-permute-start(s32[160,256]{1,0:T(8,128)S(1)} %dynamic-slice_bitcast_fusion.refs_2_), channel_id=1, source_target_pairs={{32,0},{40,8},{48,16},{56,24},{64,32},{72,40},{80,48},{88,56},{96,... | collective-permute-start | bytes 491528 | tf_op jit(solution)/shard_map/ppermute | solution.py:654
  6.4 1.2 %collective-permute-start.1 = (s32[160,256]{1,0:T(8,128)S(1)}, s32[160,256]{1,0:T(8,128)S(1)}, u32[]{:S(2)}, u32[]{:S(2)}) collective-permute-start(s32[160,256]{1,0:T(8,128)S(1)} %dynamic-slice_bitcast_fusion.refs_2_), channel_id=1, source_target_pairs={{24,0},{0,8},{8,16},{16,24},{56,32},{32,40},{40,48},{48,56},{88,64... | collective-permute-start | bytes 491528 | tf_op jit(solution)/shard_map/ppermute | solution.py:654
  7.6 1.5 %collective-permute-start = (s32[160,256]{1,0:T(8,128)S(1)}, s32[160,256]{1,0:T(8,128)S(1)}, u32[]{:S(2)}, u32[]{:S(2)}) collective-permute-start(s32[160,256]{1,0:T(8,128)S(1)} %dynamic-slice_bitcast_fusion.refs_2_), channel_id=1, source_target_pairs={{8,0},{16,8},{24,16},{0,24},{40,32},{48,40},{56,48},{32,56},{72,64... | collective-permute-start | bytes 491528 | tf_op jit(solution)/shard_map/ppermute | solution.py:654
  9.0 3.8 %pack.1 = (f32[2304,128]{1,0:T(8,128)}, f32[4,18,8,128]{3,2,1,0:T(8,128)S(1)}) custom-call(f32[2]{0:T(128)} %times.1, f32[3,8,16,20]{3,2,1,0:T(8,128)} %bitcast.35, f32[2,8,8,16,20]{4,3,2,1,0:T(8,128)} %bitcast.40, f32[3,20,8,256]{3,2,1,0:T(8,128)} %bitcast.46, f32[2,4,2,20,8,256]{5,4,3,2,1,0:T(8,128)} %bitcast.39), custom_call_target="tpu_custom_call" | custom-call | flops 1600000000 | bytes 8000000 | tf_op jit(solution)/shard_map/pack/pallas_call | solution.py:608
  12.9 7.9 %all-to-all-start = ((f32[64,1,4608]{2,1,0:T(1,128)}), f32[64,1,4608]{2,1,0:T(1,128)S(1)}, u32[]{:S(2)}, u32[]{:S(2)}) async-start(f32[64,1,4608]{2,1,0:T(1,128)} %bitcast.34), calls=%async_computation | async-start | bytes 2359296 | tf_op jit(solution)/shard_map/all_to_all | solution.py:589
  20.7 2.8 %dense.1.residual = f32[4,18,8,128]{3,2,1,0:T(8,128)S(1)} custom-call(f32[3,8,16,20]{3,2,1,0:T(8,128)} %bitcast.37, f32[2,8,8,16,20]{4,3,2,1,0:T(8,128)} %bitcast.42), custom_call_target="tpu_custom_call" | custom-call | flops 1200000000 | bytes 6000000 | tf_op jit(solution)/shard_map/dense/pallas_call | solution.py:633
  23.6 14.2 %all-to-all-done = f32[64,1,4608]{2,1,0:T(1,128)S(1)} async-done(((f32[64,1,4608]{2,1,0:T(1,128)}), f32[64,1,4608]{2,1,0:T(1,128)S(1)}, u32[]{:S(2)}, u32[]{:S(2)}) %all-to-all-start) | async-done | bytes 1179680 | tf_op jit(solution)/shard_map/all_to_all | solution.py:589
  37.8 4.0 %collective-permute-start.5 = (f32[2304,128]{1,0:T(8,128)S(1)}, f32[2304,128]{1,0:T(8,128)S(1)}, u32[]{:S(2)}, u32[]{:S(2)}) collective-permute-start(f32[2304,128]{1,0:T(8,128)S(1)} %bitcast.25), channel_id=1, source_target_pairs={{0,1},{1,0},{2,3},{3,2},{4,5},{5,4},{6,7},{7,6},{8,9},{9,8},{10,11... | collective-permute-start | bytes 3538952 | tf_op jit(solution)/shard_map/ppermute | solution.py:583
  41.8 0.5 collective-permute-start.4
  42.2 1.6 %tables.1 = (bf16[2,768,256]{2,1,0:T(8,128)(2,1)S(1)}, bf16[2,160,512]{2,1,0:T(8,128)(2,1)S(1)}, bf16[2,768,256]{2,1,0:T(8,128)(2,1)S(1)}, bf16[2,160,512]{2,1,0:T(8,128)(2,1)S(1)}, bf16[256,256]{1,0:T(8,128)(2,1)S(1)}) custom-call(f32[2304,128]{1,0:T(8,128)S(1)} %bitcast.26, bf16[2,768,256]{2,1,0:T(8,128)(2,1)} %constant.22.clone.refs_0_, ...), custom_call_target="tpu_custom_call" | custom-call | flops 800000000 | bytes 4000000 | tf_op jit(solution)/shard_map/tables/pallas_call | solution.py:669
  43.9 0.4 collective-permute-done.5.refs_1_
  44.2 10.8 %first.1 = (f32[3,2,2,160,256]{4,3,2,1,0:T(8,128)S(1)}, f32[2,1120,128]{2,1,0:T(8,128)S(1)}, f32[8,8,128]{2,1,0:T(8,128)S(1)}, f32[2,1120,128]{2,1,0:T(8,128)S(1)}) custom-call(f32[2304,128]{1,0:T(8,128)S(1)} %bitcast.27, f32[2304,128]{1,0:T(8,128)S(1)} %collective-permute-done.5.refs_1_, s32[160,256]{1,0:T(8,128)S(1)} %dynamic-slice_bitcast_fusion.refs_2_, ...), custom_call_target="tpu_custom_call" | custom-call | flops 6000000000 | bytes 30000000 | tf_op jit(solution)/shard_map/first/pallas_call | solution.py:680
  55.0 3.2 %second.1 = (f32[1152,128]{1,0:T(8,128)S(1)}, f32[1152,128]{1,0:T(8,128)S(1)}) custom-call(s32[3,160,256]{2,1,0:T(8,128)S(1)} %collective-permute-done.4.mask, f32[3,2,2,160,256]{4,3,2,1,0:T(8,128)S(1)} %get-tuple-element.53.spectra, f32[2,1120,128]{2,1,0:T(8,128)S(1)} %get-tuple-element.54.point, f32[8,8,128]{2,1,0:T(8,128)S(1)} %get-tuple-element.55.taus, ...), custom_call_target="tpu_custom_call" | custom-call | flops 1600000000 | bytes 8000000 | tf_op jit(solution)/shard_map/second/pallas_call | solution.py:708
  58.3 0.5 collective-permute-start.6
  58.7 1.6 %collective-permute-done.6 = f32[1152,128]{1,0:T(8,128)S(1)} collective-permute-done((f32[1152,128]{1,0:T(8,128)S(1)}, f32[1152,128]{1,0:T(8,128)S(1)}, u32[]{:S(2)}, u32[]{:S(2)}) %collective-permute-start.6) | collective-permute-done | bytes 589856 | tf_op jit(solution)/shard_map/ppermute | solution.py:583
  60.4 0.1 add.8
  60.4 18.3 %all_to_all.15 = f32[64,1,2304]{2,1,0:T(1,128)S(1)} all-to-all(f32[64,1,2304]{2,1,0:T(1,128)S(1)} %bitcast.33), channel_id=1, replica_groups={{0,2,4,6,8,10,12,14,16,18,20,22,24,26,28,30,32,34,36,38,40,42,44,46,48,..., dimensions={0} | all-to-all | bytes 1179648 | tf_op jit(solution)/shard_map/all_to_all | solution.py:589
  78.7 1.5 %sums.1 = (f32[18,4,8,128]{3,2,1,0:T(8,128)}, f32[128,128]{1,0:T(8,128)}) custom-call(f32[1152,128]{1,0:T(8,128)S(1)} %bitcast.28, f32[4,18,8,128]{3,2,1,0:T(8,128)S(1)} %get-tuple-element.38.direction, f32[4,18,8,128]{3,2,1,0:T(8,128)S(1)} %dense.1.residual), custom_call_target="tpu_custom_call" | custom-call | flops 400000000 | bytes 2000000 | tf_op jit(solution)/shard_map/sums/pallas_call | solution.py:724
  80.2 5.4 %all-to-all-start.2 = ((f32[128,1,128]{2,1,0:T(1,128)}), f32[128,1,128]{2,1,0:T(1,128)S(1)}, u32[]{:S(2)}, u32[]{:S(2)}) async-start(f32[128,1,128]{2,1,0:T(1,128)} %bitcast.16), calls=%async_computation.2 | async-start | bytes 131072 | tf_op jit(solution)/shard_map/all_to_all | solution.py:734
  85.6 2.5 %native.1 = (f32[3,8,16,20]{3,2,1,0:T(8,128)}, f32[48,8,16,20]{3,2,1,0:T(8,128)S(1)}) custom-call(f32[18,4,8,128]{3,2,1,0:T(8,128)} %get-tuple-element.61.dense_in, f32[2,8,8,16,20]{4,3,2,1,0:T(8,128)} %bitcast.41, f32[2,8,8,16,20]{4,3,2,1,0:T(8,128)} %bitcast.43), custom_call_target="tpu_custom_call" | custom-call | flops 1200000000 | bytes 6000000 | tf_op jit(solution)/shard_map/native/pallas_call | solution.py:737
  88.1 7.2 %all-to-all-done.2 = f32[128,1,128]{2,1,0:T(1,128)S(1)} async-done(((f32[128,1,128]{2,1,0:T(1,128)}), f32[128,1,128]{2,1,0:T(1,128)S(1)}, u32[]{:S(2)}, u32[]{:S(2)}) %all-to-all-start.2) | async-done | bytes 65568 | tf_op jit(solution)/shard_map/all_to_all | solution.py:734
  95.3 2.3 %step.1 = (f32[3,8,16,20]{3,2,1,0:T(8,128)}, f32[2,8,8,16,20]{4,3,2,1,0:T(8,128)}, f32[3,8,16,20]{3,2,1,0:T(8,128)}, f32[2,8,8,16,20]{4,3,2,1,0:T(8,128)}) custom-call(f32[128,128]{1,0:T(8,128)S(1)} %bitcast.29, f32[48,8,16,20]{3,2,1,0:T(8,128)S(1)} %get-tuple-element.62.fields, f32[3,8,16,20]{3,2,1,0:T(8,128)} %get-tuple-element.63.app_maps, ...), custom_call_target="tpu_custom_call" | custom-call | flops 800000000 | bytes 4000000 | tf_op jit(solution)/shard_map/step/pallas_call | solution.py:754
  (8 shorter events, 0.1 us)
Async XLA Ops:
  0.6 1.0 %copy-start = (s32[2,160,256]{2,1,0:T(8,128)S(1)}, s32[2,160,256]{2,1,0:T(8,128)}, u32[]{:S(2)}) copy-start(s32[2,160,256]{2,1,0:T(8,128)} %param.20) | copy-start | bytes 983044
  1.6 11.2 %collective-permute-start.3 = (s32[160,256]{1,0:T(8,128)S(1)}, s32[160,256]{1,0:T(8,128)S(1)}, u32[]{:S(2)}, u32[]{:S(2)}) collective-permute-start(s32[160,256]{1,0:T(8,128)S(1)} %dynamic-slice_bitcast_fusion.refs_2_), channel_id=1, source_target_pairs={{96,0},{104,8},{112,16},{120,24},{0,32},{8,40},{16,48},{24,56},{32... | collective-permute-start | bytes 491528 | tf_op jit(solution)/shard_map/ppermute | solution.py:654
  4.2 8.7 %collective-permute-start.2 = (s32[160,256]{1,0:T(8,128)S(1)}, s32[160,256]{1,0:T(8,128)S(1)}, u32[]{:S(2)}, u32[]{:S(2)}) collective-permute-start(s32[160,256]{1,0:T(8,128)S(1)} %dynamic-slice_bitcast_fusion.refs_2_), channel_id=1, source_target_pairs={{32,0},{40,8},{48,16},{56,24},{64,32},{72,40},{80,48},{88,56},{96,... | collective-permute-start | bytes 491528 | tf_op jit(solution)/shard_map/ppermute | solution.py:654
  6.4 6.5 %collective-permute-start.1 = (s32[160,256]{1,0:T(8,128)S(1)}, s32[160,256]{1,0:T(8,128)S(1)}, u32[]{:S(2)}, u32[]{:S(2)}) collective-permute-start(s32[160,256]{1,0:T(8,128)S(1)} %dynamic-slice_bitcast_fusion.refs_2_), channel_id=1, source_target_pairs={{24,0},{0,8},{8,16},{16,24},{56,32},{32,40},{40,48},{48,56},{88,64... | collective-permute-start | bytes 491528 | tf_op jit(solution)/shard_map/ppermute | solution.py:654
  7.6 5.3 %collective-permute-start = (s32[160,256]{1,0:T(8,128)S(1)}, s32[160,256]{1,0:T(8,128)S(1)}, u32[]{:S(2)}, u32[]{:S(2)}) collective-permute-start(s32[160,256]{1,0:T(8,128)S(1)} %dynamic-slice_bitcast_fusion.refs_2_), channel_id=1, source_target_pairs={{8,0},{16,8},{24,16},{0,24},{40,32},{48,40},{56,48},{32,56},{72,64... | collective-permute-start | bytes 491528 | tf_op jit(solution)/shard_map/ppermute | solution.py:654
  12.9 24.9 %all-to-all-start = ((f32[64,1,4608]{2,1,0:T(1,128)}), f32[64,1,4608]{2,1,0:T(1,128)S(1)}, u32[]{:S(2)}, u32[]{:S(2)}) async-start(f32[64,1,4608]{2,1,0:T(1,128)} %bitcast.34), calls=%async_computation | async-start | bytes 2359296 | tf_op jit(solution)/shard_map/all_to_all | solution.py:589
  37.8 6.5 %collective-permute-start.5 = (f32[2304,128]{1,0:T(8,128)S(1)}, f32[2304,128]{1,0:T(8,128)S(1)}, u32[]{:S(2)}, u32[]{:S(2)}) collective-permute-start(f32[2304,128]{1,0:T(8,128)S(1)} %bitcast.25), channel_id=1, source_target_pairs={{0,1},{1,0},{2,3},{3,2},{4,5},{5,4},{6,7},{7,6},{8,9},{9,8},{10,11... | collective-permute-start | bytes 3538952 | tf_op jit(solution)/shard_map/ppermute | solution.py:583
  41.8 13.3 %collective-permute-start.4 = (s32[3,160,256]{2,1,0:T(8,128)S(1)}, s32[3,160,256]{2,1,0:T(8,128)S(1)}, u32[]{:S(2)}, u32[]{:S(2)}) collective-permute-start(s32[3,160,256]{2,1,0:T(8,128)S(1)} %pad_add_fusion), channel_id=1, source_target_pairs={{32,0},{40,8},{48,16},{56,24},{64,32},{72,40},{80,48},{88,56},{96,... | collective-permute-start | bytes 1474568 | tf_op jit(solution)/shard_map/ppermute | solution.py:654
  58.3 2.1 %collective-permute-start.6 = (f32[1152,128]{1,0:T(8,128)S(1)}, f32[1152,128]{1,0:T(8,128)S(1)}, u32[]{:S(2)}, u32[]{:S(2)}) collective-permute-start(f32[1152,128]{1,0:T(8,128)S(1)} %get-tuple-element.58), channel_id=1, source_target_pairs={{0,1},{1,0},{2,3},{3,2},{4,5},{5,4},{6,7},{7,6},{8,9},{9,8},{10,11... | collective-permute-start | bytes 1769480 | tf_op jit(solution)/shard_map/ppermute | solution.py:583
  80.2 15.1 %all-to-all-start.2 = ((f32[128,1,128]{2,1,0:T(1,128)}), f32[128,1,128]{2,1,0:T(1,128)S(1)}, u32[]{:S(2)}, u32[]{:S(2)}) async-start(f32[128,1,128]{2,1,0:T(1,128)} %bitcast.16), calls=%async_computation.2 | async-start | bytes 131072 | tf_op jit(solution)/shard_map/all_to_all | solution.py:734

commit v8 on v7

--- a/solution.py
+++ b/solution.py
@@ -370,7 +370,7 @@
 
 def tables_kernel(after, *refs):
     del after
-    sources, targets, sems = refs[:5], refs[5:10], refs[10]
+    sources, targets, sems = refs[:2], refs[2:4], refs[4]
     copies = [pltpu.make_async_copy(a, b, sems.at[i]) for i, (a, b) in enumerate(zip(sources, targets))]
     for copy in copies:
         copy.start()
@@ -380,12 +380,16 @@
 
 def first_kernel(*refs):
     own, other, *masks = refs[: 2 + NEAR]
-    forward_y, forward_z, backward_y, backward_z, order = refs[2 + NEAR : 7 + NEAR]
-    spectra, point, taus, total, direction, rest, kept = refs[7 + NEAR :]
+    forward_y, forward_z, *tables_in = refs[2 + NEAR : 7 + NEAR]
+    spectra, point, taus, total, *tables, direction, rest, kept, sems = refs[7 + NEAR :]
+    backward_y, backward_z, order = tables
+    copies = [pltpu.make_async_copy(a, b, sems.at[i]) for i, (a, b) in enumerate(zip(tables_in, tables))]
     step = pl.program_id(0)
     t, core = lax.axis_index("ti"), lax.axis_index("kz") & 1
 
     def prepare():
+        for copy in copies:
+            copy.start()
         total[...] = jnp.zeros_like(total)
         unpack(own, core, point, direction, rest)
         unpack(other, 1 - core, point, direction, rest)
@@ -411,6 +415,9 @@
                 tau = bin_time(n)
                 spectrum = kept.at[n & 1] if n < NEAR else spectra.at[n - NEAR]
                 done.append((n, tau, spectrum, forward_bin(tau, point, direction, forward_y, forward_z, spectrum)))
+            if first == 0:
+                for copy in copies:
+                    copy.wait()
             for n, tau, spectrum, terms in done:
                 if n < NEAR:
                     backward_bin(tau, *terms, masks[n][...], spectrum, point, backward_y, backward_z, order, total)
@@ -668,16 +675,16 @@
     near_tables = in_vmem(
         *pl.pallas_call(
             tables_kernel,
-            out_shape=[pltpu.VMEM(table.shape, bf16) for table in tables],
-            in_specs=[pl.BlockSpec(memory_space=pl.ANY)] + [HBM] * 5,
-            out_specs=[VMEM] * 5,
-            scratch_shapes=[pltpu.SemaphoreType.DMA((5,))],
+            out_shape=[pltpu.VMEM(table.shape, bf16) for table in tables[:2]],
+            in_specs=[pl.BlockSpec(memory_space=pl.ANY)] + [HBM] * 2,
+            out_specs=[VMEM] * 2,
+            scratch_shapes=[pltpu.SemaphoreType.DMA((2,))],
             compiler_params=params(),
-            cost_estimate=cost(2),
+            cost_estimate=cost(1),
             name="tables",
-        )(own, *in_hbm(*tables))
+        )(own, *in_hbm(*tables[:2]))
     )
-    spectra, point, taus, total = pl.pallas_call(
+    spectra, point, taus, total, *back_tables = pl.pallas_call(
         first_kernel,
         grid=(BINS // 2,),
         out_shape=(
@@ -685,25 +692,29 @@
             near(*planes),
             near(BINS, 8, LANES),
             near(*planes),
+            *[pltpu.VMEM(table.shape, bf16) for table in tables[2:]],
         ),
         in_specs=[constant_block(own.shape)] * 2
         + [constant_block((NZ, NY))] * NEAR
-        + [VMEM] * 5,
+        + [VMEM] * 2
+        + [HBM] * 3,
         out_specs=(
             constant_block((BINS - NEAR, 2, 2, NZ, NY)),
             constant_block(planes),
             constant_block((BINS, 8, LANES)),
             constant_block(planes),
+            *[VMEM] * 3,
         ),
         scratch_shapes=[
             pltpu.VMEM(planes, f32),
             pltpu.VMEM((2, LANES, LANES), f32),
             pltpu.VMEM((2, 2, 2, NZ, NY), f32),
+            pltpu.SemaphoreType.DMA((3,)),
         ],
         compiler_params=params(),
         cost_estimate=cost(15),
         name="first",
-    )(own, other, *masks, *near_tables)
+    )(own, other, *masks, *near_tables, *in_hbm(*tables[2:]))
 
     mine, theirs = pl.pallas_call(
         second_kernel,
@@ -718,7 +729,7 @@
         compiler_params=params(),
         cost_estimate=cost(4),
         name="second",
-    )(far_masks, *in_vmem(spectra, point, taus, total), *near_tables[2:])
+    )(far_masks, *in_vmem(spectra, point, taus, total, *back_tables))
 
     received = by_parity(mine + core_swap(theirs))
     app_dense, sums = pl.pallas_call(

time: 98.2 us -> 98.2 us (level)
  no operation moved by 1% of the time
where the time goes in v8:
time: 98.2 us; the launch traced here: 97.7 us
  Pallas kernels  28.3 us (29%)
  starting transfers between devices  25.6 us (26%)
  waiting for transfers between devices  23.8 us (24%)
  blocking collectives  18 us (18%)
    all_to_all x1, blocking collectives, by_parity(): lax.all_to_all(messages, AXES, 0, 0, axis_index_groups=groups)  18 us
    all_to_all x1, waiting for transfers between devices, by_parity(): lax.all_to_all(messages, AXES, 0, 0, axis_index_groups=groups)  14.2 us
    pallas_call x1, Pallas kernels, shards(): pl.pallas_call(first_kernel, grid=(BINS // 2,), out_shape=(near(BINS - NE...  11 us
    ppermute x5, starting transfers between devices, from_ti(): return lax.ppermute(values, 'ti', pairs)  7.88 us
    all_to_all x1, starting transfers between devices, by_parity(): lax.all_to_all(messages, AXES, 0, 0, axis_index_groups=groups)  7.85 us
    all_to_all x1, waiting for transfers between devices, shards(): lax.all_to_all(sums.reshape(128, 1, LANES), AXES, 0, 0).reshape(128, LANES)  7.19 us
    all_to_all x1, starting transfers between devices, shards(): lax.all_to_all(sums.reshape(128, 1, LANES), AXES, 0, 0).reshape(128, LANES)  5.41 us
    ppermute x2, starting transfers between devices, core_swap(): return lax.ppermute(values, 'kz', [(i, i ^ 1) for i in range(8)])  4.44 us
  transfers between devices with their start and end apart: 9, of which 4 were waited for; matrix products, arithmetic and copies ran while one was open for 0% of the time, Pallas kernels for 22%

profile of v8, /device:TPU:1, one launch (start us, length us, event | category | flops | bytes accessed | tf_op | source)
XLA Modules:
  0.0 97.7 jit_solution(6551264976702937921)
XLA Ops:
  0.6 1.0 copy-done
  1.6 2.5 %collective-permute-start.3 = (s32[160,256]{1,0:T(8,128)S(1)}, s32[160,256]{1,0:T(8,128)S(1)}, u32[]{:S(2)}, u32[]{:S(2)}) collective-permute-start(s32[160,256]{1,0:T(8,128)S(1)} %dynamic-slice_bitcast_fusion.refs_2_), channel_id=1, source_target_pairs={{96,0},{104,8},{112,16},{120,24},{0,32},{8,40},{16,48},{24,56},{32... | collective-permute-start | bytes 491528 | tf_op jit(solution)/shard_map/ppermute | solution.py:661
  4.2 2.2 %collective-permute-start.2 = (s32[160,256]{1,0:T(8,128)S(1)}, s32[160,256]{1,0:T(8,128)S(1)}, u32[]{:S(2)}, u32[]{:S(2)}) collective-permute-start(s32[160,256]{1,0:T(8,128)S(1)} %dynamic-slice_bitcast_fusion.refs_2_), channel_id=1, source_target_pairs={{32,0},{40,8},{48,16},{56,24},{64,32},{72,40},{80,48},{88,56},{96,... | collective-permute-start | bytes 491528 | tf_op jit(solution)/shard_map/ppermute | solution.py:661
  6.4 1.2 %collective-permute-start.1 = (s32[160,256]{1,0:T(8,128)S(1)}, s32[160,256]{1,0:T(8,128)S(1)}, u32[]{:S(2)}, u32[]{:S(2)}) collective-permute-start(s32[160,256]{1,0:T(8,128)S(1)} %dynamic-slice_bitcast_fusion.refs_2_), channel_id=1, source_target_pairs={{24,0},{0,8},{8,16},{16,24},{56,32},{32,40},{40,48},{48,56},{88,64... | collective-permute-start | bytes 491528 | tf_op jit(solution)/shard_map/ppermute | solution.py:661
  7.6 1.5 %collective-permute-start = (s32[160,256]{1,0:T(8,128)S(1)}, s32[160,256]{1,0:T(8,128)S(1)}, u32[]{:S(2)}, u32[]{:S(2)}) collective-permute-start(s32[160,256]{1,0:T(8,128)S(1)} %dynamic-slice_bitcast_fusion.refs_2_), channel_id=1, source_target_pairs={{8,0},{16,8},{24,16},{0,24},{40,32},{48,40},{56,48},{32,56},{72,64... | collective-permute-start | bytes 491528 | tf_op jit(solution)/shard_map/ppermute | solution.py:661
  9.0 3.8 %pack.1 = (f32[2304,128]{1,0:T(8,128)}, f32[4,18,8,128]{3,2,1,0:T(8,128)S(1)}) custom-call(f32[2]{0:T(128)} %times.1, f32[3,8,16,20]{3,2,1,0:T(8,128)} %bitcast.35, f32[2,8,8,16,20]{4,3,2,1,0:T(8,128)} %bitcast.40, f32[3,20,8,256]{3,2,1,0:T(8,128)} %bitcast.46, f32[2,4,2,20,8,256]{5,4,3,2,1,0:T(8,128)} %bitcast.39), custom_call_target="tpu_custom_call" | custom-call | flops 1600000000 | bytes 8000000 | tf_op jit(solution)/shard_map/pack/pallas_call | solution.py:615
  12.9 7.9 %all-to-all-start = ((f32[64,1,4608]{2,1,0:T(1,128)}), f32[64,1,4608]{2,1,0:T(1,128)S(1)}, u32[]{:S(2)}, u32[]{:S(2)}) async-start(f32[64,1,4608]{2,1,0:T(1,128)} %bitcast.34), calls=%async_computation | async-start | bytes 2359296 | tf_op jit(solution)/shard_map/all_to_all | solution.py:596
  20.7 2.8 %dense.1.residual = f32[4,18,8,128]{3,2,1,0:T(8,128)S(1)} custom-call(f32[3,8,16,20]{3,2,1,0:T(8,128)} %bitcast.37, f32[2,8,8,16,20]{4,3,2,1,0:T(8,128)} %bitcast.42), custom_call_target="tpu_custom_call" | custom-call | flops 1200000000 | bytes 6000000 | tf_op jit(solution)/shard_map/dense/pallas_call | solution.py:640
  23.6 14.2 %all-to-all-done = f32[64,1,4608]{2,1,0:T(1,128)S(1)} async-done(((f32[64,1,4608]{2,1,0:T(1,128)}), f32[64,1,4608]{2,1,0:T(1,128)S(1)}, u32[]{:S(2)}, u32[]{:S(2)}) %all-to-all-start) | async-done | bytes 1179680 | tf_op jit(solution)/shard_map/all_to_all | solution.py:596
  37.8 4.0 %collective-permute-start.5 = (f32[2304,128]{1,0:T(8,128)S(1)}, f32[2304,128]{1,0:T(8,128)S(1)}, u32[]{:S(2)}, u32[]{:S(2)}) collective-permute-start(f32[2304,128]{1,0:T(8,128)S(1)} %bitcast.25), channel_id=1, source_target_pairs={{0,1},{1,0},{2,3},{3,2},{4,5},{5,4},{6,7},{7,6},{8,9},{9,8},{10,11... | collective-permute-start | bytes 3538952 | tf_op jit(solution)/shard_map/ppermute | solution.py:590
  41.8 0.5 collective-permute-start.4
  42.2 1.2 %tables.1 = (bf16[2,768,256]{2,1,0:T(8,128)(2,1)S(1)}, bf16[2,160,512]{2,1,0:T(8,128)(2,1)S(1)}) custom-call(f32[2304,128]{1,0:T(8,128)S(1)} %bitcast.26, bf16[2,768,256]{2,1,0:T(8,128)(2,1)} %constant.22.clone.refs_0_, bf16[2,160,512]{2,1,0:T(8,128)(2,1)} %constant.23.clone.refs_1_), custom_call_target="tpu_custom_call" | custom-call | flops 400000000 | bytes 2000000 | tf_op jit(solution)/shard_map/tables/pallas_call | solution.py:676
  43.5 0.8 collective-permute-done.5.refs_1_
  44.2 11.0 %first.1 = (f32[3,2,2,160,256]{4,3,2,1,0:T(8,128)S(1)}, f32[2,1120,128]{2,1,0:T(8,128)S(1)}, f32[8,8,128]{2,1,0:T(8,128)S(1)}, f32[2,1120,128]{2,1,0:T(8,128)S(1...) custom-call(f32[2304,128]{1,0:T(8,128)S(1)} %bitcast.27, ...), custom_call_target="tpu_custom_call" | custom-call | flops 6000000000 | bytes 30000000 | tf_op jit(solution)/shard_map/first/pallas_call | solution.py:687
  55.3 3.2 %second.1 = (f32[1152,128]{1,0:T(8,128)S(1)}, f32[1152,128]{1,0:T(8,128)S(1)}) custom-call(s32[3,160,256]{2,1,0:T(8,128)S(1)} %collective-permute-done.4.mask, f32[3,2,2,160,256]{4,3,2,1,0:T(8,128)S(1)} %get-tuple-element.50.spectra, f32[2,1120,128]{2,1,0:T(8,128)S(1)} %get-tuple-element.51.point, f32[8,8,128]{2,1,0:T(8,128)S(1)} %get-tuple-element.52.taus, ...), custom_call_target="tpu_custom_call" | custom-call | flops 1600000000 | bytes 8000000 | tf_op jit(solution)/shard_map/second/pallas_call | solution.py:719
  58.5 0.5 collective-permute-start.6
  59.0 1.6 %collective-permute-done.6 = f32[1152,128]{1,0:T(8,128)S(1)} collective-permute-done((f32[1152,128]{1,0:T(8,128)S(1)}, f32[1152,128]{1,0:T(8,128)S(1)}, u32[]{:S(2)}, u32[]{:S(2)}) %collective-permute-start.6) | collective-permute-done | bytes 589856 | tf_op jit(solution)/shard_map/ppermute | solution.py:590
  60.6 0.1 add.8
  60.7 18.0 %all_to_all.15 = f32[64,1,2304]{2,1,0:T(1,128)S(1)} all-to-all(f32[64,1,2304]{2,1,0:T(1,128)S(1)} %bitcast.33), channel_id=1, replica_groups={{0,2,4,6,8,10,12,14,16,18,20,22,24,26,28,30,32,34,36,38,40,42,44,46,48,..., dimensions={0} | all-to-all | bytes 1179648 | tf_op jit(solution)/shard_map/all_to_all | solution.py:596
  78.7 1.5 %sums.1 = (f32[18,4,8,128]{3,2,1,0:T(8,128)}, f32[128,128]{1,0:T(8,128)}) custom-call(f32[1152,128]{1,0:T(8,128)S(1)} %bitcast.28, f32[4,18,8,128]{3,2,1,0:T(8,128)S(1)} %get-tuple-element.38.direction, f32[4,18,8,128]{3,2,1,0:T(8,128)S(1)} %dense.1.residual), custom_call_target="tpu_custom_call" | custom-call | flops 400000000 | bytes 2000000 | tf_op jit(solution)/shard_map/sums/pallas_call | solution.py:735
  80.2 5.4 %all-to-all-start.2 = ((f32[128,1,128]{2,1,0:T(1,128)}), f32[128,1,128]{2,1,0:T(1,128)S(1)}, u32[]{:S(2)}, u32[]{:S(2)}) async-start(f32[128,1,128]{2,1,0:T(1,128)} %bitcast.16), calls=%async_computation.2 | async-start | bytes 131072 | tf_op jit(solution)/shard_map/all_to_all | solution.py:745
  85.6 2.5 %native.1 = (f32[3,8,16,20]{3,2,1,0:T(8,128)}, f32[48,8,16,20]{3,2,1,0:T(8,128)S(1)}) custom-call(f32[18,4,8,128]{3,2,1,0:T(8,128)} %get-tuple-element.61.dense_in, f32[2,8,8,16,20]{4,3,2,1,0:T(8,128)} %bitcast.41, f32[2,8,8,16,20]{4,3,2,1,0:T(8,128)} %bitcast.43), custom_call_target="tpu_custom_call" | custom-call | flops 1200000000 | bytes 6000000 | tf_op jit(solution)/shard_map/native/pallas_call | solution.py:748
  88.1 7.2 %all-to-all-done.2 = f32[128,1,128]{2,1,0:T(1,128)S(1)} async-done(((f32[128,1,128]{2,1,0:T(1,128)}), f32[128,1,128]{2,1,0:T(1,128)S(1)}, u32[]{:S(2)}, u32[]{:S(2)}) %all-to-all-start.2) | async-done | bytes 65568 | tf_op jit(solution)/shard_map/all_to_all | solution.py:745
  95.3 2.3 %step.1 = (f32[3,8,16,20]{3,2,1,0:T(8,128)}, f32[2,8,8,16,20]{4,3,2,1,0:T(8,128)}, f32[3,8,16,20]{3,2,1,0:T(8,128)}, f32[2,8,8,16,20]{4,3,2,1,0:T(8,128)}) custom-call(f32[128,128]{1,0:T(8,128)S(1)} %bitcast.29, f32[48,8,16,20]{3,2,1,0:T(8,128)S(1)} %get-tuple-element.62.fields, f32[3,8,16,20]{3,2,1,0:T(8,128)} %get-tuple-element.63.app_maps, ...), custom_call_target="tpu_custom_call" | custom-call | flops 800000000 | bytes 4000000 | tf_op jit(solution)/shard_map/step/pallas_call | solution.py:765
  (8 shorter events, 0.1 us)
Async XLA Ops:
  0.6 1.0 %copy-start = (s32[2,160,256]{2,1,0:T(8,128)S(1)}, s32[2,160,256]{2,1,0:T(8,128)}, u32[]{:S(2)}) copy-start(s32[2,160,256]{2,1,0:T(8,128)} %param.20) | copy-start | bytes 983044
  1.6 11.2 %collective-permute-start.3 = (s32[160,256]{1,0:T(8,128)S(1)}, s32[160,256]{1,0:T(8,128)S(1)}, u32[]{:S(2)}, u32[]{:S(2)}) collective-permute-start(s32[160,256]{1,0:T(8,128)S(1)} %dynamic-slice_bitcast_fusion.refs_2_), channel_id=1, source_target_pairs={{96,0},{104,8},{112,16},{120,24},{0,32},{8,40},{16,48},{24,56},{32... | collective-permute-start | bytes 491528 | tf_op jit(solution)/shard_map/ppermute | solution.py:661
  4.2 8.7 %collective-permute-start.2 = (s32[160,256]{1,0:T(8,128)S(1)}, s32[160,256]{1,0:T(8,128)S(1)}, u32[]{:S(2)}, u32[]{:S(2)}) collective-permute-start(s32[160,256]{1,0:T(8,128)S(1)} %dynamic-slice_bitcast_fusion.refs_2_), channel_id=1, source_target_pairs={{32,0},{40,8},{48,16},{56,24},{64,32},{72,40},{80,48},{88,56},{96,... | collective-permute-start | bytes 491528 | tf_op jit(solution)/shard_map/ppermute | solution.py:661
  6.4 6.5 %collective-permute-start.1 = (s32[160,256]{1,0:T(8,128)S(1)}, s32[160,256]{1,0:T(8,128)S(1)}, u32[]{:S(2)}, u32[]{:S(2)}) collective-permute-start(s32[160,256]{1,0:T(8,128)S(1)} %dynamic-slice_bitcast_fusion.refs_2_), channel_id=1, source_target_pairs={{24,0},{0,8},{8,16},{16,24},{56,32},{32,40},{40,48},{48,56},{88,64... | collective-permute-start | bytes 491528 | tf_op jit(solution)/shard_map/ppermute | solution.py:661
  7.6 5.3 %collective-permute-start = (s32[160,256]{1,0:T(8,128)S(1)}, s32[160,256]{1,0:T(8,128)S(1)}, u32[]{:S(2)}, u32[]{:S(2)}) collective-permute-start(s32[160,256]{1,0:T(8,128)S(1)} %dynamic-slice_bitcast_fusion.refs_2_), channel_id=1, source_target_pairs={{8,0},{16,8},{24,16},{0,24},{40,32},{48,40},{56,48},{32,56},{72,64... | collective-permute-start | bytes 491528 | tf_op jit(solution)/shard_map/ppermute | solution.py:661
  12.9 24.9 %all-to-all-start = ((f32[64,1,4608]{2,1,0:T(1,128)}), f32[64,1,4608]{2,1,0:T(1,128)S(1)}, u32[]{:S(2)}, u32[]{:S(2)}) async-start(f32[64,1,4608]{2,1,0:T(1,128)} %bitcast.34), calls=%async_computation | async-start | bytes 2359296 | tf_op jit(solution)/shard_map/all_to_all | solution.py:596
  37.8 6.5 %collective-permute-start.5 = (f32[2304,128]{1,0:T(8,128)S(1)}, f32[2304,128]{1,0:T(8,128)S(1)}, u32[]{:S(2)}, u32[]{:S(2)}) collective-permute-start(f32[2304,128]{1,0:T(8,128)S(1)} %bitcast.25), channel_id=1, source_target_pairs={{0,1},{1,0},{2,3},{3,2},{4,5},{5,4},{6,7},{7,6},{8,9},{9,8},{10,11... | collective-permute-start | bytes 3538952 | tf_op jit(solution)/shard_map/ppermute | solution.py:590
  41.8 13.5 %collective-permute-start.4 = (s32[3,160,256]{2,1,0:T(8,128)S(1)}, s32[3,160,256]{2,1,0:T(8,128)S(1)}, u32[]{:S(2)}, u32[]{:S(2)}) collective-permute-start(s32[3,160,256]{2,1,0:T(8,128)S(1)} %pad_add_fusion), channel_id=1, source_target_pairs={{32,0},{40,8},{48,16},{56,24},{64,32},{72,40},{80,48},{88,56},{96,... | collective-permute-start | bytes 1474568 | tf_op jit(solution)/shard_map/ppermute | solution.py:661
  58.5 2.1 %collective-permute-start.6 = (f32[1152,128]{1,0:T(8,128)S(1)}, f32[1152,128]{1,0:T(8,128)S(1)}, u32[]{:S(2)}, u32[]{:S(2)}) collective-permute-start(f32[1152,128]{1,0:T(8,128)S(1)} %get-tuple-element.58), channel_id=1, source_target_pairs={{0,1},{1,0},{2,3},{3,2},{4,5},{5,4},{6,7},{7,6},{8,9},{9,8},{10,11... | collective-permute-start | bytes 1769480 | tf_op jit(solution)/shard_map/ppermute | solution.py:590
  80.2 15.1 %all-to-all-start.2 = ((f32[128,1,128]{2,1,0:T(1,128)}), f32[128,1,128]{2,1,0:T(1,128)S(1)}, u32[]{:S(2)}, u32[]{:S(2)}) async-start(f32[128,1,128]{2,1,0:T(1,128)} %bitcast.16), calls=%async_computation.2 | async-start | bytes 131072 | tf_op jit(solution)/shard_map/all_to_all | solution.py:745
